TPU v7x, 32 devices: a whole 2x2x4 slice. The times are simulated.
32 devices in a mesh: shard: 8 (over z, x), rep: 4 (over y, core).
Axes of the slice: x: 2, y: 2, z: 4, core: 2. Of those that a mesh axis runs over, the one named last changes fastest.
Arguments:
- grad_pooled: bfloat16 [4096, 8, 128], P(('shard', 'rep')), may hold values from -6 to 6
- lookup_weight: float32 [65536], P(('shard', 'rep')), may hold values from 0.25 to 4
- owner: int32 [65536, 1], P(('shard', 'rep')), may hold values from 0 to 7; in each aligned block of 2048 rows (0 to 2047, 2048 to 4095, ...) at most 384 rows name the same one
- local_row: int32 [65536], P(('shard', 'rep')), may hold values from 0 to 4095
- weight: float32 [32768, 128], P('shard'), may hold values from -6 to 6
- accum: float32 [32768], P('shard'), may hold values from 0.1 to 10
Outputs:
- new_weight: float32 [32768, 128], P('shard')
- new_accum: float32 [32768], P('shard')
Inputs may be any that keep to these rules, and one draw needn't show every extreme that they name: Among the lookups of one device no owner is named more than 384 times, a bound that some block reaches.
All inputs are finite; a program needn't handle non-finite values.
Results may differ from a plain program's by a relative error of at most 0.0011.
Values may be sent and summed in bfloat16 or wider, within the bound.
No kernel may reach another device: no remote copies, remote signals or barrier semaphores. Data moves between devices by JAX's collectives and lax.ppermute only.
A program may use at most 64 MiB of HBM per device.

v0:
```python
import jax
import jax.numpy as jnp
from jax import lax
from jax.sharding import PartitionSpec as P

step_size = 0.25
epsilon = 1e-08


def adagrad(weight, accum, table_grad):
    new_accum = accum + jnp.mean(table_grad * table_grad, axis=1)
    new_weight = weight - step_size * table_grad / (jnp.sqrt(new_accum)[:, None] + epsilon)
    return (new_weight, new_accum)


def body(grad_pooled, lookup_weight, owner, local_row, weight, accum):
    width = grad_pooled.shape[-1]
    lookups = lookup_weight.shape[0]
    pooling = lookups // (grad_pooled.shape[0] * grad_pooled.shape[1])
    shards = lax.axis_size("shard")
    capacity = (3 * lookups + 2 * shards - 1) // (2 * shards)
    bags = grad_pooled.reshape(-1, width).astype(jnp.float32)
    rows = (bags[:, None, :] * lookup_weight.reshape(-1, pooling, 1)).reshape(lookups, width)
    rows = rows.astype(jnp.bfloat16)
    target_shard = owner[:, 0]
    hits = (target_shard[:, None] == jnp.arange(shards, dtype=jnp.int32)[None, :]).astype(jnp.int32)
    ranks = jnp.sum(jnp.cumsum(hits, axis=0) * hits, axis=1) - 1
    slots = target_shard * capacity + ranks
    outgoing = jnp.zeros((shards * capacity, width), jnp.bfloat16).at[slots].set(rows)
    row_ids = jnp.full((shards * capacity,), -1, jnp.int32).at[slots].set(local_row)
    received, received_ids = (
        lax.all_to_all(
            outgoing.reshape(shards, capacity, width),
            "shard",
            split_axis=0,
            concat_axis=0,
            tiled=True,
        ),
        lax.all_to_all(
            row_ids.reshape(shards, capacity), "shard", split_axis=0, concat_axis=0, tiled=True
        ),
    )
    flat_rows = received.reshape(-1, width)
    flat_ids = received_ids.reshape(-1)
    window_rows = weight.shape[0]
    span = 512
    starts = jnp.arange(window_rows // span, dtype=jnp.int32) * span

    def one_block(start):
        shifted = flat_ids - start
        onehot = (jnp.arange(span, dtype=jnp.int32)[:, None] == shifted[None, :]).astype(
            jnp.bfloat16
        )
        return jnp.dot(onehot, flat_rows, preferred_element_type=jnp.float32)

    partial_grad = lax.map(one_block, starts).reshape(window_rows, width)
    table_grad = lax.psum(partial_grad, "rep")
    new_weight, new_accum = adagrad(weight, accum, table_grad)
    return (new_weight, new_accum)


def solution(mesh):
    in_specs = (
        P(("shard", "rep"), None, None),
        P(("shard", "rep")),
        P(("shard", "rep"), None),
        P(("shard", "rep")),
        P("shard", None),
        P("shard"),
    )
    out_specs = (P("shard", None), P("shard"))
    return jax.shard_map(body, mesh=mesh, in_specs=in_specs, out_specs=out_specs, check_vma=False)
```

profile of v0, /device:TPU:0, one launch (start us, length us, event | category | flops | bytes accessed | tf_op | source)
XLA Modules:
  0.0 149.2 jit_solution(17626736822952429710)
XLA Ops:
  7.2 0.7 fusion.9
  7.9 2.3 %reduce-window.6 = s32[8,16,128]{2,1,0:T(8,128)S(1)} reduce-window(s32[8,16,128]{2,1,0:T(8,128)S(1)} %fusion.9, s32[]{:T(128)} %copy.19), window={size=1x1x128 pad=0_0x0_0x127_0}, to_apply=%region_0.0 | reduce-window | flops 2080768 | bytes 131076 | tf_op jit(solution)/shard_map/reduce-window
  10.7 0.7 fusion.8
  11.5 0.7 compare_select_fusion
  12.2 8.8 %scatter_custom_fusion = s32[3072]{0:T(1024)} fusion(s32[2048]{0:T(1024)S(1)} %bitcast.48, s32[2048]{0:T(1024)} %param.11, s32[]{:T(128)} %constant.19.clone.1), kind=kCustom, calls=%fused_computation.26 | custom fusion | bytes 12800 | tf_op jit(solution)/shard_map/scatter | solution.py:30
  21.0 7.3 %all-to-all-start = ((s32[8,1,384]{2,1,0:T(1,128)}), s32[8,1,384]{2,1,0:T(1,128)S(1)}, u32[]{:S(2)}, u32[]{:S(2)}) async-start(s32[8,1,384]{2,1,0:T(1,128)} %bitcast.7), calls=%async_computation | async-start | bytes 24576 | tf_op jit(solution)/shard_map/all_to_all | solution.py:39
  28.2 1.0 bitcast_convert_fusion
  29.6 7.6 %scatter_custom_fusion.1 = bf16[3072,128]{1,0:T(8,128)(2,1)} fusion(s32[2048]{0:T(1024)S(1)} %bitcast.49, f32[2048,128]{1,0:T(8,128)S(1)} %bitcast.40, f32[2048]{0:T(1024)S(1)} %copy-done.3, bf16[]{:T(256)} %constant.13.clone.1), kind=kCustom, calls=%fused_computation.11 | custom fusion | flops 524288 | bytes 1843202 | tf_op jit(solution)/shard_map/scatter | solution.py:29
  37.2 6.0 %all-to-all-start.1 = ((bf16[8,384,128]{2,1,0:T(8,128)(2,1)}), bf16[8,384,128]{2,1,0:T(8,128)(2,1)S(1)}, u32[]{:S(2)}, u32[]{:S(2)}) async-start(bf16[8,384,128]{2,1,0:T(8,128)(2,1)} %bitcast.11), calls=%async_computation.1 | async-start | bytes 1572864 | tf_op jit(solution)/shard_map/all_to_all | solution.py:32
  43.3 19.6 %all-to-all-done.1 = bf16[8,384,128]{2,1,0:T(8,128)(2,1)S(1)} async-done(((bf16[8,384,128]{2,1,0:T(8,128)(2,1)}), bf16[8,384,128]{2,1,0:T(8,128)(2,1)S(1)}, u32[]{:S(2)}, u32[]{:S(2)}) %all-to-all-start.1) | async-done | bytes 786464 | tf_op jit(solution)/shard_map/all_to_all | solution.py:32
  62.9 24.3 %while.10 = (s32[]{:T(128)}, f32[8,512,128]{2,1,0:T(8,128)}, s32[8]{0:T(128)S(1)}, s32[3072]{0:T(1024)S(1)}, bf16[3072,128]{1,0:T(8,128)(2,1)S(1)}, /*index=5*/s32[]{:T(128)}) while((s32[]{:T(128)}, f32[8,512,128]{2,1,0:T(8,128)}, s32[8]{0:T(128)S(1)}, s32[3072]{0:T(1024)S(1)}, bf16[3072,128]{1,0:T(8,128)(2,1)S(1)}, /*index=5*/s32[]{:T(128)}) %tuple.29), condition=%wide.region_6.7_spmd, body=%wide.region_5.6_spmd.sunk | while | flops 404229120 | bytes 1086037 | solution.py:56
  62.9 0.6 dynamic_slice.5
  63.5 0.6 broadcast_subtract_fusion.2
  64.1 1.8 %fusion.16 = f32[8,512,128]{2,1,0:T(8,128)} fusion(f32[8,512,128]{2,1,0:T(8,128)} %get-tuple-element.80, s32[]{:T(128)} %get-tuple-element.79, bf16[3072,128]{1,0:T(8,128)(2,1)S(1)} %get-tuple-element.89, s32[3072]{0:T(1024)S(1)} %broadcast_subtract_fusion.2), kind=kOutput, calls=%fused_computation.6.clone.1 | convolution fusion | flops 404226048 | bytes 1061376 | tf_op jit(solution)/shard_map/while/body/eval_jaxpr/dot_general | solution.py:54
  66.5 0.6 broadcast_subtract_fusion.2
  67.2 1.8 %fusion.16 = f32[8,512,128]{2,1,0:T(8,128)} fusion(f32[8,512,128]{2,1,0:T(8,128)} %get-tuple-element.80, s32[]{:T(128)} %get-tuple-element.79, bf16[3072,128]{1,0:T(8,128)(2,1)S(1)} %get-tuple-element.89, s32[3072]{0:T(1024)S(1)} %broadcast_subtract_fusion.2), kind=kOutput, calls=%fused_computation.6.clone.1 | convolution fusion | flops 404226048 | bytes 1061376 | tf_op jit(solution)/shard_map/while/body/eval_jaxpr/dot_general | solution.py:54
  69.6 0.6 broadcast_subtract_fusion.2
  70.2 1.8 %fusion.16 = f32[8,512,128]{2,1,0:T(8,128)} fusion(f32[8,512,128]{2,1,0:T(8,128)} %get-tuple-element.80, s32[]{:T(128)} %get-tuple-element.79, bf16[3072,128]{1,0:T(8,128)(2,1)S(1)} %get-tuple-element.89, s32[3072]{0:T(1024)S(1)} %broadcast_subtract_fusion.2), kind=kOutput, calls=%fused_computation.6.clone.1 | convolution fusion | flops 404226048 | bytes 1061376 | tf_op jit(solution)/shard_map/while/body/eval_jaxpr/dot_general | solution.py:54
  72.6 0.6 broadcast_subtract_fusion.2
  73.2 1.8 %fusion.16 = f32[8,512,128]{2,1,0:T(8,128)} fusion(f32[8,512,128]{2,1,0:T(8,128)} %get-tuple-element.80, s32[]{:T(128)} %get-tuple-element.79, bf16[3072,128]{1,0:T(8,128)(2,1)S(1)} %get-tuple-element.89, s32[3072]{0:T(1024)S(1)} %broadcast_subtract_fusion.2), kind=kOutput, calls=%fused_computation.6.clone.1 | convolution fusion | flops 404226048 | bytes 1061376 | tf_op jit(solution)/shard_map/while/body/eval_jaxpr/dot_general | solution.py:54
  75.6 0.6 broadcast_subtract_fusion.2
  76.3 1.8 %fusion.16 = f32[8,512,128]{2,1,0:T(8,128)} fusion(f32[8,512,128]{2,1,0:T(8,128)} %get-tuple-element.80, s32[]{:T(128)} %get-tuple-element.79, bf16[3072,128]{1,0:T(8,128)(2,1)S(1)} %get-tuple-element.89, s32[3072]{0:T(1024)S(1)} %broadcast_subtract_fusion.2), kind=kOutput, calls=%fused_computation.6.clone.1 | convolution fusion | flops 404226048 | bytes 1061376 | tf_op jit(solution)/shard_map/while/body/eval_jaxpr/dot_general | solution.py:54
  78.7 0.6 broadcast_subtract_fusion.2
  79.3 1.8 %fusion.16 = f32[8,512,128]{2,1,0:T(8,128)} fusion(f32[8,512,128]{2,1,0:T(8,128)} %get-tuple-element.80, s32[]{:T(128)} %get-tuple-element.79, bf16[3072,128]{1,0:T(8,128)(2,1)S(1)} %get-tuple-element.89, s32[3072]{0:T(1024)S(1)} %broadcast_subtract_fusion.2), kind=kOutput, calls=%fused_computation.6.clone.1 | convolution fusion | flops 404226048 | bytes 1061376 | tf_op jit(solution)/shard_map/while/body/eval_jaxpr/dot_general | solution.py:54
  81.7 0.6 broadcast_subtract_fusion.2
  82.4 1.8 %fusion.16 = f32[8,512,128]{2,1,0:T(8,128)} fusion(f32[8,512,128]{2,1,0:T(8,128)} %get-tuple-element.80, s32[]{:T(128)} %get-tuple-element.79, bf16[3072,128]{1,0:T(8,128)(2,1)S(1)} %get-tuple-element.89, s32[3072]{0:T(1024)S(1)} %broadcast_subtract_fusion.2), kind=kOutput, calls=%fused_computation.6.clone.1 | convolution fusion | flops 404226048 | bytes 1061376 | tf_op jit(solution)/shard_map/while/body/eval_jaxpr/dot_general | solution.py:54
  84.7 0.6 broadcast_subtract_fusion.2
  85.4 1.8 %fusion.16 = f32[8,512,128]{2,1,0:T(8,128)} fusion(f32[8,512,128]{2,1,0:T(8,128)} %get-tuple-element.80, s32[]{:T(128)} %get-tuple-element.79, bf16[3072,128]{1,0:T(8,128)(2,1)S(1)} %get-tuple-element.89, s32[3072]{0:T(1024)S(1)} %broadcast_subtract_fusion.2), kind=kOutput, calls=%fused_computation.6.clone.1 | convolution fusion | flops 404226048 | bytes 1061376 | tf_op jit(solution)/shard_map/while/body/eval_jaxpr/dot_general | solution.py:54
  87.2 50.5 %all-reduce.2.cloned.1.call-done = f32[4096,128]{1,0:T(8,128)} async-done(((f32[4096,128]{1,0:T(8,128)}), f32[4096,128]{1,0:T(8,128)}) %all-reduce.2.cloned.1.call-update) | async-done | bytes 2097168 | tf_op jit(solution)/shard_map/psum | solution.py:57
  137.7 2.4 %multiply_reduce_fusion = f32[4096]{0:T(1024)S(1)} fusion(f32[4096,128]{1,0:T(8,128)} %all-reduce.2.cloned.1.call-done), kind=kLoop, calls=%fused_computation.9 | loop fusion | flops 1044480 | bytes 2113536 | tf_op jit(solution)/shard_map/reduce_sum | solution.py:11
  140.1 0.6 sqrt_add_fusion
  140.7 1.7 %divide_subtract_fusion = f32[4096,128]{1,0:T(8,128)} fusion(f32[4096,128]{1,0:T(8,128)S(1)} %copy-done.1, f32[4096,128]{1,0:T(8,128)S(1)} %copy-done, f32[4096]{0:T(1024)S(1)} %get-tuple-element.40), kind=kLoop, calls=%fused_computation.8 | loop fusion | flops 1572864 | bytes 6307840 | tf_op jit(solution)/shard_map/sub | solution.py:12
  (25 shorter events, 5.1 us)
Async XLA Ops:
  7.2 22.4 %copy-start.3 = (f32[2048]{0:T(1024)S(1)}, f32[2048]{0:T(1024)}, u32[]{:S(2)}) copy-start(f32[2048]{0:T(1024)} %param.9) | copy-start | bytes 24580
  21.0 16.3 %all-to-all-start = ((s32[8,1,384]{2,1,0:T(1,128)}), s32[8,1,384]{2,1,0:T(1,128)S(1)}, u32[]{:S(2)}, u32[]{:S(2)}) async-start(s32[8,1,384]{2,1,0:T(1,128)} %bitcast.7), calls=%async_computation | async-start | bytes 24576 | tf_op jit(solution)/shard_map/all_to_all | solution.py:39
  37.2 25.7 %all-to-all-start.1 = ((bf16[8,384,128]{2,1,0:T(8,128)(2,1)}), bf16[8,384,128]{2,1,0:T(8,128)(2,1)S(1)}, u32[]{:S(2)}, u32[]{:S(2)}) async-start(bf16[8,384,128]{2,1,0:T(8,128)(2,1)} %bitcast.11), calls=%async_computation.1 | async-start | bytes 1572864 | tf_op jit(solution)/shard_map/all_to_all | solution.py:32
  43.2 94.5 %all-reduce.2.cloned.1.call-start = ((), (), s32[]{:S(2)}) async-start(), calls=%async_computation.2 | async-start | bytes 4194304 | tf_op jit(solution)/shard_map/psum | solution.py:57
  87.2 52.9 %copy-start.2 = (f32[4096]{0:T(1024)S(1)}, f32[4096]{0:T(1024)}, u32[]{:S(2)}) copy-start(f32[4096]{0:T(1024)} %param.13) | copy-start | bytes 49156
  87.2 53.5 %copy-start.1 = (f32[4096,128]{1,0:T(8,128)S(1)}, f32[4096,128]{1,0:T(8,128)}, u32[]{:S(2)}) copy-start(f32[4096,128]{1,0:T(8,128)} %param.12) | copy-start | bytes 6291460
  137.7 3.0 %copy-start = (f32[4096,128]{1,0:T(8,128)S(1)}, f32[4096,128]{1,0:T(8,128)}, u32[]{:S(2)}) copy-start(f32[4096,128]{1,0:T(8,128)} %all-reduce.2.cloned.1.call-done) | copy-start | bytes 6291460
Sparse Core Ops, SparseCore 0:
  87.3 50.3 all-reduce.1
where the time goes:
time: 150 us; the launch traced here: 149 us
  waiting for transfers between devices  70.1 us (47%)
  other arithmetic  23.1 us (15%)
  matrix products  14.4 us (10%)
  local copies, waits for them, and re-layouts  14.1 us (9%)
  between operations  14.1 us (9%)
  starting transfers between devices  13.3 us (9%)
    psum x1, waiting for transfers between devices, body(): table_grad = lax.psum(partial_grad, 'rep')  50.5 us
    all_to_all x1, waiting for transfers between devices, body(): lax.all_to_all(outgoing.reshape(shards, capacity, width), 'shard', split_...  19.6 us
    dot_general x8, matrix products, one_block(): return jnp.dot(onehot, flat_rows, preferred_element_type=jnp.float32)  14.4 us
    scatter x1, local copies, waits for them, and re-layouts, body(): jnp.full((shards * capacity,), -1, jnp.int32).at[slots].set(local_row)  8.79 us
    scatter x1, other arithmetic, body(): jnp.zeros((shards * capacity, width), jnp.bfloat16).at[slots].set(rows)  7.63 us
    all_to_all x1, starting transfers between devices, body(): lax.all_to_all(row_ids.reshape(shards, capacity), 'shard', split_axis=0,...  7.25 us
    all_to_all x1, starting transfers between devices, body(): lax.all_to_all(outgoing.reshape(shards, capacity, width), 'shard', split_...  6 us
    sub x8, other arithmetic, one_block(): shifted = flat_ids - start  5.18 us
  transfers between devices with their start and end apart: 3, of which 2 were waited for; matrix products, arithmetic and copies ran while one was open for 6% of the time, Pallas kernels for 0%

commit v1 on v0

v1 whole, which is shorter than its diff:
```python
import functools

import jax
import jax.numpy as jnp
from jax import lax
from jax.experimental import pallas as pl
from jax.experimental.pallas import tpu as pltpu
from jax.sharding import PartitionSpec as P

step_size = 0.25
epsilon = 1e-08
f32, bf16, i32 = jnp.float32, jnp.bfloat16, jnp.int32
LANES = 128
PAD = 16
VMEM_LIMIT = 48 * 1024 * 1024


def adagrad(weight, accum, table_grad):
    new_accum = accum + jnp.mean(table_grad * table_grad, axis=1)
    new_weight = weight - step_size * table_grad / (jnp.sqrt(new_accum)[:, None] + epsilon)
    return (new_weight, new_accum)


def general_body(grad_pooled, lookup_weight, owner, local_row, weight, accum):
    width = grad_pooled.shape[-1]
    lookups = lookup_weight.shape[0]
    pooling = lookups // (grad_pooled.shape[0] * grad_pooled.shape[1])
    shards = lax.axis_size("shard")
    capacity = (3 * lookups + 2 * shards - 1) // (2 * shards)
    bags = grad_pooled.reshape(-1, width).astype(f32)
    rows = (bags[:, None, :] * lookup_weight.reshape(-1, pooling, 1)).reshape(lookups, width)
    rows = rows.astype(bf16)
    target_shard = owner[:, 0]
    hits = (target_shard[:, None] == jnp.arange(shards, dtype=i32)[None, :]).astype(i32)
    ranks = jnp.sum(jnp.cumsum(hits, axis=0) * hits, axis=1) - 1
    slots = target_shard * capacity + ranks
    outgoing = jnp.zeros((shards * capacity, width), bf16).at[slots].set(rows)
    row_ids = jnp.full((shards * capacity,), -1, i32).at[slots].set(local_row)
    received, received_ids = (
        lax.all_to_all(outgoing.reshape(shards, capacity, width), "shard", split_axis=0, concat_axis=0, tiled=True),
        lax.all_to_all(row_ids.reshape(shards, capacity), "shard", split_axis=0, concat_axis=0, tiled=True),
    )
    flat_rows = received.reshape(-1, width)
    flat_ids = received_ids.reshape(-1)
    window_rows = weight.shape[0]
    span = 512
    starts = jnp.arange(window_rows // span, dtype=i32) * span

    def one_block(start):
        shifted = flat_ids - start
        onehot = (jnp.arange(span, dtype=i32)[:, None] == shifted[None, :]).astype(bf16)
        return jnp.dot(onehot, flat_rows, preferred_element_type=f32)

    partial_grad = lax.map(one_block, starts).reshape(window_rows, width)
    table_grad = lax.psum(partial_grad, "rep")
    return adagrad(weight, accum, table_grad)


def iota(shape, dim, dtype=i32):
    return lax.broadcasted_iota(i32, shape, dim).astype(dtype)


def pack_kernel(groups, capacity, key_ref, owner_ref, row_ref, w_ref, bags_ref, keep_ref, give_ref, ext_ref):
    blocks = owner_ref.shape[0]
    wide = groups * blocks
    group = owner_ref[...] ^ key_ref[0]
    hits = [(group == g).astype(f32) for g in range(groups)]
    stacked = jnp.concatenate(hits, axis=0).astype(bf16)
    upper = (iota((LANES, LANES), 0) <= iota((LANES, LANES), 1)).astype(bf16)
    inside = jnp.dot(stacked, upper, preferred_element_type=f32)
    totals = jnp.dot(stacked, jnp.ones((LANES, LANES), bf16), preferred_element_type=f32)
    at, to = iota((wide, wide), 0), iota((wide, wide), 1)
    earlier = ((at // blocks == to // blocks) & (to < at)).astype(bf16)
    carry = jnp.dot(earlier, totals.astype(bf16), preferred_element_type=f32)
    rank = inside + carry - 1.0
    slot = jnp.zeros((blocks, LANES), f32)
    for g in range(groups):
        slot = slot + hits[g] * (rank[g * blocks:(g + 1) * blocks] + float(g * capacity))

    digits = jnp.concatenate(
        [(row_ref[...] >> 8).astype(f32), (row_ref[...] & 255).astype(f32), w_ref[...]]
        + [jnp.zeros((LANES - 3 * blocks, LANES), f32)], axis=0)
    columns = digits.T
    lane = iota((LANES, LANES), 1)
    repeat = ((iota((LANES, LANES // 2), 0) >> 1) == iota((LANES, LANES // 2), 1)).astype(bf16)
    for r in range(blocks):
        bag = jnp.dot(repeat, bags_ref[r * LANES // 2:(r + 1) * LANES // 2, :], preferred_element_type=f32)
        here = slice(r * LANES, (r + 1) * LANES)
        ext_ref[here, 0:LANES] = (bag * columns[:, 2 * blocks + r:2 * blocks + r + 1]).astype(bf16)
        high, low = columns[:, r:r + 1], columns[:, blocks + r:blocks + r + 1]
        ext_ref[here, LANES:2 * LANES] = jnp.where(
            lane == 0, high, jnp.where(lane == 1, low, 0.0)).astype(bf16)

    place = iota((LANES, LANES), 0, f32)
    chunks = capacity // LANES
    for turn in range(groups):
        g = (2 * (turn % (groups // 2)) + 1) if turn < groups // 2 else 2 * (turn - groups // 2)
        out_ref = give_ref if g % 2 else keep_ref
        high, low = [], []
        for k in range(chunks):
            moved = slot - float(g * capacity + k * LANES)
            picks = jnp.concatenate(
                [(place == moved[r:r + 1, :]).astype(bf16) for r in range(blocks)], axis=1)
            packed = jnp.dot(picks, ext_ref[...], preferred_element_type=f32)
            out_ref[g // 2, k * LANES:(k + 1) * LANES, :] = packed[:, :LANES].astype(bf16)
            turned = packed[:, LANES:].T
            high.append(turned[0:1])
            low.append(turned[1:2])
        out_ref[g // 2, capacity:capacity + PAD, :] = jnp.concatenate(
            high + low + [jnp.zeros((PAD - 2 * chunks, LANES), f32)], axis=0).astype(bf16)


def pack(key, owner, local_row, lookup_weight, bags, groups, capacity):
    blocks = owner.shape[0] // LANES
    shape = jax.ShapeDtypeStruct((groups // 2, capacity + PAD, LANES), bf16)
    vmem = pl.BlockSpec(memory_space=pltpu.VMEM)
    return pl.pallas_call(
        functools.partial(pack_kernel, groups, capacity),
        out_shape=[shape, shape],
        in_specs=[pl.BlockSpec(memory_space=pltpu.SMEM), vmem, vmem, vmem, vmem],
        out_specs=[vmem, vmem],
        scratch_shapes=[pltpu.VMEM((blocks * LANES, 2 * LANES), bf16)],
        compiler_params=pltpu.CompilerParams(vmem_limit_bytes=VMEM_LIMIT),
        name="pack",
    )(key, owner.reshape(blocks, LANES), local_row.reshape(blocks, LANES),
      lookup_weight.reshape(blocks, LANES), bags)


def add_kernel(capacity, lists, first, core_ref, *refs):
    in_refs, refs = refs[:lists], refs[lists:]
    before, (keep_ref, give_ref, rhs_ref) = (None, refs) if first else (refs[:2], refs[2:])
    half = keep_ref.shape[0]
    chunks = capacity // LANES
    highs, lows = [], []
    at = 0
    for ref in in_refs:
        for part in range(2):
            base = part * (capacity + PAD)
            digits = ref[base + capacity:base + capacity + PAD, :].astype(f32)
            high = digits[0:chunks]
            upper = (high >= float(half // 256)).astype(f32)
            give = jnp.where(core_ref[0] == 0, upper, 1.0 - upper)
            highs += [high[k:k + 1] - upper[k:k + 1] * float(half // 256) for k in range(chunks)]
            lows += [digits[chunks + k:chunks + k + 1] for k in range(chunks)]
            turned = jnp.concatenate([give, jnp.zeros((LANES - chunks, LANES), f32)], axis=0).T
            for k in range(chunks):
                rows = ref[base + k * LANES:base + (k + 1) * LANES, :].astype(f32)
                given = turned[:, k:k + 1] > 0.5
                here = slice(at, at + LANES)
                rhs_ref[here, 0:LANES] = jnp.where(given, 0.0, rows).astype(bf16)
                rhs_ref[here, LANES:2 * LANES] = jnp.where(given, rows, 0.0).astype(bf16)
                at += LANES
    place = iota((256, LANES), 0, f32)
    for h in range(half // 256):
        picks = jnp.concatenate(
            [(place == jnp.where(hi == float(h), lo, -1.0)).astype(bf16) for hi, lo in zip(highs, lows)], axis=1)
        part = jnp.dot(picks, rhs_ref[...], preferred_element_type=f32)
        here = slice(h * 256, (h + 1) * 256)
        keep, give = part[:, :LANES], part[:, LANES:]
        if before is not None:
            keep, give = keep + before[0][here, :], give + before[1][here, :]
        keep_ref[here, :] = keep
        give_ref[here, :] = give


def add_lists(core, lists, before, half, capacity):
    shape = jax.ShapeDtypeStruct((half, LANES), f32)
    vmem = pl.BlockSpec(memory_space=pltpu.VMEM)
    n = len(lists)
    depth = n * 2 * capacity
    return pl.pallas_call(
        functools.partial(add_kernel, capacity, n, before is None),
        out_shape=[shape, shape],
        in_specs=[pl.BlockSpec(memory_space=pltpu.SMEM)] + [vmem] * (n + (0 if before is None else 2)),
        out_specs=[vmem, vmem],
        scratch_shapes=[pltpu.VMEM((depth, 2 * LANES), bf16)],
        input_output_aliases={} if before is None else {n + 1: 0, n + 2: 1},
        compiler_params=pltpu.CompilerParams(vmem_limit_bytes=VMEM_LIMIT),
        cost_estimate=pl.CostEstimate(flops=4 * half * depth * LANES, bytes_accessed=4 * half * LANES * 4, transcendentals=0),
        name="add_lists",
    )(core, *lists, *([] if before is None else before))


def update_kernel(steps, core_ref, own_ref, own_y_ref, other_ref, other_y_ref, weight_ref, accum_ref,
                  new_weight_ref, new_accum_ref, columns_ref, sums_ref):
    step = pl.program_id(0)
    blocks = accum_ref.shape[0]
    span = weight_ref.shape[0]

    @pl.when(step == 0)
    def _():
        columns_ref[...] = jnp.concatenate(
            [accum_ref[...], jnp.zeros((LANES - blocks, LANES), f32)], axis=0).T
        sums_ref[...] = jnp.zeros((LANES, LANES), f32)

    mine = (step >= steps // 2) == (core_ref[0] == 1)
    lane = iota((LANES, LANES), 1)
    start = (step % (steps // 2)) * span
    for k in range(span // LANES):
        at = pl.ds(pl.multiple_of(start + k * LANES, LANES), LANES)
        here = slice(k * LANES, (k + 1) * LANES)
        near = own_ref[at, :].astype(f32) + own_y_ref[at, :].astype(f32)
        far = other_ref[at, :].astype(f32) + other_y_ref[at, :].astype(f32)
        grad = jnp.where(mine, near, far)
        hit = lane == step * (span // LANES) + k
        old = jnp.sum(jnp.where(hit, columns_ref[...], 0.0), axis=1, keepdims=True)
        new = old + jnp.sum(grad * grad, axis=1, keepdims=True) * (1.0 / LANES)
        sums_ref[...] = jnp.where(hit, new, sums_ref[...])
        new_weight_ref[here, :] = weight_ref[here, :] - grad * (step_size / (jnp.sqrt(new) + epsilon))

    @pl.when(step == steps - 1)
    def _():
        new_accum_ref[...] = sums_ref[...].T[:blocks]


def update(core, own, own_y, other, other_y, weight, accum):
    rows = weight.shape[0]
    blocks = rows // LANES
    steps = 8
    span = rows // steps
    whole = pl.BlockSpec(memory_space=pltpu.VMEM)
    new_weight, new_accum = pl.pallas_call(
        functools.partial(update_kernel, steps),
        grid=(steps,),
        out_shape=[jax.ShapeDtypeStruct(weight.shape, f32), jax.ShapeDtypeStruct((blocks, LANES), f32)],
        in_specs=[pl.BlockSpec(memory_space=pltpu.SMEM), whole, whole, whole, whole,
                  pl.BlockSpec((span, LANES), lambda i: (i, 0)), whole],
        out_specs=[pl.BlockSpec((span, LANES), lambda i: (i, 0)), pl.BlockSpec((blocks, LANES), lambda i: (0, 0))],
        scratch_shapes=[pltpu.VMEM((LANES, LANES), f32), pltpu.VMEM((LANES, LANES), f32)],
        compiler_params=pltpu.CompilerParams(vmem_limit_bytes=VMEM_LIMIT),
        name="update",
    )(core, own, own_y, other, other_y, weight, accum.reshape(blocks, LANES))
    return new_weight, new_accum.reshape(-1)


def paired_body(shards, reps, grad_pooled, lookup_weight, owner, local_row, weight, accum):
    width = grad_pooled.shape[-1]
    lookups = lookup_weight.shape[0]
    capacity = (3 * lookups + 2 * shards - 1) // (2 * shards)
    half = weight.shape[0] // 2
    axes = ("shard", "rep")

    def permute(value, target):
        pairs = [(s * reps + r, target(s, r)) for s in range(shards) for r in range(reps)]
        return lax.ppermute(value, axes, pairs)

    to_core = functools.partial(permute, target=lambda s, r: s * reps + (r ^ 1))
    to_copy = functools.partial(permute, target=lambda s, r: s * reps + (r ^ 2))
    core = (lax.axis_index("rep") & 1).astype(i32)
    key = (lax.axis_index("shard").astype(i32) ^ core).reshape(1)
    core = core.reshape(1)

    keep, give = pack(key, owner, local_row, lookup_weight, grad_pooled.reshape(-1, width), shards, capacity)
    got = to_core(give)
    arrived = {}
    for q in reversed(range(shards // 2)):
        arrived[q] = permute(jnp.concatenate([keep[q], got[q]], axis=0),
                             lambda s, r: (s ^ (2 * q + (r & 1))) * reps + r)
    near, far = range(shards // 4), range(shards // 4, shards // 2)
    sums = add_lists(core, [arrived[q] for q in near], None, half, capacity)
    for q in far:
        sums = add_lists(core, [arrived[q]], sums, half, capacity)
    mine, other = sums
    own = (mine + to_core(other)).astype(bf16)
    own_y = to_copy(own)
    return update(core, own, own_y, to_core(own), to_core(own_y), weight, accum)


def solution(mesh):
    shards, reps = mesh.shape["shard"], mesh.shape["rep"]
    in_specs = (
        P(("shard", "rep"), None, None),
        P(("shard", "rep")),
        P(("shard", "rep"), None),
        P(("shard", "rep")),
        P("shard", None),
        P("shard"),
    )
    out_specs = (P("shard", None), P("shard"))
    paired = reps == 4 and shards == 8
    body = functools.partial(paired_body, shards, reps) if paired else general_body
    return jax.shard_map(body, mesh=mesh, in_specs=in_specs, out_specs=out_specs, check_vma=False)
```

time: 150 us -> 59.6 us (0.40)
  waiting for transfers between devices: 70.1 us -> 27.3 us
  other arithmetic: 23.1 us -> 0.16 us
  matrix products: 14.4 us -> 0 us
  Pallas kernels: 0 us -> 13.8 us
  between operations: 14.1 us -> 0.74 us
  local copies, waits for them, and re-layouts: 14.1 us -> 3.09 us
    psum x1 -> x0, waiting for transfers between devices: 50.5 us -> none  [body(): table_grad = lax.psum(partial_grad, 'rep')]
    ppermute x0 -> x9, waiting for transfers between devices: none -> 27.3 us  [permute(): return lax.ppermute(value, axes, pairs)]
    all_to_all x2 -> x0, waiting for transfers between devices: 19.6 us -> none  [the longest x1 19.6 us: body(): lax.all_to_all(outgoing.reshape(shards, capacity, width), 'shard', split_...]
    dot_general x8 -> x0, matrix products: 14.4 us -> none  [one_block(): return jnp.dot(onehot, flat_rows, preferred_element_type=jnp.float32)]
    ppermute x0 -> x9, starting transfers between devices: none -> 14.2 us  [permute(): return lax.ppermute(value, axes, pairs)]
    pallas_call x0 -> x5, Pallas kernels: none -> 13.8 us  [the longest x3 5.01 us: add_lists(): pl.pallas_call(functools.partial(add_kernel, capacity, n, before is None)...]
    all_to_all x2 -> x0, starting transfers between devices: 13.3 us -> none  [the longest x1 7.25 us: body(): lax.all_to_all(row_ids.reshape(shards, capacity), 'shard', split_axis=0,...]
    scatter x1 -> x0, local copies, waits for them, and re-layouts: 8.79 us -> none  [body(): jnp.full((shards * capacity,), -1, jnp.int32).at[slots].set(local_row)]
  transfers between devices with their start and end apart: 3 -> 9, of which waited for: 2 -> 7; matrix products, arithmetic and copies ran while one was open for 6% -> 0% of each run, Pallas kernels for 0% -> 6%
where the time goes in v1:
time: 59.6 us; the launch traced here: 59.3 us
  waiting for transfers between devices  27.3 us (46%)
  starting transfers between devices  14.2 us (24%)
  Pallas kernels  13.8 us (23%)
  local copies, waits for them, and re-layouts  3.09 us (5%)
  between operations  0.74 us (1%)
    ppermute x9, waiting for transfers between devices, permute(): return lax.ppermute(value, axes, pairs)  27.3 us
    ppermute x9, starting transfers between devices, permute(): return lax.ppermute(value, axes, pairs)  14.2 us
    pallas_call x3, Pallas kernels, add_lists(): pl.pallas_call(functools.partial(add_kernel, capacity, n, before is None)...  5.01 us
    pallas_call x1, Pallas kernels, pack(): pl.pallas_call(functools.partial(pack_kernel, groups, capacity), out_shap...  4.56 us
    pallas_call x1, Pallas kernels, update(): pl.pallas_call(functools.partial(update_kernel, steps), grid=(steps,), ou...  4.26 us
    unnamed x12, local copies, waits for them, and re-layouts  3.04 us
  transfers between devices with their start and end apart: 9, of which 7 were waited for; matrix products, arithmetic and copies ran while one was open for 0% of the time, Pallas kernels for 6%

profile of v1, /device:TPU:0, one launch (start us, length us, event | category | flops | bytes accessed | tf_op | source)
XLA Modules:
  0.0 59.3 jit_solution(2074256689497151874)
XLA Ops:
  0.6 0.0 copy-start.1
  0.6 0.9 %copy-done.1 = bf16[128,8,128]{2,1,0:T(8,128)(2,1)S(1)} copy-done((bf16[128,8,128]{2,1,0:T(8,128)(2,1)S(1)}, bf16[128,8,128]{2,1,0:T(8,128)(2,1)}, u32[]{:S(2)}) %copy-start.1) | copy-done | bytes 262168
  1.6 0.0 copy-start.3
  1.6 0.7 %copy-done.3 = s32[2048,1]{0,1:T(1,128)S(1)} copy-done((s32[2048,1]{0,1:T(1,128)S(1)}, s32[2048,1]{0,1:T(1,128)}, u32[]{:S(2)}) %copy-start.3) | copy-done | bytes 8216
  2.3 0.7 %copy-done.4 = s32[2048]{0:T(1024)S(1)} copy-done((s32[2048]{0:T(1024)S(1)}, s32[2048]{0:T(1024)}, u32[]{:S(2)}) %copy-start.4) | copy-done | bytes 8216
  3.0 0.7 %copy-done.5 = f32[2048]{0:T(1024)S(1)} copy-done((f32[2048]{0:T(1024)S(1)}, f32[2048]{0:T(1024)}, u32[]{:S(2)}) %copy-start.5) | copy-done | bytes 8216
  3.7 4.6 %pack.1 = (bf16[4,400,128]{2,1,0:T(8,128)(2,1)S(1)}, bf16[4,400,128]{2,1,0:T(8,128)(2,1)S(1)}) custom-call(s32[1]{0:T(128)} %bitcast.1.key_ref, s32[16,128]{1,0:T(8,128)S(1)} %bitcast.26, s32[16,128]{1,0:T(8,128)S(1)} %bitcast.27, f32[16,128]{1,0:T(8,128)S(1)} %bitcast.28, bf16[1024,128]{1,0:T(8,128)(2,1)S(1)} %bitcast.24), custom_call_target="tpu_custom_call" | custom-call | tf_op jit(solution)/shard_map/pack/pallas_call | solution.py:117
  8.2 0.5 collective-permute-start
  8.8 1.3 %collective-permute-done = bf16[4,400,128]{2,1,0:T(8,128)(2,1)S(1)} collective-permute-done((bf16[4,400,128]{2,1,0:T(8,128)(2,1)S(1)}, bf16[4,400,128]{2,1,0:T(8,128)(2,1)S(1)}, u32[]{:S(2)}, u32[]{:S(2)}) %collective-permute-start) | collective-permute-done | bytes 409632 | tf_op jit(solution)/shard_map/ppermute | solution.py:245
  10.2 0.7 %collective-permute-start.3 = (bf16[800,128]{1,0:T(8,128)(2,1)S(1)}, bf16[800,128]{1,0:T(8,128)(2,1)S(1)}, u32[]{:S(2)}, u32[]{:S(2)}) collective-permute-start(bf16[800,128]{1,0:T(8,128)(2,1)S(1)} %pad_maximum_fusion.2), channel_id=1, source_target_pairs={{0,0},{1,5},{2,2},{3,7},{4,4},{5,1},{6,6},{7,3},{8,8},{9,13},{10,1... | collective-permute-start | bytes 614408 | tf_op jit(solution)/shard_map/ppermute | solution.py:245
  10.9 3.0 %collective-permute-start.4 = (bf16[800,128]{1,0:T(8,128)(2,1)S(1)}, bf16[800,128]{1,0:T(8,128)(2,1)S(1)}, u32[]{:S(2)}, u32[]{:S(2)}) collective-permute-start(bf16[800,128]{1,0:T(8,128)(2,1)S(1)} %pad_maximum_fusion.3), channel_id=1, source_target_pairs={{0,8},{1,13},{2,10},{3,15},{4,12},{5,9},{6,14},{7,11},{8,0},{9,5},... | collective-permute-start | bytes 614408 | tf_op jit(solution)/shard_map/ppermute | solution.py:245
  13.9 2.7 %collective-permute-start.2 = (bf16[800,128]{1,0:T(8,128)(2,1)S(1)}, bf16[800,128]{1,0:T(8,128)(2,1)S(1)}, u32[]{:S(2)}, u32[]{:S(2)}) collective-permute-start(bf16[800,128]{1,0:T(8,128)(2,1)S(1)} %pad_maximum_fusion.1), channel_id=1, source_target_pairs={{0,16},{1,21},{2,18},{3,23},{4,20},{5,17},{6,22},{7,19},{8,24},{9,... | collective-permute-start | bytes 614408 | tf_op jit(solution)/shard_map/ppermute | solution.py:245
  16.6 0.1 collective-permute-start.1
  16.6 0.0 collective-permute-done.3.refs_0_
  16.7 1.2 %collective-permute-done.4.refs_1_ = bf16[800,128]{1,0:T(8,128)(2,1)S(1)} collective-permute-done((bf16[800,128]{1,0:T(8,128)(2,1)S(1)}, bf16[800,128]{1,0:T(8,128)(2,1)S(1)}, u32[]{:S(2)}, u32[]{:S(2)}) %collective-permute-start.4) | collective-permute-done | bytes 204832 | tf_op jit(solution)/shard_map/ppermute | solution.py:245
  17.9 2.3 %add_lists.3 = (f32[2048,128]{1,0:T(8,128)S(1)}, f32[2048,128]{1,0:T(8,128)S(1)}) custom-call(s32[1]{0:T(128)} %bitcast.core_ref, bf16[800,128]{1,0:T(8,128)(2,1)S(1)} %collective-permute-done.3.refs_0_, bf16[800,128]{1,0:T(8,128)(2,1)S(1)} %collective-permute-done.4.refs_1_), custom_call_target="tpu_custom_call" | custom-call | flops 1610612736 | bytes 4194304 | tf_op jit(solution)/shard_map/add_lists/pallas_call | solution.py:171
  20.2 2.0 %collective-permute-done.2.refs_0_ = bf16[800,128]{1,0:T(8,128)(2,1)S(1)} collective-permute-done((bf16[800,128]{1,0:T(8,128)(2,1)S(1)}, bf16[800,128]{1,0:T(8,128)(2,1)S(1)}, u32[]{:S(2)}, u32[]{:S(2)}) %collective-permute-start.2) | collective-permute-done | bytes 204832 | tf_op jit(solution)/shard_map/ppermute | solution.py:245
  22.1 1.4 %add_lists.4 = (f32[2048,128]{1,0:T(8,128)S(1)}, f32[2048,128]{1,0:T(8,128)S(1)}) custom-call(s32[1]{0:T(128)} %bitcast.core_ref, bf16[800,128]{1,0:T(8,128)(2,1)S(1)} %collective-permute-done.2.refs_0_, f32[2048,128]{1,0:T(8,128)S(1)} %get-tuple-element.14.refs_1_, ...), custom_call_target="tpu_custom_call", output_to_operand_aliasing={{0}: (2, {}), {1}: (3, {})} | custom-call | flops 805306368 | bytes 4194304 | tf_op jit(solution)/shard_map/add_lists/pallas_call | solution.py:171
  23.5 6.0 %collective-permute-done.1.refs_0_ = bf16[800,128]{1,0:T(8,128)(2,1)S(1)} collective-permute-done((bf16[800,128]{1,0:T(8,128)(2,1)S(1)}, bf16[800,128]{1,0:T(8,128)(2,1)S(1)}, u32[]{:S(2)}, u32[]{:S(2)}) %collective-permute-start.1) | collective-permute-done | bytes 204832 | tf_op jit(solution)/shard_map/ppermute | solution.py:245
  29.5 1.3 %add_lists.5 = (f32[2048,128]{1,0:T(8,128)S(1)}, f32[2048,128]{1,0:T(8,128)S(1)}) custom-call(s32[1]{0:T(128)} %bitcast.core_ref, bf16[800,128]{1,0:T(8,128)(2,1)S(1)} %collective-permute-done.1.refs_0_, f32[2048,128]{1,0:T(8,128)S(1)} %get-tuple-element.16.refs_1_, ...), custom_call_target="tpu_custom_call", output_to_operand_aliasing={{0}: (2, {}), {1}: (3, {})} | custom-call | flops 805306368 | bytes 4194304 | tf_op jit(solution)/shard_map/add_lists/pallas_call | solution.py:171
  30.9 5.6 %collective-permute-start.5 = (f32[2048,128]{1,0:T(8,128)S(1)}, f32[2048,128]{1,0:T(8,128)S(1)}, u32[]{:S(2)}, u32[]{:S(2)}) collective-permute-start(f32[2048,128]{1,0:T(8,128)S(1)} %get-tuple-element.19), channel_id=1, source_target_pairs={{0,1},{1,0},{2,3},{3,2},{4,5},{5,4},{6,7},{7,6},{8,9},{9,8},{10,11... | collective-permute-start | bytes 3145736 | tf_op jit(solution)/shard_map/ppermute | solution.py:245
  36.5 2.3 %collective-permute-done.5 = f32[2048,128]{1,0:T(8,128)S(1)} collective-permute-done((f32[2048,128]{1,0:T(8,128)S(1)}, f32[2048,128]{1,0:T(8,128)S(1)}, u32[]{:S(2)}, u32[]{:S(2)}) %collective-permute-start.5) | collective-permute-done | bytes 1048608 | tf_op jit(solution)/shard_map/ppermute | solution.py:245
  38.8 0.1 add_convert_fusion.own_ref
  38.9 1.6 %collective-permute-start.6 = (bf16[2048,128]{1,0:T(8,128)(2,1)S(1)}, bf16[2048,128]{1,0:T(8,128)(2,1)S(1)}, u32[]{:S(2)}, u32[]{:S(2)}) collective-permute-start(bf16[2048,128]{1,0:T(8,128)(2,1)S(1)} %add_convert_fusion.own_ref), channel_id=1, source_target_pairs={{0,2},{1,3},{2,0},{3,1},{4,6},{5,7},{6,4},{7,5},{8,10},{9,11},{10,... | collective-permute-start | bytes 1572872 | tf_op jit(solution)/shard_map/ppermute | solution.py:245
  40.5 0.1 collective-permute-start.7
  40.5 12.6 %collective-permute-done.6.own_y_ref = bf16[2048,128]{1,0:T(8,128)(2,1)S(1)} collective-permute-done((bf16[2048,128]{1,0:T(8,128)(2,1)S(1)}, bf16[2048,128]{1,0:T(8,128)(2,1)S(1)}, u32[]{:S(2)}, u32[]{:S(2)}) %collective-permute-start.6) | collective-permute-done | bytes 524320 | tf_op jit(solution)/shard_map/ppermute | solution.py:245
  53.1 0.0 collective-permute-start.8
  53.1 0.0 collective-permute-done.7.other_ref
  53.1 1.9 %collective-permute-done.8.other_y_ref = bf16[2048,128]{1,0:T(8,128)(2,1)S(1)} collective-permute-done((bf16[2048,128]{1,0:T(8,128)(2,1)S(1)}, bf16[2048,128]{1,0:T(8,128)(2,1)S(1)}, u32[]{:S(2)}, u32[]{:S(2)}) %collective-permute-start.8) | collective-permute-done | bytes 524320 | tf_op jit(solution)/shard_map/ppermute | solution.py:245
  55.0 0.0 copy-done
  55.0 0.0 copy-done.2
  55.0 4.3 %update.1 = (f32[4096,128]{1,0:T(8,128)}, f32[32,128]{1,0:T(8,128)}) custom-call(s32[1]{0:T(128)} %bitcast.core_ref, bf16[2048,128]{1,0:T(8,128)(2,1)S(1)} %add_convert_fusion.own_ref, bf16[2048,128]{1,0:T(8,128)(2,1)S(1)} %collective-permute-done.6.own_y_ref, bf16[2048,128]{1,0:T(8,128)(2,1)S(1)} %collective-permute-done.7.other_ref, ...), custom_call_target="tpu_custom_call" | custom-call | tf_op jit(solution)/shard_map/update/pallas_call | solution.py:222
  (10 shorter events, 0.1 us)
Async XLA Ops:
  0.6 1.0 %copy-start.1 = (bf16[128,8,128]{2,1,0:T(8,128)(2,1)S(1)}, bf16[128,8,128]{2,1,0:T(8,128)(2,1)}, u32[]{:S(2)}) copy-start(bf16[128,8,128]{2,1,0:T(8,128)(2,1)} %param.6) | copy-start | bytes 786436
  1.6 0.7 %copy-start.3 = (s32[2048,1]{0,1:T(1,128)S(1)}, s32[2048,1]{0,1:T(1,128)}, u32[]{:S(2)}) copy-start(s32[2048,1]{0,1:T(1,128)} %param.8) | copy-start | bytes 24580
  2.3 0.7 %copy-start.4 = (s32[2048]{0:T(1024)S(1)}, s32[2048]{0:T(1024)}, u32[]{:S(2)}) copy-start(s32[2048]{0:T(1024)} %param.9) | copy-start | bytes 24580
  3.0 0.7 %copy-start.5 = (f32[2048]{0:T(1024)S(1)}, f32[2048]{0:T(1024)}, u32[]{:S(2)}) copy-start(f32[2048]{0:T(1024)} %param.7) | copy-start | bytes 24580
  8.2 1.9 %collective-permute-start = (bf16[4,400,128]{2,1,0:T(8,128)(2,1)S(1)}, bf16[4,400,128]{2,1,0:T(8,128)(2,1)S(1)}, u32[]{:S(2)}, u32[]{:S(2)}) collective-permute-start(bf16[4,400,128]{2,1,0:T(8,128)(2,1)S(1)} %get-tuple-element.13), channel_id=1, source_target_pairs={{0,1},{1,0},{2,3},{3,2},{4,5},{5,4},{6,7},{7,6},{8,9},{9,8},{10,11... | collective-permute-start | bytes 1228808 | tf_op jit(solution)/shard_map/ppermute | solution.py:245
  10.2 6.5 %collective-permute-start.3 = (bf16[800,128]{1,0:T(8,128)(2,1)S(1)}, bf16[800,128]{1,0:T(8,128)(2,1)S(1)}, u32[]{:S(2)}, u32[]{:S(2)}) collective-permute-start(bf16[800,128]{1,0:T(8,128)(2,1)S(1)} %pad_maximum_fusion.2), channel_id=1, source_target_pairs={{0,0},{1,5},{2,2},{3,7},{4,4},{5,1},{6,6},{7,3},{8,8},{9,13},{10,1... | collective-permute-start | bytes 614408 | tf_op jit(solution)/shard_map/ppermute | solution.py:245
  10.9 7.0 %collective-permute-start.4 = (bf16[800,128]{1,0:T(8,128)(2,1)S(1)}, bf16[800,128]{1,0:T(8,128)(2,1)S(1)}, u32[]{:S(2)}, u32[]{:S(2)}) collective-permute-start(bf16[800,128]{1,0:T(8,128)(2,1)S(1)} %pad_maximum_fusion.3), channel_id=1, source_target_pairs={{0,8},{1,13},{2,10},{3,15},{4,12},{5,9},{6,14},{7,11},{8,0},{9,5},... | collective-permute-start | bytes 614408 | tf_op jit(solution)/shard_map/ppermute | solution.py:245
  13.9 8.2 %collective-permute-start.2 = (bf16[800,128]{1,0:T(8,128)(2,1)S(1)}, bf16[800,128]{1,0:T(8,128)(2,1)S(1)}, u32[]{:S(2)}, u32[]{:S(2)}) collective-permute-start(bf16[800,128]{1,0:T(8,128)(2,1)S(1)} %pad_maximum_fusion.1), channel_id=1, source_target_pairs={{0,16},{1,21},{2,18},{3,23},{4,20},{5,17},{6,22},{7,19},{8,24},{9,... | collective-permute-start | bytes 614408 | tf_op jit(solution)/shard_map/ppermute | solution.py:245
  16.6 12.9 %collective-permute-start.1 = (bf16[800,128]{1,0:T(8,128)(2,1)S(1)}, bf16[800,128]{1,0:T(8,128)(2,1)S(1)}, u32[]{:S(2)}, u32[]{:S(2)}) collective-permute-start(bf16[800,128]{1,0:T(8,128)(2,1)S(1)} %pad_maximum_fusion), channel_id=1, source_target_pairs={{0,24},{1,29},{2,26},{3,31},{4,28},{5,25},{6,30},{7,27},{8,16},{9,... | collective-permute-start | bytes 614408 | tf_op jit(solution)/shard_map/ppermute | solution.py:245
  29.5 25.5 %copy-start = (f32[4096,128]{1,0:T(8,128)S(1)}, f32[4096,128]{1,0:T(8,128)}, u32[]{:S(2)}) copy-start(f32[4096,128]{1,0:T(8,128)} %weight_ref.1) | copy-start | bytes 6291460
  29.5 25.5 %copy-start.2 = (f32[4096]{0:T(1024)S(1)}, f32[4096]{0:T(1024)}, u32[]{:S(2)}) copy-start(f32[4096]{0:T(1024)} %param.11) | copy-start | bytes 49156
  30.9 7.9 %collective-permute-start.5 = (f32[2048,128]{1,0:T(8,128)S(1)}, f32[2048,128]{1,0:T(8,128)S(1)}, u32[]{:S(2)}, u32[]{:S(2)}) collective-permute-start(f32[2048,128]{1,0:T(8,128)S(1)} %get-tuple-element.19), channel_id=1, source_target_pairs={{0,1},{1,0},{2,3},{3,2},{4,5},{5,4},{6,7},{7,6},{8,9},{9,8},{10,11... | collective-permute-start | bytes 3145736 | tf_op jit(solution)/shard_map/ppermute | solution.py:245
  38.9 14.3 %collective-permute-start.6 = (bf16[2048,128]{1,0:T(8,128)(2,1)S(1)}, bf16[2048,128]{1,0:T(8,128)(2,1)S(1)}, u32[]{:S(2)}, u32[]{:S(2)}) collective-permute-start(bf16[2048,128]{1,0:T(8,128)(2,1)S(1)} %add_convert_fusion.own_ref), channel_id=1, source_target_pairs={{0,2},{1,3},{2,0},{3,1},{4,6},{5,7},{6,4},{7,5},{8,10},{9,11},{10,... | collective-permute-start | bytes 1572872 | tf_op jit(solution)/shard_map/ppermute | solution.py:245
  40.5 12.7 %collective-permute-start.7 = (bf16[2048,128]{1,0:T(8,128)(2,1)S(1)}, bf16[2048,128]{1,0:T(8,128)(2,1)S(1)}, u32[]{:S(2)}, u32[]{:S(2)}) collective-permute-start(bf16[2048,128]{1,0:T(8,128)(2,1)S(1)} %add_convert_fusion.own_ref), channel_id=1, source_target_pairs={{0,1},{1,0},{2,3},{3,2},{4,5},{5,4},{6,7},{7,6},{8,9},{9,8},{10,11... | collective-permute-start | bytes 1572872 | tf_op jit(solution)/shard_map/ppermute | solution.py:245
  53.1 1.9 %collective-permute-start.8 = (bf16[2048,128]{1,0:T(8,128)(2,1)S(1)}, bf16[2048,128]{1,0:T(8,128)(2,1)S(1)}, u32[]{:S(2)}, u32[]{:S(2)}) collective-permute-start(bf16[2048,128]{1,0:T(8,128)(2,1)S(1)} %collective-permute-done.6.own_y_ref), channel_id=1, source_target_pairs={{0,1},{1,0},{2,3},{3,2},{4,5},{5,4},{6,7},{7,6},{8,9},{9,8},{10,11... | collective-permute-start | bytes 1572872 | tf_op jit(solution)/shard_map/ppermute | solution.py:245

commit v2 on v0

v2 whole, which is shorter than its diff:
```python
import functools

import jax
import jax.numpy as jnp
from jax import lax
from jax.experimental import pallas as pl
from jax.experimental.pallas import tpu as pltpu
from jax.sharding import PartitionSpec as P

step_size = 0.25
epsilon = 1e-08
f32, bf16, i32 = jnp.float32, jnp.bfloat16, jnp.int32
LANES = 128
PAD = 16
VMEM_LIMIT = 48 * 1024 * 1024
MEDIUM = pl.CostEstimate(flops=100_000_000, bytes_accessed=1024, transcendentals=0)
SMALL = pl.CostEstimate(flops=1024, bytes_accessed=1024, transcendentals=0)


def adagrad(weight, accum, table_grad):
    new_accum = accum + jnp.mean(table_grad * table_grad, axis=1)
    new_weight = weight - step_size * table_grad / (jnp.sqrt(new_accum)[:, None] + epsilon)
    return (new_weight, new_accum)


def general_body(grad_pooled, lookup_weight, owner, local_row, weight, accum):
    width = grad_pooled.shape[-1]
    lookups = lookup_weight.shape[0]
    pooling = lookups // (grad_pooled.shape[0] * grad_pooled.shape[1])
    shards = lax.axis_size("shard")
    capacity = (3 * lookups + 2 * shards - 1) // (2 * shards)
    bags = grad_pooled.reshape(-1, width).astype(f32)
    rows = (bags[:, None, :] * lookup_weight.reshape(-1, pooling, 1)).reshape(lookups, width)
    rows = rows.astype(bf16)
    target_shard = owner[:, 0]
    hits = (target_shard[:, None] == jnp.arange(shards, dtype=i32)[None, :]).astype(i32)
    ranks = jnp.sum(jnp.cumsum(hits, axis=0) * hits, axis=1) - 1
    slots = target_shard * capacity + ranks
    outgoing = jnp.zeros((shards * capacity, width), bf16).at[slots].set(rows)
    row_ids = jnp.full((shards * capacity,), -1, i32).at[slots].set(local_row)
    received, received_ids = (
        lax.all_to_all(outgoing.reshape(shards, capacity, width), "shard", split_axis=0, concat_axis=0, tiled=True),
        lax.all_to_all(row_ids.reshape(shards, capacity), "shard", split_axis=0, concat_axis=0, tiled=True),
    )
    flat_rows = received.reshape(-1, width)
    flat_ids = received_ids.reshape(-1)
    window_rows = weight.shape[0]
    span = 512
    starts = jnp.arange(window_rows // span, dtype=i32) * span

    def one_block(start):
        shifted = flat_ids - start
        onehot = (jnp.arange(span, dtype=i32)[:, None] == shifted[None, :]).astype(bf16)
        return jnp.dot(onehot, flat_rows, preferred_element_type=f32)

    partial_grad = lax.map(one_block, starts).reshape(window_rows, width)
    table_grad = lax.psum(partial_grad, "rep")
    return adagrad(weight, accum, table_grad)


def iota(shape, dim, dtype=i32):
    return lax.broadcasted_iota(i32, shape, dim).astype(dtype)


def pack_groups(groups, capacity, wanted, slot, ext_ref, out_ref):
    blocks = slot.shape[0]
    chunks = capacity // LANES
    place = iota((LANES, LANES), 0, f32)
    for n, g in enumerate(wanted):
        high, low = [], []
        for k in range(chunks):
            moved = slot - float(g * capacity + k * LANES)
            picks = jnp.concatenate(
                [(place == moved[r:r + 1, :]).astype(bf16) for r in range(blocks)], axis=1)
            packed = jnp.dot(picks, ext_ref[...], preferred_element_type=f32)
            out_ref[n, k * LANES:(k + 1) * LANES, :] = packed[:, :LANES].astype(bf16)
            turned = packed[:, LANES:].T
            high.append(turned[0:1])
            low.append(turned[1:2])
        out_ref[n, capacity:capacity + PAD, :] = jnp.concatenate(
            high + low + [jnp.zeros((PAD - 2 * chunks, LANES), f32)], axis=0).astype(bf16)


def first_kernel(groups, capacity, wanted, facts_ref, bags_ref, out_ref, slot_ref, ext_ref):
    blocks = slot_ref.shape[0]
    wide = groups * blocks
    upper = (iota((LANES, LANES), 0) <= iota((LANES, LANES), 1)).astype(bf16)
    at, to = iota((wide, wide), 0), iota((wide, wide), 1)
    earlier = ((at // blocks == to // blocks) & (to < at)).astype(bf16)
    lane = iota((LANES, LANES), 1)
    repeat = ((iota((LANES, LANES // 2), 0) >> 1) == iota((LANES, LANES // 2), 1)).astype(bf16)
    group = facts_ref[0:blocks, :]
    hits = [(group == float(g)).astype(f32) for g in range(groups)]
    stacked = jnp.concatenate(hits, axis=0).astype(bf16)
    inside = jnp.dot(stacked, upper, preferred_element_type=f32)
    totals = jnp.dot(stacked, jnp.ones((LANES, LANES), bf16), preferred_element_type=f32)
    carry = jnp.dot(earlier, totals.astype(bf16), preferred_element_type=f32)
    rank = inside + carry - 1.0
    slot = jnp.zeros((blocks, LANES), f32)
    for g in range(groups):
        slot = slot + hits[g] * (rank[g * blocks:(g + 1) * blocks] + float(g * capacity))
    slot_ref[...] = slot

    columns = jnp.concatenate(
        [facts_ref[blocks:4 * blocks, :], jnp.zeros((LANES - 3 * blocks, LANES), f32)], axis=0).T
    for r in range(blocks):
        bag = jnp.dot(repeat, bags_ref[r * LANES // 2:(r + 1) * LANES // 2, :], preferred_element_type=f32)
        here = slice(r * LANES, (r + 1) * LANES)
        ext_ref[here, 0:LANES] = (bag * columns[:, 2 * blocks + r:2 * blocks + r + 1]).astype(bf16)
        high, low = columns[:, r:r + 1], columns[:, blocks + r:blocks + r + 1]
        ext_ref[here, LANES:2 * LANES] = jnp.where(
            lane == 0, high, jnp.where(lane == 1, low, 0.0)).astype(bf16)
    pack_groups(groups, capacity, wanted, slot, ext_ref, out_ref)


def next_kernel(groups, capacity, wanted, slot_ref, ext_ref, *refs):
    out_ref = refs[-1]
    pack_groups(groups, capacity, wanted, slot_ref[...], ext_ref, out_ref)


def listed(wanted, capacity):
    return jax.ShapeDtypeStruct((len(wanted), capacity + PAD, LANES), bf16)


def pack_first(facts, bags, groups, capacity, wanted):
    blocks = facts.shape[0] // 4
    vmem = pl.BlockSpec(memory_space=pltpu.VMEM)
    return pl.pallas_call(
        functools.partial(first_kernel, groups, capacity, wanted),
        out_shape=[listed(wanted, capacity), jax.ShapeDtypeStruct((blocks, LANES), f32),
                   jax.ShapeDtypeStruct((blocks * LANES, 2 * LANES), bf16)],
        in_specs=[vmem, vmem],
        out_specs=[vmem, vmem, vmem],
        compiler_params=pltpu.CompilerParams(vmem_limit_bytes=VMEM_LIMIT),
        name="pack_first",
    )(facts, bags)


def pack_next(slot, ext, groups, capacity, wanted, after=()):
    vmem = pl.BlockSpec(memory_space=pltpu.VMEM)
    return pl.pallas_call(
        functools.partial(next_kernel, groups, capacity, wanted),
        out_shape=listed(wanted, capacity),
        in_specs=[vmem, vmem] + [pl.BlockSpec(memory_space=pl.ANY)] * len(after),
        out_specs=vmem,
        compiler_params=pltpu.CompilerParams(vmem_limit_bytes=VMEM_LIMIT),
        cost_estimate=SMALL,
        name="pack_next",
    )(slot, ext, *after)


def add_kernel(capacity, lists, first, last, *refs):
    in_refs, refs = refs[:lists], list(refs[lists:])
    before = None if first else refs.pop(0)
    beside = refs.pop(0) if last else None
    out_ref, rhs_ref = refs
    half = out_ref.shape[0]
    chunks = capacity // LANES
    highs, lows = [], []
    at = 0
    for ref in in_refs:
        for part in range(ref.shape[0] // (capacity + PAD)):
            base = part * (capacity + PAD)
            digits = ref[base + capacity:base + capacity + PAD, :].astype(f32)
            high = digits[0:chunks]
            upper = (high >= float(half // 256)).astype(f32)
            high = high - upper * float(half // 256)
            highs += [high[k:k + 1] for k in range(chunks)]
            lows += [digits[chunks + k:chunks + k + 1] for k in range(chunks)]
            turned = jnp.concatenate([upper, jnp.zeros((LANES - chunks, LANES), f32)], axis=0).T
            for k in range(chunks):
                rows = ref[base + k * LANES:base + (k + 1) * LANES, :].astype(f32)
                above = turned[:, k:k + 1] > 0.5
                here = slice(at, at + LANES)
                rhs_ref[here, 0:LANES] = jnp.where(above, 0.0, rows).astype(bf16)
                rhs_ref[here, LANES:2 * LANES] = jnp.where(above, rows, 0.0).astype(bf16)
                at += LANES
    place = iota((256, LANES), 0, f32)
    for h in range(half // 256):
        picks = jnp.concatenate(
            [(place == jnp.where(hi == float(h), lo, -1.0)).astype(bf16) for hi, lo in zip(highs, lows)], axis=1)
        part = jnp.dot(picks, rhs_ref[...], preferred_element_type=f32)
        here = slice(h * 256, (h + 1) * 256)
        if before is not None:
            part = part + before[here, :]
        if beside is not None:
            part = part + beside[here, :]
        out_ref[here, :] = part.astype(out_ref.dtype)


def add_lists(lists, before, beside, half, capacity):
    vmem = pl.BlockSpec(memory_space=pltpu.VMEM)
    n = len(lists)
    depth = sum(value.shape[0] for value in lists) // (capacity + PAD) * capacity
    more = [value for value in (before, beside) if value is not None]
    return pl.pallas_call(
        functools.partial(add_kernel, capacity, n, before is None, beside is not None),
        out_shape=jax.ShapeDtypeStruct((half, 2 * LANES), f32 if beside is None else bf16),
        in_specs=[vmem] * (n + len(more)),
        out_specs=vmem,
        scratch_shapes=[pltpu.VMEM((depth, 2 * LANES), bf16)],
        input_output_aliases={n: 0} if beside is None and before is not None else {},
        compiler_params=pltpu.CompilerParams(vmem_limit_bytes=VMEM_LIMIT),
        cost_estimate=MEDIUM,
        name="add_lists",
    )(*lists, *more)


def update_kernel(own_ref, other_ref, weight_ref, accum_ref, new_weight_hbm, new_accum_ref, out_ref, sems):
    blocks = accum_ref.shape[0]
    half = own_ref.shape[0]
    parts = 4
    span = blocks // parts
    lane = iota((LANES, LANES), 1)

    def grad(b):
        top = (b * LANES) % half
        side = (b * LANES) // half
        at, to = slice(top, top + LANES), slice(side * LANES, (side + 1) * LANES)
        return own_ref[at, to].astype(f32) + other_ref[at, to].astype(f32)

    old = jnp.concatenate([accum_ref[...], jnp.zeros((LANES - blocks, LANES), f32)], axis=0).T
    new = old
    copies = []
    for p in range(parts):
        for b in range(p * span, (p + 1) * span):
            g = grad(b)
            new = jnp.where(lane == b, new + jnp.sum(g * g, axis=1, keepdims=True) * (1.0 / LANES), new)
        scale = step_size / (jnp.sqrt(new) + epsilon)
        for b in range(p * span, (p + 1) * span):
            here = slice(b * LANES, (b + 1) * LANES)
            out_ref[here, :] = weight_ref[here, :] - grad(b) * scale[:, b:b + 1]
        rows = slice(p * span * LANES, (p + 1) * span * LANES)
        copies.append(pltpu.make_async_copy(out_ref.at[rows], new_weight_hbm.at[rows], sems.at[p]))
        copies[-1].start()
    new_accum_ref[...] = new.T[:blocks]
    for copy in copies:
        copy.wait()


def update(own, other, weight, accum):
    rows = weight.shape[0]
    blocks = rows // LANES
    vmem, hbm = pl.BlockSpec(memory_space=pltpu.VMEM), pl.BlockSpec(memory_space=pltpu.HBM)
    new_weight, new_accum = pl.pallas_call(
        update_kernel,
        out_shape=[jax.ShapeDtypeStruct(weight.shape, f32), jax.ShapeDtypeStruct((blocks, LANES), f32)],
        in_specs=[vmem, vmem, vmem, vmem],
        out_specs=[hbm, vmem],
        scratch_shapes=[pltpu.VMEM(weight.shape, f32), pltpu.SemaphoreType.DMA((4,))],
        compiler_params=pltpu.CompilerParams(vmem_limit_bytes=VMEM_LIMIT),
        name="update",
    )(own, other, weight, accum.reshape(blocks, LANES))
    return new_weight, new_accum.reshape(-1)


def tied(value, after):
    return value + (after[-1:, 0:LANES] * 0.0).astype(value.dtype)


def paired_body(shards, reps, grad_pooled, lookup_weight, owner, local_row, weight, accum):
    width = grad_pooled.shape[-1]
    lookups = lookup_weight.shape[0]
    capacity = (3 * lookups + 2 * shards - 1) // (2 * shards)
    half = weight.shape[0] // 2
    axes = ("shard", "rep")

    def permute(value, target):
        pairs = [(s * reps + r, target(s, r)) for s in range(shards) for r in range(reps)]
        return lax.ppermute(value, axes, pairs)

    to_core = functools.partial(permute, target=lambda s, r: s * reps + (r ^ 1))
    to_copy = functools.partial(permute, target=lambda s, r: s * reps + (r ^ 2))
    key = lax.axis_index("shard").astype(i32) ^ (lax.axis_index("rep").astype(i32) & 1)
    blocks = lookups // LANES
    local_row = local_row.reshape(blocks, LANES)
    facts = jnp.concatenate(
        [(owner.reshape(blocks, LANES) ^ key).astype(f32), (local_row >> 8).astype(f32),
         (local_row & 255).astype(f32), lookup_weight.reshape(blocks, LANES)], axis=0)

    near = list(range(shards // 4))
    far = list(range(shards // 4, shards // 2))
    phases = [far[1:], near + far[:1]]
    order = [near, far[1:], far[:1]]
    before, arrived = (), {}
    for n, qs in enumerate(phases):
        give, hold = [2 * q + 1 for q in qs], [2 * q for q in qs]
        if n == 0:
            given, slot, ext = pack_first(facts, grad_pooled.reshape(-1, width), shards, capacity, give)
        else:
            given = pack_next(slot, ext, shards, capacity, give, before)
        got = to_core(given)
        keep = pack_next(slot, ext, shards, capacity, hold, before)
        before = [jnp.concatenate([keep[n], got[n]], axis=0) for n in range(len(qs))]
        for q, payload in zip(qs, before):
            arrived[q] = permute(payload, lambda s, r: (s ^ (2 * q + (r & 1))) * reps + r)

    own = copy = None
    for n, qs in enumerate(order):
        here = jnp.concatenate([arrived[q] for q in qs], axis=0)
        if own is not None:
            here = tied(here, own)
        there = to_copy(here)
        own = add_lists([here], own, None, half, capacity)
        copy = add_lists([there], copy, own if n == 2 else None, half, capacity)
    return update(copy, to_core(copy), weight, accum)


def solution(mesh):
    shards, reps = mesh.shape["shard"], mesh.shape["rep"]
    in_specs = (
        P(("shard", "rep"), None, None),
        P(("shard", "rep")),
        P(("shard", "rep"), None),
        P(("shard", "rep")),
        P("shard", None),
        P("shard"),
    )
    out_specs = (P("shard", None), P("shard"))
    paired = reps == 4 and shards == 8
    body = functools.partial(paired_body, shards, reps) if paired else general_body
    return jax.shard_map(body, mesh=mesh, in_specs=in_specs, out_specs=out_specs, check_vma=False)
```

time: 150 us -> 53.3 us (0.36)
  the two profiles are of different devices: /device:TPU:0 before, /device:TPU:29 now
where the time goes in v2:
time: 53.3 us; the launch traced here: 52.9 us
  Pallas kernels  18.8 us (35%)
  waiting for transfers between devices  18.3 us (34%)
  starting transfers between devices  11.6 us (22%)
  other arithmetic  2.21 us (4%)
  local copies, waits for them, and re-layouts  1.05 us (2%)
  between operations  0.96 us (2%)
    ppermute x10, waiting for transfers between devices, permute(): return lax.ppermute(value, axes, pairs)  18.3 us
    ppermute x10, starting transfers between devices, permute(): return lax.ppermute(value, axes, pairs)  11.6 us
    pallas_call x6, Pallas kernels, add_lists(): pl.pallas_call(functools.partial(add_kernel, capacity, n, before is None,...  10.6 us
    pallas_call x3, Pallas kernels, pack_next(): pl.pallas_call(functools.partial(next_kernel, groups, capacity, wanted),...  3.49 us
    pallas_call x1, Pallas kernels, update(): pl.pallas_call(update_kernel, out_shape=[jax.ShapeDtypeStruct(weight.shap...  3.16 us
    pallas_call x1, Pallas kernels, pack_first(): pl.pallas_call(functools.partial(first_kernel, groups, capacity, wanted),...  1.51 us
  transfers between devices with their start and end apart: 10, of which 7 were waited for; matrix products, arithmetic and copies ran while one was open for 0% of the time, Pallas kernels for 21%

profile of v2, /device:TPU:29, one launch (start us, length us, event | category | flops | bytes accessed | tf_op | source)
XLA Modules:
  0.0 52.9 jit_solution(4774845132398071624)
XLA Ops:
  0.6 0.7 %convert_bitcast_fusion.1 = (f32[16,128]{1,0:T(8,128)S(1)}, f32[16,128]{1,0:T(8,128)S(1)}) fusion(s32[2048]{0:T(1024)} %param.9), kind=kLoop, calls=%fused_computation.14 | loop fusion | flops 8192 | bytes 24576 | tf_op jit(solution)/shard_map/convert_element_type | solution.py:278
  1.3 0.7 %xor_convert_fusion = f32[2048,1]{0,1:T(1,128)S(1)} fusion(s32[2048,1]{0,1:T(1,128)} %param.8, s32[]{:T(128)S(6)} %xor.10), kind=kLoop, calls=%fused_computation.15 | loop fusion | flops 4096 | bytes 16388 | tf_op jit(solution)/shard_map/convert_element_type | solution.py:278
  2.0 0.7 %pad_maximum_fusion.4.facts_ref = f32[64,128]{1,0:T(8,128)S(1)} fusion(f32[16,128]{1,0:T(8,128)} %bitcast.32, f32[16,128]{1,0:T(8,128)S(1)} %get-tuple-element.19, f32[16,128]{1,0:T(8,128)S(1)} %get-tuple-element.18, f32[16,128]{1,0:T(8,128)S(1)} %bitcast.31), kind=kLoop, calls=%fused_computation.12 | loop fusion | flops 24576 | bytes 65536 | tf_op jit(solution)/shard_map/concatenate | solution.py:277
  2.7 0.9 %copy-done.1 = bf16[128,8,128]{2,1,0:T(8,128)(2,1)S(1)} copy-done((bf16[128,8,128]{2,1,0:T(8,128)(2,1)S(1)}, bf16[128,8,128]{2,1,0:T(8,128)(2,1)}, u32[]{:S(2)}) %copy-start.1) | copy-done | bytes 262168
  3.7 1.5 %pack_first.1 = (bf16[1,400,128]{2,1,0:T(8,128)(2,1)S(1)}, f32[16,128]{1,0:T(8,128)S(1)}, bf16[2048,256]{1,0:T(8,128)(2,1)S(1)}) custom-call(f32[64,128]{1,0:T(8,128)S(1)} %pad_maximum_fusion.4.facts_ref, bf16[1024,128]{1,0:T(8,128)(2,1)S(1)} %bitcast.28), custom_call_target="tpu_custom_call" | custom-call | tf_op jit(solution)/shard_map/pack_first/pallas_call | solution.py:128
  5.2 0.7 %collective-permute-start = (bf16[1,400,128]{2,1,0:T(8,128)(2,1)S(1)}, bf16[1,400,128]{2,1,0:T(8,128)(2,1)S(1)}, u32[]{:S(2)}, u32[]{:S(2)}) collective-permute-start(bf16[1,400,128]{2,1,0:T(8,128)(2,1)S(1)} %get-tuple-element.9), channel_id=1, source_target_pairs={{0,1},{1,0},{2,3},{3,2},{4,5},{5,4},{6,7},{7,6},{8,9},{9,8},{10,11... | collective-permute-start | bytes 307208 | tf_op jit(solution)/shard_map/ppermute | solution.py:270
  5.9 0.6 %pack_next.3 = bf16[1,400,128]{2,1,0:T(8,128)(2,1)S(1)} custom-call(f32[16,128]{1,0:T(8,128)S(1)} %get-tuple-element.7.slot_ref, bf16[2048,256]{1,0:T(8,128)(2,1)S(1)} %get-tuple-element.8.ext_ref), custom_call_target="tpu_custom_call" | custom-call | flops 1024 | bytes 1024 | tf_op jit(solution)/shard_map/pack_next/pallas_call | solution.py:141
  6.6 0.3 collective-permute-done
  6.9 1.4 %pack_next.5 = bf16[3,400,128]{2,1,0:T(8,128)(2,1)S(1)} custom-call(f32[16,128]{1,0:T(8,128)S(1)} %get-tuple-element.7.slot_ref, bf16[2048,256]{1,0:T(8,128)(2,1)S(1)} %get-tuple-element.8.ext_ref, bf16[800,128]{1,0:T(8,128)(2,1)S(1)} %pad_maximum_fusion.refs_0_), custom_call_target="tpu_custom_call" | custom-call | flops 1024 | bytes 1024 | tf_op jit(solution)/shard_map/pack_next/pallas_call | solution.py:141
  8.3 0.4 collective-permute-start.1
  8.7 0.9 %collective-permute-start.3 = (bf16[800,128]{1,0:T(8,128)(2,1)S(1)}, bf16[800,128]{1,0:T(8,128)(2,1)S(1)}, u32[]{:S(2)}, u32[]{:S(2)}) collective-permute-start(bf16[800,128]{1,0:T(8,128)(2,1)S(1)} %pad_maximum_fusion.refs_0_), channel_id=1, source_target_pairs={{0,24},{1,29},{2,26},{3,31},{4,28},{5,25},{6,30},{7,27},{8,16},{9,... | collective-permute-start | bytes 614408 | tf_op jit(solution)/shard_map/ppermute | solution.py:270
  9.6 1.4 %pack_next.4 = bf16[3,400,128]{2,1,0:T(8,128)(2,1)S(1)} custom-call(f32[16,128]{1,0:T(8,128)S(1)} %get-tuple-element.7.slot_ref, bf16[2048,256]{1,0:T(8,128)(2,1)S(1)} %get-tuple-element.8.ext_ref, bf16[800,128]{1,0:T(8,128)(2,1)S(1)} %pad_maximum_fusion.refs_0_), custom_call_target="tpu_custom_call" | custom-call | flops 1024 | bytes 1024 | tf_op jit(solution)/shard_map/pack_next/pallas_call | solution.py:141
  11.1 2.4 %collective-permute-start.4 = (bf16[800,128]{1,0:T(8,128)(2,1)S(1)}, bf16[800,128]{1,0:T(8,128)(2,1)S(1)}, u32[]{:S(2)}, u32[]{:S(2)}) collective-permute-start(bf16[800,128]{1,0:T(8,128)(2,1)S(1)} %pad_maximum_fusion.2), channel_id=1, source_target_pairs={{0,0},{1,5},{2,2},{3,7},{4,4},{5,1},{6,6},{7,3},{8,8},{9,13},{10,1... | collective-permute-start | bytes 614408 | tf_op jit(solution)/shard_map/ppermute | solution.py:270
  13.6 1.3 %collective-permute-start.5 = (bf16[800,128]{1,0:T(8,128)(2,1)S(1)}, bf16[800,128]{1,0:T(8,128)(2,1)S(1)}, u32[]{:S(2)}, u32[]{:S(2)}) collective-permute-start(bf16[800,128]{1,0:T(8,128)(2,1)S(1)} %pad_maximum_fusion.3), channel_id=1, source_target_pairs={{0,8},{1,13},{2,10},{3,15},{4,12},{5,9},{6,14},{7,11},{8,0},{9,5},... | collective-permute-start | bytes 614408 | tf_op jit(solution)/shard_map/ppermute | solution.py:270
  14.9 3.2 %collective-permute-start.2 = (bf16[800,128]{1,0:T(8,128)(2,1)S(1)}, bf16[800,128]{1,0:T(8,128)(2,1)S(1)}, u32[]{:S(2)}, u32[]{:S(2)}) collective-permute-start(bf16[800,128]{1,0:T(8,128)(2,1)S(1)} %pad_maximum_fusion.1), channel_id=1, source_target_pairs={{0,16},{1,21},{2,18},{3,23},{4,20},{5,17},{6,22},{7,19},{8,24},{9,... | collective-permute-start | bytes 614408 | tf_op jit(solution)/shard_map/ppermute | solution.py:270
  18.2 1.3 %collective-permute-done.4 = bf16[800,128]{1,0:T(8,128)(2,1)S(1)} collective-permute-done((bf16[800,128]{1,0:T(8,128)(2,1)S(1)}, bf16[800,128]{1,0:T(8,128)(2,1)S(1)}, u32[]{:S(2)}, u32[]{:S(2)}) %collective-permute-start.4) | collective-permute-done | bytes 204832 | tf_op jit(solution)/shard_map/ppermute | solution.py:270
  19.5 5.7 %collective-permute-done.5 = bf16[800,128]{1,0:T(8,128)(2,1)S(1)} collective-permute-done((bf16[800,128]{1,0:T(8,128)(2,1)S(1)}, bf16[800,128]{1,0:T(8,128)(2,1)S(1)}, u32[]{:S(2)}, u32[]{:S(2)}) %collective-permute-start.5) | collective-permute-done | bytes 204832 | tf_op jit(solution)/shard_map/ppermute | solution.py:270
  25.2 0.3 collective-permute-start.8
  25.4 2.3 %add_lists.6.refs_1_ = f32[2048,256]{1,0:T(8,128)S(1)} custom-call(bf16[1600,128]{1,0:T(8,128)(2,1)S(1)} %constant_dynamic-update-slice_fusion.refs_0_), custom_call_target="tpu_custom_call" | custom-call | flops 100000000 | bytes 1024 | tf_op jit(solution)/shard_map/add_lists/pallas_call | solution.py:196
  27.8 1.5 %add_lists.7.refs_1_ = f32[2048,256]{1,0:T(8,128)S(1)} custom-call(bf16[800,128]{1,0:T(8,128)(2,1)S(1)} %broadcast_add_fusion.1.refs_0_, f32[2048,256]{1,0:T(8,128)S(1)} %add_lists.6.refs_1_), custom_call_target="tpu_custom_call", output_to_operand_aliasing={{}: (1, {})} | custom-call | flops 100000000 | bytes 1024 | tf_op jit(solution)/shard_map/add_lists/pallas_call | solution.py:196
  29.3 1.3 %collective-permute-start.7 = (bf16[800,128]{1,0:T(8,128)(2,1)S(1)}, bf16[800,128]{1,0:T(8,128)(2,1)S(1)}, u32[]{:S(2)}, u32[]{:S(2)}) collective-permute-start(bf16[800,128]{1,0:T(8,128)(2,1)S(1)} %broadcast_add_fusion.1.refs_0_), channel_id=1, source_target_pairs={{0,2},{1,3},{2,0},{3,1},{4,6},{5,7},{6,4},{7,5},{8,10},{9,11},{10,... | collective-permute-start | bytes 614408 | tf_op jit(solution)/shard_map/ppermute | solution.py:270
  30.7 0.3 collective-permute-start.6
  31.0 1.5 %add_lists.10.refs_2_ = f32[2048,256]{1,0:T(8,128)S(1)} custom-call(bf16[800,128]{1,0:T(8,128)(2,1)S(1)} %broadcast_add_fusion.refs_0_, f32[2048,256]{1,0:T(8,128)S(1)} %add_lists.7.refs_1_), custom_call_target="tpu_custom_call", output_to_operand_aliasing={{}: (1, {})} | custom-call | flops 100000000 | bytes 1024 | tf_op jit(solution)/shard_map/add_lists/pallas_call | solution.py:196
  32.5 3.8 %collective-permute-done.8.refs_0_ = bf16[1600,128]{1,0:T(8,128)(2,1)S(1)} collective-permute-done((bf16[1600,128]{1,0:T(8,128)(2,1)S(1)}, bf16[1600,128]{1,0:T(8,128)(2,1)S(1)}, u32[]{:S(2)}, u32[]{:S(2)}) %collective-permute-start.8) | collective-permute-done | bytes 409632 | tf_op jit(solution)/shard_map/ppermute | solution.py:270
  36.4 2.3 %add_lists.8.refs_1_ = f32[2048,256]{1,0:T(8,128)S(1)} custom-call(bf16[1600,128]{1,0:T(8,128)(2,1)S(1)} %collective-permute-done.8.refs_0_), custom_call_target="tpu_custom_call" | custom-call | flops 100000000 | bytes 1024 | tf_op jit(solution)/shard_map/add_lists/pallas_call | solution.py:196
  38.7 2.1 %collective-permute-done.7.refs_0_ = bf16[800,128]{1,0:T(8,128)(2,1)S(1)} collective-permute-done((bf16[800,128]{1,0:T(8,128)(2,1)S(1)}, bf16[800,128]{1,0:T(8,128)(2,1)S(1)}, u32[]{:S(2)}, u32[]{:S(2)}) %collective-permute-start.7) | collective-permute-done | bytes 204832 | tf_op jit(solution)/shard_map/ppermute | solution.py:270
  40.8 1.5 %add_lists.9.refs_1_ = f32[2048,256]{1,0:T(8,128)S(1)} custom-call(bf16[800,128]{1,0:T(8,128)(2,1)S(1)} %collective-permute-done.7.refs_0_, f32[2048,256]{1,0:T(8,128)S(1)} %add_lists.8.refs_1_), custom_call_target="tpu_custom_call", output_to_operand_aliasing={{}: (1, {})} | custom-call | flops 100000000 | bytes 1024 | tf_op jit(solution)/shard_map/add_lists/pallas_call | solution.py:196
  42.3 2.8 %collective-permute-done.6.refs_0_ = bf16[800,128]{1,0:T(8,128)(2,1)S(1)} collective-permute-done((bf16[800,128]{1,0:T(8,128)(2,1)S(1)}, bf16[800,128]{1,0:T(8,128)(2,1)S(1)}, u32[]{:S(2)}, u32[]{:S(2)}) %collective-permute-start.6) | collective-permute-done | bytes 204832 | tf_op jit(solution)/shard_map/ppermute | solution.py:270
  45.2 1.4 %add_lists.11.own_ref = bf16[2048,256]{1,0:T(8,128)(2,1)S(1)} custom-call(bf16[800,128]{1,0:T(8,128)(2,1)S(1)} %collective-permute-done.6.refs_0_, f32[2048,256]{1,0:T(8,128)S(1)} %add_lists.9.refs_1_, f32[2048,256]{1,0:T(8,128)S(1)} %add_lists.10.refs_2_), custom_call_target="tpu_custom_call" | custom-call | flops 100000000 | bytes 1024 | tf_op jit(solution)/shard_map/add_lists/pallas_call | solution.py:196
  46.5 0.8 %collective-permute-start.9 = (bf16[2048,256]{1,0:T(8,128)(2,1)S(1)}, bf16[2048,256]{1,0:T(8,128)(2,1)S(1)}, u32[]{:S(2)}, u32[]{:S(2)}) collective-permute-start(bf16[2048,256]{1,0:T(8,128)(2,1)S(1)} %add_lists.11.own_ref), channel_id=1, source_target_pairs={{0,1},{1,0},{2,3},{3,2},{4,5},{5,4},{6,7},{7,6},{8,9},{9,8},{10,11... | collective-permute-start | bytes 3145736 | tf_op jit(solution)/shard_map/ppermute | solution.py:270
  47.3 2.3 %collective-permute-done.9.other_ref = bf16[2048,256]{1,0:T(8,128)(2,1)S(1)} collective-permute-done((bf16[2048,256]{1,0:T(8,128)(2,1)S(1)}, bf16[2048,256]{1,0:T(8,128)(2,1)S(1)}, u32[]{:S(2)}, u32[]{:S(2)}) %collective-permute-start.9) | collective-permute-done | bytes 1048608 | tf_op jit(solution)/shard_map/ppermute | solution.py:270
  49.6 3.2 %update.1 = (f32[4096,128]{1,0:T(8,128)}, f32[32,128]{1,0:T(8,128)}) custom-call(bf16[2048,256]{1,0:T(8,128)(2,1)S(1)} %add_lists.11.own_ref, bf16[2048,256]{1,0:T(8,128)(2,1)S(1)} %collective-permute-done.9.other_ref, f32[4096,128]{1,0:T(8,128)S(1)} %copy-done, f32[32,128]{1,0:T(8,128)S(1)} %bitcast.29), custom_call_target="tpu_custom_call" | custom-call | tf_op jit(solution)/shard_map/update/pallas_call | solution.py:245
  (20 shorter events, 0.2 us)
Async XLA Ops:
  2.7 0.9 %copy-start.1 = (bf16[128,8,128]{2,1,0:T(8,128)(2,1)S(1)}, bf16[128,8,128]{2,1,0:T(8,128)(2,1)}, u32[]{:S(2)}) copy-start(bf16[128,8,128]{2,1,0:T(8,128)(2,1)} %param.6) | copy-start | bytes 786436
  5.2 1.7 %collective-permute-start = (bf16[1,400,128]{2,1,0:T(8,128)(2,1)S(1)}, bf16[1,400,128]{2,1,0:T(8,128)(2,1)S(1)}, u32[]{:S(2)}, u32[]{:S(2)}) collective-permute-start(bf16[1,400,128]{2,1,0:T(8,128)(2,1)S(1)} %get-tuple-element.9), channel_id=1, source_target_pairs={{0,1},{1,0},{2,3},{3,2},{4,5},{5,4},{6,7},{7,6},{8,9},{9,8},{10,11... | collective-permute-start | bytes 307208 | tf_op jit(solution)/shard_map/ppermute | solution.py:270
  8.3 2.7 %collective-permute-start.1 = (bf16[3,400,128]{2,1,0:T(8,128)(2,1)S(1)}, bf16[3,400,128]{2,1,0:T(8,128)(2,1)S(1)}, u32[]{:S(2)}, u32[]{:S(2)}) collective-permute-start(bf16[3,400,128]{2,1,0:T(8,128)(2,1)S(1)} %pack_next.5), channel_id=1, source_target_pairs={{0,1},{1,0},{2,3},{3,2},{4,5},{5,4},{6,7},{7,6},{8,9},{9,8},{10,11... | collective-permute-start | bytes 921608 | tf_op jit(solution)/shard_map/ppermute | solution.py:270
  8.7 19.0 %collective-permute-start.3 = (bf16[800,128]{1,0:T(8,128)(2,1)S(1)}, bf16[800,128]{1,0:T(8,128)(2,1)S(1)}, u32[]{:S(2)}, u32[]{:S(2)}) collective-permute-start(bf16[800,128]{1,0:T(8,128)(2,1)S(1)} %pad_maximum_fusion.refs_0_), channel_id=1, source_target_pairs={{0,24},{1,29},{2,26},{3,31},{4,28},{5,25},{6,30},{7,27},{8,16},{9,... | collective-permute-start | bytes 614408 | tf_op jit(solution)/shard_map/ppermute | solution.py:270
  11.1 8.3 %collective-permute-start.4 = (bf16[800,128]{1,0:T(8,128)(2,1)S(1)}, bf16[800,128]{1,0:T(8,128)(2,1)S(1)}, u32[]{:S(2)}, u32[]{:S(2)}) collective-permute-start(bf16[800,128]{1,0:T(8,128)(2,1)S(1)} %pad_maximum_fusion.2), channel_id=1, source_target_pairs={{0,0},{1,5},{2,2},{3,7},{4,4},{5,1},{6,6},{7,3},{8,8},{9,13},{10,1... | collective-permute-start | bytes 614408 | tf_op jit(solution)/shard_map/ppermute | solution.py:270
  13.6 11.5 %collective-permute-start.5 = (bf16[800,128]{1,0:T(8,128)(2,1)S(1)}, bf16[800,128]{1,0:T(8,128)(2,1)S(1)}, u32[]{:S(2)}, u32[]{:S(2)}) collective-permute-start(bf16[800,128]{1,0:T(8,128)(2,1)S(1)} %pad_maximum_fusion.3), channel_id=1, source_target_pairs={{0,8},{1,13},{2,10},{3,15},{4,12},{5,9},{6,14},{7,11},{8,0},{9,5},... | collective-permute-start | bytes 614408 | tf_op jit(solution)/shard_map/ppermute | solution.py:270
  14.9 15.8 %collective-permute-start.2 = (bf16[800,128]{1,0:T(8,128)(2,1)S(1)}, bf16[800,128]{1,0:T(8,128)(2,1)S(1)}, u32[]{:S(2)}, u32[]{:S(2)}) collective-permute-start(bf16[800,128]{1,0:T(8,128)(2,1)S(1)} %pad_maximum_fusion.1), channel_id=1, source_target_pairs={{0,16},{1,21},{2,18},{3,23},{4,20},{5,17},{6,22},{7,19},{8,24},{9,... | collective-permute-start | bytes 614408 | tf_op jit(solution)/shard_map/ppermute | solution.py:270
  25.2 11.2 %collective-permute-start.8 = (bf16[1600,128]{1,0:T(8,128)(2,1)S(1)}, bf16[1600,128]{1,0:T(8,128)(2,1)S(1)}, u32[]{:S(2)}, u32[]{:S(2)}) collective-permute-start(bf16[1600,128]{1,0:T(8,128)(2,1)S(1)} %constant_dynamic-update-slice_fusion.refs_0_), channel_id=1, source_target_pairs={{0,2},{1,3},{2,0},{3,1},{4,6},{5,7},{6,4},{7,5},{8,10},{9,11},{10,... | collective-permute-start | bytes 1228808 | tf_op jit(solution)/shard_map/ppermute | solution.py:270
  29.3 11.4 %collective-permute-start.7 = (bf16[800,128]{1,0:T(8,128)(2,1)S(1)}, bf16[800,128]{1,0:T(8,128)(2,1)S(1)}, u32[]{:S(2)}, u32[]{:S(2)}) collective-permute-start(bf16[800,128]{1,0:T(8,128)(2,1)S(1)} %broadcast_add_fusion.1.refs_0_), channel_id=1, source_target_pairs={{0,2},{1,3},{2,0},{3,1},{4,6},{5,7},{6,4},{7,5},{8,10},{9,11},{10,... | collective-permute-start | bytes 614408 | tf_op jit(solution)/shard_map/ppermute | solution.py:270
  30.7 14.5 %collective-permute-start.6 = (bf16[800,128]{1,0:T(8,128)(2,1)S(1)}, bf16[800,128]{1,0:T(8,128)(2,1)S(1)}, u32[]{:S(2)}, u32[]{:S(2)}) collective-permute-start(bf16[800,128]{1,0:T(8,128)(2,1)S(1)} %broadcast_add_fusion.refs_0_), channel_id=1, source_target_pairs={{0,2},{1,3},{2,0},{3,1},{4,6},{5,7},{6,4},{7,5},{8,10},{9,11},{10,... | collective-permute-start | bytes 614408 | tf_op jit(solution)/shard_map/ppermute | solution.py:270
  42.3 7.3 %copy-start = (f32[4096,128]{1,0:T(8,128)S(1)}, f32[4096,128]{1,0:T(8,128)}, u32[]{:S(2)}) copy-start(f32[4096,128]{1,0:T(8,128)} %weight_ref.1) | copy-start | bytes 6291460
  42.3 7.3 %copy-start.2 = (f32[4096]{0:T(1024)S(1)}, f32[4096]{0:T(1024)}, u32[]{:S(2)}) copy-start(f32[4096]{0:T(1024)} %param.11) | copy-start | bytes 49156
  46.5 3.1 %collective-permute-start.9 = (bf16[2048,256]{1,0:T(8,128)(2,1)S(1)}, bf16[2048,256]{1,0:T(8,128)(2,1)S(1)}, u32[]{:S(2)}, u32[]{:S(2)}) collective-permute-start(bf16[2048,256]{1,0:T(8,128)(2,1)S(1)} %add_lists.11.own_ref), channel_id=1, source_target_pairs={{0,1},{1,0},{2,3},{3,2},{4,5},{5,4},{6,7},{7,6},{8,9},{9,8},{10,11... | collective-permute-start | bytes 3145736 | tf_op jit(solution)/shard_map/ppermute | solution.py:270

commit v3 on v2

--- a/solution.py
+++ b/solution.py
@@ -81,16 +81,15 @@
             high + low + [jnp.zeros((PAD - 2 * chunks, LANES), f32)], axis=0).astype(bf16)
 
 
-def first_kernel(groups, capacity, wanted, facts_ref, bags_ref, out_ref, slot_ref, ext_ref):
+def rank_kernel(groups, capacity, code_ref, owner_ref, slot_ref):
     blocks = slot_ref.shape[0]
     wide = groups * blocks
     upper = (iota((LANES, LANES), 0) <= iota((LANES, LANES), 1)).astype(bf16)
     at, to = iota((wide, wide), 0), iota((wide, wide), 1)
     earlier = ((at // blocks == to // blocks) & (to < at)).astype(bf16)
-    lane = iota((LANES, LANES), 1)
-    repeat = ((iota((LANES, LANES // 2), 0) >> 1) == iota((LANES, LANES // 2), 1)).astype(bf16)
-    group = facts_ref[0:blocks, :]
-    hits = [(group == float(g)).astype(f32) for g in range(groups)]
+    offset = owner_ref[...] ^ (code_ref[0] >> 1)
+    group = jnp.where(offset < 2, offset, offset ^ (code_ref[0] & 1))
+    hits = [(group == g).astype(f32) for g in range(groups)]
     stacked = jnp.concatenate(hits, axis=0).astype(bf16)
     inside = jnp.dot(stacked, upper, preferred_element_type=f32)
     totals = jnp.dot(stacked, jnp.ones((LANES, LANES), bf16), preferred_element_type=f32)
@@ -101,8 +100,14 @@
         slot = slot + hits[g] * (rank[g * blocks:(g + 1) * blocks] + float(g * capacity))
     slot_ref[...] = slot
 
+
+def first_kernel(groups, capacity, wanted, slot_ref, row_ref, w_ref, bags_ref, out_ref, ext_ref):
+    blocks = slot_ref.shape[0]
+    lane = iota((LANES, LANES), 1)
+    repeat = ((iota((LANES, LANES // 2), 0) >> 1) == iota((LANES, LANES // 2), 1)).astype(bf16)
     columns = jnp.concatenate(
-        [facts_ref[blocks:4 * blocks, :], jnp.zeros((LANES - 3 * blocks, LANES), f32)], axis=0).T
+        [(row_ref[...] >> 8).astype(f32), (row_ref[...] & 255).astype(f32), w_ref[...],
+         jnp.zeros((LANES - 3 * blocks, LANES), f32)], axis=0).T
     for r in range(blocks):
         bag = jnp.dot(repeat, bags_ref[r * LANES // 2:(r + 1) * LANES // 2, :], preferred_element_type=f32)
         here = slice(r * LANES, (r + 1) * LANES)
@@ -110,7 +115,7 @@
         high, low = columns[:, r:r + 1], columns[:, blocks + r:blocks + r + 1]
         ext_ref[here, LANES:2 * LANES] = jnp.where(
             lane == 0, high, jnp.where(lane == 1, low, 0.0)).astype(bf16)
-    pack_groups(groups, capacity, wanted, slot, ext_ref, out_ref)
+    pack_groups(groups, capacity, wanted, slot_ref[...], ext_ref, out_ref)
 
 
 def next_kernel(groups, capacity, wanted, slot_ref, ext_ref, *refs):
@@ -122,18 +127,29 @@
     return jax.ShapeDtypeStruct((len(wanted), capacity + PAD, LANES), bf16)
 
 
-def pack_first(facts, bags, groups, capacity, wanted):
-    blocks = facts.shape[0] // 4
+def find_slots(code, owner, groups, capacity):
+    vmem = pl.BlockSpec(memory_space=pltpu.VMEM)
+    return pl.pallas_call(
+        functools.partial(rank_kernel, groups, capacity),
+        out_shape=jax.ShapeDtypeStruct(owner.shape, f32),
+        in_specs=[pl.BlockSpec(memory_space=pltpu.SMEM), vmem],
+        out_specs=vmem,
+        compiler_params=pltpu.CompilerParams(vmem_limit_bytes=VMEM_LIMIT),
+        cost_estimate=pl.CostEstimate(flops=20_000_000_000, bytes_accessed=1024, transcendentals=0),
+        name="find_slots",
+    )(code, owner)
+
+
+def pack_first(slot, local_row, lookup_weight, bags, groups, capacity, wanted):
     vmem = pl.BlockSpec(memory_space=pltpu.VMEM)
     return pl.pallas_call(
         functools.partial(first_kernel, groups, capacity, wanted),
-        out_shape=[listed(wanted, capacity), jax.ShapeDtypeStruct((blocks, LANES), f32),
-                   jax.ShapeDtypeStruct((blocks * LANES, 2 * LANES), bf16)],
-        in_specs=[vmem, vmem],
-        out_specs=[vmem, vmem, vmem],
+        out_shape=[listed(wanted, capacity), jax.ShapeDtypeStruct((slot.size, 2 * LANES), bf16)],
+        in_specs=[vmem] * 4,
+        out_specs=[vmem, vmem],
         compiler_params=pltpu.CompilerParams(vmem_limit_bytes=VMEM_LIMIT),
         name="pack_first",
-    )(facts, bags)
+    )(slot, local_row, lookup_weight, bags)
 
 
 def pack_next(slot, ext, groups, capacity, wanted, after=()):
@@ -271,38 +287,39 @@
 
     to_core = functools.partial(permute, target=lambda s, r: s * reps + (r ^ 1))
     to_copy = functools.partial(permute, target=lambda s, r: s * reps + (r ^ 2))
-    key = lax.axis_index("shard").astype(i32) ^ (lax.axis_index("rep").astype(i32) & 1)
-    blocks = lookups // LANES
-    local_row = local_row.reshape(blocks, LANES)
-    facts = jnp.concatenate(
-        [(owner.reshape(blocks, LANES) ^ key).astype(f32), (local_row >> 8).astype(f32),
-         (local_row & 255).astype(f32), lookup_weight.reshape(blocks, LANES)], axis=0)
-
-    near = list(range(shards // 4))
-    far = list(range(shards // 4, shards // 2))
-    phases = [far[1:], near + far[:1]]
-    order = [near, far[1:], far[:1]]
-    before, arrived = (), {}
-    for n, qs in enumerate(phases):
-        give, hold = [2 * q + 1 for q in qs], [2 * q for q in qs]
-        if n == 0:
-            given, slot, ext = pack_first(facts, grad_pooled.reshape(-1, width), shards, capacity, give)
-        else:
-            given = pack_next(slot, ext, shards, capacity, give, before)
-        got = to_core(given)
-        keep = pack_next(slot, ext, shards, capacity, hold, before)
-        before = [jnp.concatenate([keep[n], got[n]], axis=0) for n in range(len(qs))]
-        for q, payload in zip(qs, before):
-            arrived[q] = permute(payload, lambda s, r: (s ^ (2 * q + (r & 1))) * reps + r)
+    code = lax.axis_index("shard").astype(i32) * 2 + (lax.axis_index("rep").astype(i32) & 1)
+    dense = (lookups // LANES, LANES)
+    slot = find_slots(code.reshape(1), owner.reshape(dense), shards, capacity)
+
+    def swapped(qs, pack_given, after):
+        got = to_core(pack_given)
+        keep = pack_next(slot, ext, shards, capacity, [2 * q for q in qs], after)
+        return [jnp.concatenate([keep[n], got[n]], axis=0) for n in range(len(qs))]
+
+    def send(q, payload):
+        return permute(payload, lambda s, r: (s ^ (2 * q + (r & 1))) * reps + r)
+
+    far = shards // 2 - 1
+    near = [1, far - 1]
+    given, ext = pack_first(slot, local_row.reshape(dense), lookup_weight.reshape(dense),
+                            grad_pooled.reshape(-1, width), shards, capacity, [2 * far + 1])
+    first = swapped([far], given, ())
+    lists = {far: send(far, first[0])}
+    given = pack_next(slot, ext, shards, capacity, [2 * q + 1 for q in near], first)
+    got = to_core(given)
+    kept = pack_next(slot, ext, shards, capacity, [2 * q for q in near], first)
+    beside = pack_next(slot, ext, shards, capacity, [0, 1], [got])
+    lists[0] = jnp.concatenate([beside[0], permute(beside[1], lambda s, r: (s ^ 1) * reps + r)], axis=0)
+    for n, q in enumerate(near):
+        lists[q] = send(q, jnp.concatenate([kept[n], got[n]], axis=0))
 
     own = copy = None
-    for n, qs in enumerate(order):
-        here = jnp.concatenate([arrived[q] for q in qs], axis=0)
-        if own is not None:
-            here = tied(here, own)
+    order = (0, far, 1, far - 1)
+    for q in order:
+        here = lists[q] if own is None else tied(lists[q], own)
         there = to_copy(here)
         own = add_lists([here], own, None, half, capacity)
-        copy = add_lists([there], copy, own if n == 2 else None, half, capacity)
+        copy = add_lists([there], copy, own if q == order[-1] else None, half, capacity)
     return update(copy, to_core(copy), weight, accum)
 
 

time: 53.3 us -> 49.3 us (0.925)
  the two profiles are of different devices: /device:TPU:29 before, /device:TPU:19 now
where the time goes in v3:
time: 49.3 us; the launch traced here: 49.1 us
  Pallas kernels  20.6 us (42%)
  waiting for transfers between devices  14.1 us (29%)
  starting transfers between devices  11.9 us (24%)
  local copies, waits for them, and re-layouts  1.41 us (3%)
  between operations  0.99 us (2%)
    ppermute x11, waiting for transfers between devices, permute(): return lax.ppermute(value, axes, pairs)  14.1 us
    pallas_call x8, Pallas kernels, add_lists(): pl.pallas_call(functools.partial(add_kernel, capacity, n, before is None,...  11.9 us
    ppermute x11, starting transfers between devices, permute(): return lax.ppermute(value, axes, pairs)  11.9 us
    pallas_call x4, Pallas kernels, pack_next(): pl.pallas_call(functools.partial(next_kernel, groups, capacity, wanted),...  3.72 us
    pallas_call x1, Pallas kernels, update(): pl.pallas_call(update_kernel, out_shape=[jax.ShapeDtypeStruct(weight.shap...  3.16 us
    pallas_call x1, Pallas kernels, pack_first(): pl.pallas_call(functools.partial(first_kernel, groups, capacity, wanted),...  1.52 us
    unnamed x12, local copies, waits for them, and re-layouts  1.36 us
  transfers between devices with their start and end apart: 11, of which 6 were waited for; matrix products, arithmetic and copies ran while one was open for 0% of the time, Pallas kernels for 25%

profile of v3, /device:TPU:19, one launch (start us, length us, event | category | flops | bytes accessed | tf_op | source)
XLA Modules:
  0.0 49.1 jit_solution(14568787012324278501)
XLA Ops:
  0.6 0.7 %copy-done.5 = s32[2048,1]{0,1:T(1,128)S(1)} copy-done((s32[2048,1]{0,1:T(1,128)S(1)}, s32[2048,1]{0,1:T(1,128)}, u32[]{:S(2)}) %copy-start.5) | copy-done | bytes 8216
  1.3 0.3 find_slots.1.slot_ref
  1.6 0.6 %copy-done.1 = bf16[128,8,128]{2,1,0:T(8,128)(2,1)S(1)} copy-done((bf16[128,8,128]{2,1,0:T(8,128)(2,1)S(1)}, bf16[128,8,128]{2,1,0:T(8,128)(2,1)}, u32[]{:S(2)}) %copy-start.1) | copy-done | bytes 262168
  2.3 1.5 %pack_first.1 = (bf16[1,400,128]{2,1,0:T(8,128)(2,1)S(1)}, bf16[2048,256]{1,0:T(8,128)(2,1)S(1)}) custom-call(f32[16,128]{1,0:T(8,128)S(1)} %find_slots.1.slot_ref, s32[16,128]{1,0:T(8,128)S(1)} %bitcast.30, f32[16,128]{1,0:T(8,128)S(1)} %bitcast.31, bf16[1024,128]{1,0:T(8,128)(2,1)S(1)} %bitcast.28), custom_call_target="tpu_custom_call" | custom-call | tf_op jit(solution)/shard_map/pack_first/pallas_call | solution.py:145
  3.8 0.7 %collective-permute-start = (bf16[1,400,128]{2,1,0:T(8,128)(2,1)S(1)}, bf16[1,400,128]{2,1,0:T(8,128)(2,1)S(1)}, u32[]{:S(2)}, u32[]{:S(2)}) collective-permute-start(bf16[1,400,128]{2,1,0:T(8,128)(2,1)S(1)} %get-tuple-element.7), channel_id=1, source_target_pairs={{0,1},{1,0},{2,3},{3,2},{4,5},{5,4},{6,7},{7,6},{8,9},{9,8},{10,11... | collective-permute-start | bytes 307208 | tf_op jit(solution)/shard_map/ppermute | solution.py:286
  4.5 0.6 %pack_next.4 = bf16[1,400,128]{2,1,0:T(8,128)(2,1)S(1)} custom-call(f32[16,128]{1,0:T(8,128)S(1)} %find_slots.1.slot_ref, bf16[2048,256]{1,0:T(8,128)(2,1)S(1)} %get-tuple-element.6.ext_ref), custom_call_target="tpu_custom_call" | custom-call | flops 1024 | bytes 1024 | tf_op jit(solution)/shard_map/pack_next/pallas_call | solution.py:157
  5.2 0.3 collective-permute-done
  5.5 1.0 %pack_next.6 = bf16[2,400,128]{2,1,0:T(8,128)(2,1)S(1)} custom-call(f32[16,128]{1,0:T(8,128)S(1)} %find_slots.1.slot_ref, bf16[2048,256]{1,0:T(8,128)(2,1)S(1)} %get-tuple-element.6.ext_ref, bf16[800,128]{1,0:T(8,128)(2,1)S(1)} %pad_maximum_fusion.refs_0_), custom_call_target="tpu_custom_call" | custom-call | flops 1024 | bytes 1024 | tf_op jit(solution)/shard_map/pack_next/pallas_call | solution.py:157
  6.5 1.0 %pack_next.5 = bf16[2,400,128]{2,1,0:T(8,128)(2,1)S(1)} custom-call(f32[16,128]{1,0:T(8,128)S(1)} %find_slots.1.slot_ref, bf16[2048,256]{1,0:T(8,128)(2,1)S(1)} %get-tuple-element.6.ext_ref, bf16[800,128]{1,0:T(8,128)(2,1)S(1)} %pad_maximum_fusion.refs_0_), custom_call_target="tpu_custom_call" | custom-call | flops 1024 | bytes 1024 | tf_op jit(solution)/shard_map/pack_next/pallas_call | solution.py:157
  7.7 0.7 %collective-permute-start.1 = (bf16[2,400,128]{2,1,0:T(8,128)(2,1)S(1)}, bf16[2,400,128]{2,1,0:T(8,128)(2,1)S(1)}, u32[]{:S(2)}, u32[]{:S(2)}) collective-permute-start(bf16[2,400,128]{2,1,0:T(8,128)(2,1)S(1)} %pack_next.6), channel_id=1, source_target_pairs={{0,1},{1,0},{2,3},{3,2},{4,5},{5,4},{6,7},{7,6},{8,9},{9,8},{10,11... | collective-permute-start | bytes 614408 | tf_op jit(solution)/shard_map/ppermute | solution.py:286
  8.4 1.1 %collective-permute-done.1.refs_0_ = bf16[2,400,128]{2,1,0:T(8,128)(2,1)S(1)} collective-permute-done((bf16[2,400,128]{2,1,0:T(8,128)(2,1)S(1)}, bf16[2,400,128]{2,1,0:T(8,128)(2,1)S(1)}, u32[]{:S(2)}, u32[]{:S(2)}) %collective-permute-start.1) | collective-permute-done | bytes 204832 | tf_op jit(solution)/shard_map/ppermute | solution.py:286
  9.5 1.0 %pack_next.7 = bf16[2,400,128]{2,1,0:T(8,128)(2,1)S(1)} custom-call(f32[16,128]{1,0:T(8,128)S(1)} %find_slots.1.slot_ref, bf16[2048,256]{1,0:T(8,128)(2,1)S(1)} %get-tuple-element.6.ext_ref, bf16[2,400,128]{2,1,0:T(8,128)(2,1)S(1)} %collective-permute-done.1.refs_0_), custom_call_target="tpu_custom_call" | custom-call | flops 1024 | bytes 1024 | tf_op jit(solution)/shard_map/pack_next/pallas_call | solution.py:157
  10.6 1.0 %collective-permute-start.5 = (bf16[400,128]{1,0:T(8,128)(2,1)S(1)}, bf16[400,128]{1,0:T(8,128)(2,1)S(1)}, u32[]{:S(2)}, u32[]{:S(2)}) collective-permute-start(bf16[400,128]{1,0:T(8,128)(2,1)S(1)} %get-tuple-element.11), channel_id=1, source_target_pairs={{0,4},{1,5},{2,6},{3,7},{4,0},{5,1},{6,2},{7,3},{8,12},{9,13},{10,... | collective-permute-start | bytes 307208 | tf_op jit(solution)/shard_map/ppermute | solution.py:286
  11.6 3.5 %collective-permute-start.2 = (bf16[800,128]{1,0:T(8,128)(2,1)S(1)}, bf16[800,128]{1,0:T(8,128)(2,1)S(1)}, u32[]{:S(2)}, u32[]{:S(2)}) collective-permute-start(bf16[800,128]{1,0:T(8,128)(2,1)S(1)} %pad_maximum_fusion.1), channel_id=1, source_target_pairs={{0,16},{1,21},{2,18},{3,23},{4,20},{5,17},{6,22},{7,19},{8,24},{9,... | collective-permute-start | bytes 614408 | tf_op jit(solution)/shard_map/ppermute | solution.py:286
  15.3 1.3 %collective-permute-start.9 = (bf16[800,128]{1,0:T(8,128)(2,1)S(1)}, bf16[800,128]{1,0:T(8,128)(2,1)S(1)}, u32[]{:S(2)}, u32[]{:S(2)}) collective-permute-start(bf16[800,128]{1,0:T(8,128)(2,1)S(1)} %pad_maximum_fusion.3.refs_0_), channel_id=1, source_target_pairs={{0,2},{1,3},{2,0},{3,1},{4,6},{5,7},{6,4},{7,5},{8,10},{9,11},{10,... | collective-permute-start | bytes 614408 | tf_op jit(solution)/shard_map/ppermute | solution.py:286
  16.6 1.3 %add_lists.8.refs_1_ = f32[2048,256]{1,0:T(8,128)S(1)} custom-call(bf16[800,128]{1,0:T(8,128)(2,1)S(1)} %pad_maximum_fusion.3.refs_0_), custom_call_target="tpu_custom_call" | custom-call | flops 100000000 | bytes 1024 | tf_op jit(solution)/shard_map/add_lists/pallas_call | solution.py:212
  17.9 6.2 %collective-permute-done.4 = bf16[800,128]{1,0:T(8,128)(2,1)S(1)} collective-permute-done((bf16[800,128]{1,0:T(8,128)(2,1)S(1)}, bf16[800,128]{1,0:T(8,128)(2,1)S(1)}, u32[]{:S(2)}, u32[]{:S(2)}) %collective-permute-start.4) | collective-permute-done | bytes 204832 | tf_op jit(solution)/shard_map/ppermute | solution.py:286
  24.2 1.6 %add_lists.9.refs_1_ = f32[2048,256]{1,0:T(8,128)S(1)} custom-call(bf16[800,128]{1,0:T(8,128)(2,1)S(1)} %broadcast_add_fusion.2.refs_0_, f32[2048,256]{1,0:T(8,128)S(1)} %add_lists.8.refs_1_), custom_call_target="tpu_custom_call", output_to_operand_aliasing={{}: (1, {})} | custom-call | flops 100000000 | bytes 1024 | tf_op jit(solution)/shard_map/add_lists/pallas_call | solution.py:212
  25.7 1.3 %collective-permute-start.8 = (bf16[800,128]{1,0:T(8,128)(2,1)S(1)}, bf16[800,128]{1,0:T(8,128)(2,1)S(1)}, u32[]{:S(2)}, u32[]{:S(2)}) collective-permute-start(bf16[800,128]{1,0:T(8,128)(2,1)S(1)} %broadcast_add_fusion.2.refs_0_), channel_id=1, source_target_pairs={{0,2},{1,3},{2,0},{3,1},{4,6},{5,7},{6,4},{7,5},{8,10},{9,11},{10,... | collective-permute-start | bytes 614408 | tf_op jit(solution)/shard_map/ppermute | solution.py:286
  27.1 1.6 %add_lists.10.refs_1_ = f32[2048,256]{1,0:T(8,128)S(1)} custom-call(bf16[800,128]{1,0:T(8,128)(2,1)S(1)} %broadcast_add_fusion.1.refs_0_, f32[2048,256]{1,0:T(8,128)S(1)} %add_lists.9.refs_1_), custom_call_target="tpu_custom_call", output_to_operand_aliasing={{}: (1, {})} | custom-call | flops 100000000 | bytes 1024 | tf_op jit(solution)/shard_map/add_lists/pallas_call | solution.py:212
  28.6 0.3 collective-permute-start.7
  28.9 1.3 %collective-permute-start.6 = (bf16[800,128]{1,0:T(8,128)(2,1)S(1)}, bf16[800,128]{1,0:T(8,128)(2,1)S(1)}, u32[]{:S(2)}, u32[]{:S(2)}) collective-permute-start(bf16[800,128]{1,0:T(8,128)(2,1)S(1)} %broadcast_add_fusion.refs_0_), channel_id=1, source_target_pairs={{0,2},{1,3},{2,0},{3,1},{4,6},{5,7},{6,4},{7,5},{8,10},{9,11},{10,... | collective-permute-start | bytes 614408 | tf_op jit(solution)/shard_map/ppermute | solution.py:286
  30.2 1.5 %add_lists.14.refs_2_ = f32[2048,256]{1,0:T(8,128)S(1)} custom-call(bf16[800,128]{1,0:T(8,128)(2,1)S(1)} %broadcast_add_fusion.refs_0_, f32[2048,256]{1,0:T(8,128)S(1)} %add_lists.10.refs_1_), custom_call_target="tpu_custom_call", output_to_operand_aliasing={{}: (1, {})} | custom-call | flops 100000000 | bytes 1024 | tf_op jit(solution)/shard_map/add_lists/pallas_call | solution.py:212
  31.8 1.3 %add_lists.11.refs_1_ = f32[2048,256]{1,0:T(8,128)S(1)} custom-call(bf16[800,128]{1,0:T(8,128)(2,1)S(1)} %collective-permute-done.9.refs_0_), custom_call_target="tpu_custom_call" | custom-call | flops 100000000 | bytes 1024 | tf_op jit(solution)/shard_map/add_lists/pallas_call | solution.py:212
  33.1 1.5 %add_lists.12.refs_1_ = f32[2048,256]{1,0:T(8,128)S(1)} custom-call(bf16[800,128]{1,0:T(8,128)(2,1)S(1)} %collective-permute-done.8.refs_0_, f32[2048,256]{1,0:T(8,128)S(1)} %add_lists.11.refs_1_), custom_call_target="tpu_custom_call", output_to_operand_aliasing={{}: (1, {})} | custom-call | flops 100000000 | bytes 1024 | tf_op jit(solution)/shard_map/add_lists/pallas_call | solution.py:212
  34.7 1.6 %collective-permute-done.7.refs_0_ = bf16[800,128]{1,0:T(8,128)(2,1)S(1)} collective-permute-done((bf16[800,128]{1,0:T(8,128)(2,1)S(1)}, bf16[800,128]{1,0:T(8,128)(2,1)S(1)}, u32[]{:S(2)}, u32[]{:S(2)}) %collective-permute-start.7) | collective-permute-done | bytes 204832 | tf_op jit(solution)/shard_map/ppermute | solution.py:286
  36.3 1.7 %add_lists.13.refs_1_ = f32[2048,256]{1,0:T(8,128)S(1)} custom-call(bf16[800,128]{1,0:T(8,128)(2,1)S(1)} %collective-permute-done.7.refs_0_, f32[2048,256]{1,0:T(8,128)S(1)} %add_lists.12.refs_1_), custom_call_target="tpu_custom_call", output_to_operand_aliasing={{}: (1, {})} | custom-call | flops 100000000 | bytes 1024 | tf_op jit(solution)/shard_map/add_lists/pallas_call | solution.py:212
  38.0 2.6 %collective-permute-done.6.refs_0_ = bf16[800,128]{1,0:T(8,128)(2,1)S(1)} collective-permute-done((bf16[800,128]{1,0:T(8,128)(2,1)S(1)}, bf16[800,128]{1,0:T(8,128)(2,1)S(1)}, u32[]{:S(2)}, u32[]{:S(2)}) %collective-permute-start.6) | collective-permute-done | bytes 204832 | tf_op jit(solution)/shard_map/ppermute | solution.py:286
  40.6 1.4 %add_lists.15.own_ref = bf16[2048,256]{1,0:T(8,128)(2,1)S(1)} custom-call(bf16[800,128]{1,0:T(8,128)(2,1)S(1)} %collective-permute-done.6.refs_0_, f32[2048,256]{1,0:T(8,128)S(1)} %add_lists.13.refs_1_, f32[2048,256]{1,0:T(8,128)S(1)} %add_lists.14.refs_2_), custom_call_target="tpu_custom_call" | custom-call | flops 100000000 | bytes 1024 | tf_op jit(solution)/shard_map/add_lists/pallas_call | solution.py:212
  42.0 1.5 %collective-permute-start.10 = (bf16[2048,256]{1,0:T(8,128)(2,1)S(1)}, bf16[2048,256]{1,0:T(8,128)(2,1)S(1)}, u32[]{:S(2)}, u32[]{:S(2)}) collective-permute-start(bf16[2048,256]{1,0:T(8,128)(2,1)S(1)} %add_lists.15.own_ref), channel_id=1, source_target_pairs={{0,1},{1,0},{2,3},{3,2},{4,5},{5,4},{6,7},{7,6},{8,9},{9,8},{10,11... | collective-permute-start | bytes 3145736 | tf_op jit(solution)/shard_map/ppermute | solution.py:286
  43.5 2.3 %collective-permute-done.10.other_ref = bf16[2048,256]{1,0:T(8,128)(2,1)S(1)} collective-permute-done((bf16[2048,256]{1,0:T(8,128)(2,1)S(1)}, bf16[2048,256]{1,0:T(8,128)(2,1)S(1)}, u32[]{:S(2)}, u32[]{:S(2)}) %collective-permute-start.10) | collective-permute-done | bytes 1048608 | tf_op jit(solution)/shard_map/ppermute | solution.py:286
  45.8 3.2 %update.1 = (f32[4096,128]{1,0:T(8,128)}, f32[32,128]{1,0:T(8,128)}) custom-call(bf16[2048,256]{1,0:T(8,128)(2,1)S(1)} %add_lists.15.own_ref, bf16[2048,256]{1,0:T(8,128)(2,1)S(1)} %collective-permute-done.10.other_ref, f32[4096,128]{1,0:T(8,128)S(1)} %copy-done, f32[32,128]{1,0:T(8,128)S(1)} %bitcast.29), custom_call_target="tpu_custom_call" | custom-call | tf_op jit(solution)/shard_map/update/pallas_call | solution.py:261
  (30 shorter events, 0.5 us)
Async XLA Ops:
  0.6 0.7 %copy-start.5 = (s32[2048,1]{0,1:T(1,128)S(1)}, s32[2048,1]{0,1:T(1,128)}, u32[]{:S(2)}) copy-start(s32[2048,1]{0,1:T(1,128)} %param.8) | copy-start | bytes 24580
  1.3 0.9 %copy-start.1 = (bf16[128,8,128]{2,1,0:T(8,128)(2,1)S(1)}, bf16[128,8,128]{2,1,0:T(8,128)(2,1)}, u32[]{:S(2)}) copy-start(bf16[128,8,128]{2,1,0:T(8,128)(2,1)} %param.6) | copy-start | bytes 786436
  1.3 1.0 %copy-start.3 = (s32[2048]{0:T(1024)S(1)}, s32[2048]{0:T(1024)}, u32[]{:S(2)}) copy-start(s32[2048]{0:T(1024)} %param.9) | copy-start | bytes 24580
  1.3 1.0 %copy-start.4 = (f32[2048]{0:T(1024)S(1)}, f32[2048]{0:T(1024)}, u32[]{:S(2)}) copy-start(f32[2048]{0:T(1024)} %param.7) | copy-start | bytes 24580
  3.8 1.7 %collective-permute-start = (bf16[1,400,128]{2,1,0:T(8,128)(2,1)S(1)}, bf16[1,400,128]{2,1,0:T(8,128)(2,1)S(1)}, u32[]{:S(2)}, u32[]{:S(2)}) collective-permute-start(bf16[1,400,128]{2,1,0:T(8,128)(2,1)S(1)} %get-tuple-element.7), channel_id=1, source_target_pairs={{0,1},{1,0},{2,3},{3,2},{4,5},{5,4},{6,7},{7,6},{8,9},{9,8},{10,11... | collective-permute-start | bytes 307208 | tf_op jit(solution)/shard_map/ppermute | solution.py:286
  7.6 16.6 %collective-permute-start.4 = (bf16[800,128]{1,0:T(8,128)(2,1)S(1)}, bf16[800,128]{1,0:T(8,128)(2,1)S(1)}, u32[]{:S(2)}, u32[]{:S(2)}) collective-permute-start(bf16[800,128]{1,0:T(8,128)(2,1)S(1)} %pad_maximum_fusion.refs_0_), channel_id=1, source_target_pairs={{0,24},{1,29},{2,26},{3,31},{4,28},{5,25},{6,30},{7,27},{8,16},{9,... | collective-permute-start | bytes 614408 | tf_op jit(solution)/shard_map/ppermute | solution.py:286
  7.7 1.8 %collective-permute-start.1 = (bf16[2,400,128]{2,1,0:T(8,128)(2,1)S(1)}, bf16[2,400,128]{2,1,0:T(8,128)(2,1)S(1)}, u32[]{:S(2)}, u32[]{:S(2)}) collective-permute-start(bf16[2,400,128]{2,1,0:T(8,128)(2,1)S(1)} %pack_next.6), channel_id=1, source_target_pairs={{0,1},{1,0},{2,3},{3,2},{4,5},{5,4},{6,7},{7,6},{8,9},{9,8},{10,11... | collective-permute-start | bytes 614408 | tf_op jit(solution)/shard_map/ppermute | solution.py:286
  10.6 4.7 %collective-permute-start.5 = (bf16[400,128]{1,0:T(8,128)(2,1)S(1)}, bf16[400,128]{1,0:T(8,128)(2,1)S(1)}, u32[]{:S(2)}, u32[]{:S(2)}) collective-permute-start(bf16[400,128]{1,0:T(8,128)(2,1)S(1)} %get-tuple-element.11), channel_id=1, source_target_pairs={{0,4},{1,5},{2,6},{3,7},{4,0},{5,1},{6,2},{7,3},{8,12},{9,13},{10,... | collective-permute-start | bytes 307208 | tf_op jit(solution)/shard_map/ppermute | solution.py:286
  11.6 17.3 %collective-permute-start.2 = (bf16[800,128]{1,0:T(8,128)(2,1)S(1)}, bf16[800,128]{1,0:T(8,128)(2,1)S(1)}, u32[]{:S(2)}, u32[]{:S(2)}) collective-permute-start(bf16[800,128]{1,0:T(8,128)(2,1)S(1)} %pad_maximum_fusion.1), channel_id=1, source_target_pairs={{0,16},{1,21},{2,18},{3,23},{4,20},{5,17},{6,22},{7,19},{8,24},{9,... | collective-permute-start | bytes 614408 | tf_op jit(solution)/shard_map/ppermute | solution.py:286
  15.1 11.9 %collective-permute-start.3 = (bf16[800,128]{1,0:T(8,128)(2,1)S(1)}, bf16[800,128]{1,0:T(8,128)(2,1)S(1)}, u32[]{:S(2)}, u32[]{:S(2)}) collective-permute-start(bf16[800,128]{1,0:T(8,128)(2,1)S(1)} %pad_maximum_fusion.2), channel_id=1, source_target_pairs={{0,8},{1,13},{2,10},{3,15},{4,12},{5,9},{6,14},{7,11},{8,0},{9,5},... | collective-permute-start | bytes 614408 | tf_op jit(solution)/shard_map/ppermute | solution.py:286
  15.3 16.5 %collective-permute-start.9 = (bf16[800,128]{1,0:T(8,128)(2,1)S(1)}, bf16[800,128]{1,0:T(8,128)(2,1)S(1)}, u32[]{:S(2)}, u32[]{:S(2)}) collective-permute-start(bf16[800,128]{1,0:T(8,128)(2,1)S(1)} %pad_maximum_fusion.3.refs_0_), channel_id=1, source_target_pairs={{0,2},{1,3},{2,0},{3,1},{4,6},{5,7},{6,4},{7,5},{8,10},{9,11},{10,... | collective-permute-start | bytes 614408 | tf_op jit(solution)/shard_map/ppermute | solution.py:286
  25.7 7.4 %collective-permute-start.8 = (bf16[800,128]{1,0:T(8,128)(2,1)S(1)}, bf16[800,128]{1,0:T(8,128)(2,1)S(1)}, u32[]{:S(2)}, u32[]{:S(2)}) collective-permute-start(bf16[800,128]{1,0:T(8,128)(2,1)S(1)} %broadcast_add_fusion.2.refs_0_), channel_id=1, source_target_pairs={{0,2},{1,3},{2,0},{3,1},{4,6},{5,7},{6,4},{7,5},{8,10},{9,11},{10,... | collective-permute-start | bytes 614408 | tf_op jit(solution)/shard_map/ppermute | solution.py:286
  28.6 7.6 %collective-permute-start.7 = (bf16[800,128]{1,0:T(8,128)(2,1)S(1)}, bf16[800,128]{1,0:T(8,128)(2,1)S(1)}, u32[]{:S(2)}, u32[]{:S(2)}) collective-permute-start(bf16[800,128]{1,0:T(8,128)(2,1)S(1)} %broadcast_add_fusion.1.refs_0_), channel_id=1, source_target_pairs={{0,2},{1,3},{2,0},{3,1},{4,6},{5,7},{6,4},{7,5},{8,10},{9,11},{10,... | collective-permute-start | bytes 614408 | tf_op jit(solution)/shard_map/ppermute | solution.py:286
  28.9 11.7 %collective-permute-start.6 = (bf16[800,128]{1,0:T(8,128)(2,1)S(1)}, bf16[800,128]{1,0:T(8,128)(2,1)S(1)}, u32[]{:S(2)}, u32[]{:S(2)}) collective-permute-start(bf16[800,128]{1,0:T(8,128)(2,1)S(1)} %broadcast_add_fusion.refs_0_), channel_id=1, source_target_pairs={{0,2},{1,3},{2,0},{3,1},{4,6},{5,7},{6,4},{7,5},{8,10},{9,11},{10,... | collective-permute-start | bytes 614408 | tf_op jit(solution)/shard_map/ppermute | solution.py:286
  38.0 7.8 %copy-start = (f32[4096,128]{1,0:T(8,128)S(1)}, f32[4096,128]{1,0:T(8,128)}, u32[]{:S(2)}) copy-start(f32[4096,128]{1,0:T(8,128)} %weight_ref.1) | copy-start | bytes 6291460
  38.0 7.8 %copy-start.2 = (f32[4096]{0:T(1024)S(1)}, f32[4096]{0:T(1024)}, u32[]{:S(2)}) copy-start(f32[4096]{0:T(1024)} %param.11) | copy-start | bytes 49156
  42.0 3.8 %collective-permute-start.10 = (bf16[2048,256]{1,0:T(8,128)(2,1)S(1)}, bf16[2048,256]{1,0:T(8,128)(2,1)S(1)}, u32[]{:S(2)}, u32[]{:S(2)}) collective-permute-start(bf16[2048,256]{1,0:T(8,128)(2,1)S(1)} %add_lists.15.own_ref), channel_id=1, source_target_pairs={{0,1},{1,0},{2,3},{3,2},{4,5},{5,4},{6,7},{7,6},{8,9},{9,8},{10,11... | collective-permute-start | bytes 3145736 | tf_op jit(solution)/shard_map/ppermute | solution.py:286

commit v4 on v3

--- a/solution.py
+++ b/solution.py
@@ -165,12 +165,12 @@
     )(slot, ext, *after)
 
 
-def add_kernel(capacity, lists, first, last, *refs):
+def add_kernel(capacity, lists, first, last, total, start, *refs):
     in_refs, refs = refs[:lists], list(refs[lists:])
+    out_ref, rhs_ref = refs[-2:]
     before = None if first else refs.pop(0)
     beside = refs.pop(0) if last else None
-    out_ref, rhs_ref = refs
-    half = out_ref.shape[0]
+    half = total
     chunks = capacity // LANES
     highs, lows = [], []
     at = 0
@@ -192,7 +192,8 @@
                 rhs_ref[here, LANES:2 * LANES] = jnp.where(above, rows, 0.0).astype(bf16)
                 at += LANES
     place = iota((256, LANES), 0, f32)
-    for h in range(half // 256):
+    for n in range(out_ref.shape[0] // 256):
+        h = start + n
         picks = jnp.concatenate(
             [(place == jnp.where(hi == float(h), lo, -1.0)).astype(bf16) for hi, lo in zip(highs, lows)], axis=1)
         part = jnp.dot(picks, rhs_ref[...], preferred_element_type=f32)
@@ -201,73 +202,72 @@
             part = part + before[here, :]
         if beside is not None:
             part = part + beside[here, :]
-        out_ref[here, :] = part.astype(out_ref.dtype)
-
-
-def add_lists(lists, before, beside, half, capacity):
+        out_ref[n * 256:(n + 1) * 256, :] = part.astype(out_ref.dtype)
+
+
+def add_lists(lists, before, beside, half, capacity, piece=0, pieces=1, after=()):
     vmem = pl.BlockSpec(memory_space=pltpu.VMEM)
     n = len(lists)
     depth = sum(value.shape[0] for value in lists) // (capacity + PAD) * capacity
     more = [value for value in (before, beside) if value is not None]
     return pl.pallas_call(
-        functools.partial(add_kernel, capacity, n, before is None, beside is not None),
-        out_shape=jax.ShapeDtypeStruct((half, 2 * LANES), f32 if beside is None else bf16),
-        in_specs=[vmem] * (n + len(more)),
+        functools.partial(add_kernel, capacity, n, before is None, beside is not None, half, piece * (half // pieces // 256)),
+        out_shape=jax.ShapeDtypeStruct((half // pieces, 2 * LANES), f32 if beside is None else bf16),
+        in_specs=[vmem] * (n + len(more)) + [pl.BlockSpec(memory_space=pl.ANY)] * len(after),
         out_specs=vmem,
         scratch_shapes=[pltpu.VMEM((depth, 2 * LANES), bf16)],
         input_output_aliases={n: 0} if beside is None and before is not None else {},
         compiler_params=pltpu.CompilerParams(vmem_limit_bytes=VMEM_LIMIT),
         cost_estimate=MEDIUM,
         name="add_lists",
-    )(*lists, *more)
-
-
-def update_kernel(own_ref, other_ref, weight_ref, accum_ref, new_weight_hbm, new_accum_ref, out_ref, sems):
+    )(*lists, *more, *after)
+
+
+def update_kernel(first, own_ref, other_ref, weight_ref, accum_ref, *refs):
+    new_weight_hbm, new_accum_ref, out_ref, sems = refs[-4:]
     blocks = accum_ref.shape[0]
-    half = own_ref.shape[0]
-    parts = 4
-    span = blocks // parts
+    span = own_ref.shape[0] // LANES
     lane = iota((LANES, LANES), 1)
-
-    def grad(b):
-        top = (b * LANES) % half
-        side = (b * LANES) // half
-        at, to = slice(top, top + LANES), slice(side * LANES, (side + 1) * LANES)
-        return own_ref[at, to].astype(f32) + other_ref[at, to].astype(f32)
-
     old = jnp.concatenate([accum_ref[...], jnp.zeros((LANES - blocks, LANES), f32)], axis=0).T
     new = old
     copies = []
-    for p in range(parts):
-        for b in range(p * span, (p + 1) * span):
-            g = grad(b)
-            new = jnp.where(lane == b, new + jnp.sum(g * g, axis=1, keepdims=True) * (1.0 / LANES), new)
+    for side in range(2):
+        base = side * (blocks // 2) + first * span
+
+        def grad(n):
+            at, to = slice(n * LANES, (n + 1) * LANES), slice(side * LANES, (side + 1) * LANES)
+            return own_ref[at, to].astype(f32) + other_ref[at, to].astype(f32)
+
+        for n in range(span):
+            g = grad(n)
+            new = jnp.where(lane == base + n, new + jnp.sum(g * g, axis=1, keepdims=True) * (1.0 / LANES), new)
         scale = step_size / (jnp.sqrt(new) + epsilon)
-        for b in range(p * span, (p + 1) * span):
-            here = slice(b * LANES, (b + 1) * LANES)
-            out_ref[here, :] = weight_ref[here, :] - grad(b) * scale[:, b:b + 1]
-        rows = slice(p * span * LANES, (p + 1) * span * LANES)
-        copies.append(pltpu.make_async_copy(out_ref.at[rows], new_weight_hbm.at[rows], sems.at[p]))
+        for n in range(span):
+            b = base + n
+            out_ref[(side * span + n) * LANES:(side * span + n + 1) * LANES, :] = (
+                weight_ref[b * LANES:(b + 1) * LANES, :] - grad(n) * scale[:, b:b + 1])
+        copies.append(pltpu.make_async_copy(
+            out_ref.at[side * span * LANES:(side + 1) * span * LANES],
+            new_weight_hbm.at[base * LANES:(base + span) * LANES], sems.at[side]))
         copies[-1].start()
     new_accum_ref[...] = new.T[:blocks]
     for copy in copies:
         copy.wait()
 
 
-def update(own, other, weight, accum):
-    rows = weight.shape[0]
-    blocks = rows // LANES
+def update(piece, own, other, weight, accum, so_far):
     vmem, hbm = pl.BlockSpec(memory_space=pltpu.VMEM), pl.BlockSpec(memory_space=pltpu.HBM)
-    new_weight, new_accum = pl.pallas_call(
-        update_kernel,
-        out_shape=[jax.ShapeDtypeStruct(weight.shape, f32), jax.ShapeDtypeStruct((blocks, LANES), f32)],
-        in_specs=[vmem, vmem, vmem, vmem],
+    more = [] if so_far is None else [so_far]
+    return pl.pallas_call(
+        functools.partial(update_kernel, piece),
+        out_shape=[jax.ShapeDtypeStruct(weight.shape, f32), jax.ShapeDtypeStruct(accum.shape, f32)],
+        in_specs=[vmem] * 4 + [hbm] * len(more),
         out_specs=[hbm, vmem],
-        scratch_shapes=[pltpu.VMEM(weight.shape, f32), pltpu.SemaphoreType.DMA((4,))],
+        scratch_shapes=[pltpu.VMEM((2 * own.shape[0], LANES), f32), pltpu.SemaphoreType.DMA((2,))],
+        input_output_aliases={4: 0} if more else {},
         compiler_params=pltpu.CompilerParams(vmem_limit_bytes=VMEM_LIMIT),
         name="update",
-    )(own, other, weight, accum.reshape(blocks, LANES))
-    return new_weight, new_accum.reshape(-1)
+    )(own, other, weight, accum, *more)
 
 
 def tied(value, after):
@@ -313,14 +313,28 @@
     for n, q in enumerate(near):
         lists[q] = send(q, jnp.concatenate([kept[n], got[n]], axis=0))
 
-    own = copy = None
-    order = (0, far, 1, far - 1)
-    for q in order:
-        here = lists[q] if own is None else tied(lists[q], own)
-        there = to_copy(here)
-        own = add_lists([here], own, None, half, capacity)
-        copy = add_lists([there], copy, own if q == order[-1] else None, half, capacity)
-    return update(copy, to_core(copy), weight, accum)
+    last = far - 1
+    there = to_copy(lists[0])
+    own = add_lists([lists[0]], None, None, half, capacity)
+    here_far = tied(lists[far], own)
+    there_far = to_copy(here_far)
+    here_near = tied(lists[1], here_far)
+    there_near = to_copy(here_near)
+    here_last = tied(lists[last], here_near)
+    there_last = to_copy(here_last)
+    own = add_lists([here_far, here_near], own, None, half, capacity, after=[here_last])
+    copy = add_lists([there], None, None, half, capacity, after=[here_last])
+    own = add_lists([here_last], own, None, half, capacity)
+    copy = add_lists([there_far, there_near], copy, None, half, capacity)
+    there = there_last
+
+    pieces = 2
+    sums = [add_lists([there], copy, own, half, capacity, n, pieces) for n in range(pieces)]
+    others = [to_core(value) for value in sums]
+    new_weight, new_accum = None, accum.reshape(-1, LANES)
+    for n in range(pieces):
+        new_weight, new_accum = update(n, sums[n], others[n], weight, new_accum, new_weight)
+    return new_weight, new_accum.reshape(-1)
 
 
 def solution(mesh):

time: 49.3 us -> 48.3 us (0.980)
  the two profiles are of different devices: /device:TPU:19 before, /device:TPU:0 now
where the time goes in v4:
time: 48.3 us; the launch traced here: 48.1 us
  Pallas kernels  20.8 us (43%)
  starting transfers between devices  14.3 us (30%)
  waiting for transfers between devices  10.4 us (22%)
  local copies, waits for them, and re-layouts  1.41 us (3%)
  between operations  1.02 us (2%)
    ppermute x12, starting transfers between devices, permute(): return lax.ppermute(value, axes, pairs)  14.3 us
    pallas_call x7, Pallas kernels, add_lists(): pl.pallas_call(functools.partial(add_kernel, capacity, n, before is None,...  11.3 us
    ppermute x12, waiting for transfers between devices, permute(): return lax.ppermute(value, axes, pairs)  10.4 us
    pallas_call x2, Pallas kernels, update(): pl.pallas_call(functools.partial(update_kernel, piece), out_shape=[jax.Sh...  4.03 us
    pallas_call x4, Pallas kernels, pack_next(): pl.pallas_call(functools.partial(next_kernel, groups, capacity, wanted),...  3.72 us
    pallas_call x1, Pallas kernels, pack_first(): pl.pallas_call(functools.partial(first_kernel, groups, capacity, wanted),...  1.52 us
    unnamed x12, local copies, waits for them, and re-layouts  1.36 us
  transfers between devices with their start and end apart: 12, of which 7 were waited for; matrix products, arithmetic and copies ran while one was open for 0% of the time, Pallas kernels for 28%

profile of v4, /device:TPU:0, one launch (start us, length us, event | category | flops | bytes accessed | tf_op | source)
XLA Modules:
  0.0 48.1 jit_solution(3192918842881388405)
XLA Ops:
  0.6 0.7 %copy-done.5 = s32[2048,1]{0,1:T(1,128)S(1)} copy-done((s32[2048,1]{0,1:T(1,128)S(1)}, s32[2048,1]{0,1:T(1,128)}, u32[]{:S(2)}) %copy-start.5) | copy-done | bytes 8216
  1.6 0.6 %copy-done.1 = bf16[128,8,128]{2,1,0:T(8,128)(2,1)S(1)} copy-done((bf16[128,8,128]{2,1,0:T(8,128)(2,1)S(1)}, bf16[128,8,128]{2,1,0:T(8,128)(2,1)}, u32[]{:S(2)}) %copy-start.1) | copy-done | bytes 262168
  2.3 1.5 %pack_first.1 = (bf16[1,400,128]{2,1,0:T(8,128)(2,1)S(1)}, bf16[2048,256]{1,0:T(8,128)(2,1)S(1)}) custom-call(f32[16,128]{1,0:T(8,128)S(1)} %find_slots.1.slot_ref, s32[16,128]{1,0:T(8,128)S(1)} %bitcast.30, f32[16,128]{1,0:T(8,128)S(1)} %bitcast.31, bf16[1024,128]{1,0:T(8,128)(2,1)S(1)} %bitcast.28), custom_call_target="tpu_custom_call" | custom-call | tf_op jit(solution)/shard_map/pack_first/pallas_call | solution.py:145
  3.8 0.5 %collective-permute-start = (bf16[1,400,128]{2,1,0:T(8,128)(2,1)S(1)}, bf16[1,400,128]{2,1,0:T(8,128)(2,1)S(1)}, u32[]{:S(2)}, u32[]{:S(2)}) collective-permute-start(bf16[1,400,128]{2,1,0:T(8,128)(2,1)S(1)} %get-tuple-element.9), channel_id=1, source_target_pairs={{0,1},{1,0},{2,3},{3,2},{4,5},{5,4},{6,7},{7,6},{8,9},{9,8},{10,11... | collective-permute-start | bytes 307208 | tf_op jit(solution)/shard_map/ppermute | solution.py:286
  4.3 0.6 %pack_next.4 = bf16[1,400,128]{2,1,0:T(8,128)(2,1)S(1)} custom-call(f32[16,128]{1,0:T(8,128)S(1)} %find_slots.1.slot_ref, bf16[2048,256]{1,0:T(8,128)(2,1)S(1)} %get-tuple-element.8.ext_ref), custom_call_target="tpu_custom_call" | custom-call | flops 1024 | bytes 1024 | tf_op jit(solution)/shard_map/pack_next/pallas_call | solution.py:157
  4.9 0.3 collective-permute-done
  5.3 1.0 %pack_next.6 = bf16[2,400,128]{2,1,0:T(8,128)(2,1)S(1)} custom-call(f32[16,128]{1,0:T(8,128)S(1)} %find_slots.1.slot_ref, bf16[2048,256]{1,0:T(8,128)(2,1)S(1)} %get-tuple-element.8.ext_ref, bf16[800,128]{1,0:T(8,128)(2,1)S(1)} %pad_maximum_fusion.refs_0_), custom_call_target="tpu_custom_call" | custom-call | flops 1024 | bytes 1024 | tf_op jit(solution)/shard_map/pack_next/pallas_call | solution.py:157
  6.3 1.0 %pack_next.5 = bf16[2,400,128]{2,1,0:T(8,128)(2,1)S(1)} custom-call(f32[16,128]{1,0:T(8,128)S(1)} %find_slots.1.slot_ref, bf16[2048,256]{1,0:T(8,128)(2,1)S(1)} %get-tuple-element.8.ext_ref, bf16[800,128]{1,0:T(8,128)(2,1)S(1)} %pad_maximum_fusion.refs_0_), custom_call_target="tpu_custom_call" | custom-call | flops 1024 | bytes 1024 | tf_op jit(solution)/shard_map/pack_next/pallas_call | solution.py:157
  7.4 5.0 %collective-permute-start.4 = (bf16[800,128]{1,0:T(8,128)(2,1)S(1)}, bf16[800,128]{1,0:T(8,128)(2,1)S(1)}, u32[]{:S(2)}, u32[]{:S(2)}) collective-permute-start(bf16[800,128]{1,0:T(8,128)(2,1)S(1)} %pad_maximum_fusion.refs_0_), channel_id=1, source_target_pairs={{0,24},{1,29},{2,26},{3,31},{4,28},{5,25},{6,30},{7,27},{8,16},{9,... | collective-permute-start | bytes 614408 | tf_op jit(solution)/shard_map/ppermute | solution.py:286
  12.4 0.8 %collective-permute-start.1 = (bf16[2,400,128]{2,1,0:T(8,128)(2,1)S(1)}, bf16[2,400,128]{2,1,0:T(8,128)(2,1)S(1)}, u32[]{:S(2)}, u32[]{:S(2)}) collective-permute-start(bf16[2,400,128]{2,1,0:T(8,128)(2,1)S(1)} %pack_next.6), channel_id=1, source_target_pairs={{0,1},{1,0},{2,3},{3,2},{4,5},{5,4},{6,7},{7,6},{8,9},{9,8},{10,11... | collective-permute-start | bytes 614408 | tf_op jit(solution)/shard_map/ppermute | solution.py:286
  13.2 1.1 %collective-permute-done.1.refs_0_ = bf16[2,400,128]{2,1,0:T(8,128)(2,1)S(1)} collective-permute-done((bf16[2,400,128]{2,1,0:T(8,128)(2,1)S(1)}, bf16[2,400,128]{2,1,0:T(8,128)(2,1)S(1)}, u32[]{:S(2)}, u32[]{:S(2)}) %collective-permute-start.1) | collective-permute-done | bytes 204832 | tf_op jit(solution)/shard_map/ppermute | solution.py:286
  14.2 1.0 %pack_next.7 = bf16[2,400,128]{2,1,0:T(8,128)(2,1)S(1)} custom-call(f32[16,128]{1,0:T(8,128)S(1)} %find_slots.1.slot_ref, bf16[2048,256]{1,0:T(8,128)(2,1)S(1)} %get-tuple-element.8.ext_ref, bf16[2,400,128]{2,1,0:T(8,128)(2,1)S(1)} %collective-permute-done.1.refs_0_), custom_call_target="tpu_custom_call" | custom-call | flops 1024 | bytes 1024 | tf_op jit(solution)/shard_map/pack_next/pallas_call | solution.py:157
  15.3 1.1 %collective-permute-start.5 = (bf16[400,128]{1,0:T(8,128)(2,1)S(1)}, bf16[400,128]{1,0:T(8,128)(2,1)S(1)}, u32[]{:S(2)}, u32[]{:S(2)}) collective-permute-start(bf16[400,128]{1,0:T(8,128)(2,1)S(1)} %get-tuple-element.15), channel_id=1, source_target_pairs={{0,4},{1,5},{2,6},{3,7},{4,0},{5,1},{6,2},{7,3},{8,12},{9,13},{10,... | collective-permute-start | bytes 307208 | tf_op jit(solution)/shard_map/ppermute | solution.py:286
  16.6 0.8 %collective-permute-start.3 = (bf16[800,128]{1,0:T(8,128)(2,1)S(1)}, bf16[800,128]{1,0:T(8,128)(2,1)S(1)}, u32[]{:S(2)}, u32[]{:S(2)}) collective-permute-start(bf16[800,128]{1,0:T(8,128)(2,1)S(1)} %pad_maximum_fusion.2), channel_id=1, source_target_pairs={{0,8},{1,13},{2,10},{3,15},{4,12},{5,9},{6,14},{7,11},{8,0},{9,5},... | collective-permute-start | bytes 614408 | tf_op jit(solution)/shard_map/ppermute | solution.py:286
  17.4 4.2 %collective-permute-done.5 = bf16[400,128]{1,0:T(8,128)(2,1)S(1)} collective-permute-done((bf16[400,128]{1,0:T(8,128)(2,1)S(1)}, bf16[400,128]{1,0:T(8,128)(2,1)S(1)}, u32[]{:S(2)}, u32[]{:S(2)}) %collective-permute-start.5) | collective-permute-done | bytes 102432 | tf_op jit(solution)/shard_map/ppermute | solution.py:286
  21.6 1.6 %collective-permute-start.9 = (bf16[800,128]{1,0:T(8,128)(2,1)S(1)}, bf16[800,128]{1,0:T(8,128)(2,1)S(1)}, u32[]{:S(2)}, u32[]{:S(2)}) collective-permute-start(bf16[800,128]{1,0:T(8,128)(2,1)S(1)} %pad_maximum_fusion.3.refs_0_), channel_id=1, source_target_pairs={{0,2},{1,3},{2,0},{3,1},{4,6},{5,7},{6,4},{7,5},{8,10},{9,11},{10,... | collective-permute-start | bytes 614408 | tf_op jit(solution)/shard_map/ppermute | solution.py:286
  23.2 1.3 %add_lists.7.refs_2_ = f32[2048,256]{1,0:T(8,128)S(1)} custom-call(bf16[800,128]{1,0:T(8,128)(2,1)S(1)} %pad_maximum_fusion.3.refs_0_), custom_call_target="tpu_custom_call" | custom-call | flops 100000000 | bytes 1024 | tf_op jit(solution)/shard_map/add_lists/pallas_call | solution.py:213
  24.6 0.5 %collective-permute-start.7 = (bf16[800,128]{1,0:T(8,128)(2,1)S(1)}, bf16[800,128]{1,0:T(8,128)(2,1)S(1)}, u32[]{:S(2)}, u32[]{:S(2)}) collective-permute-start(bf16[800,128]{1,0:T(8,128)(2,1)S(1)} %broadcast_add_fusion.2.refs_0_), channel_id=1, source_target_pairs={{0,2},{1,3},{2,0},{3,1},{4,6},{5,7},{6,4},{7,5},{8,10},{9,11},{10,... | collective-permute-start | bytes 614408 | tf_op jit(solution)/shard_map/ppermute | solution.py:286
  25.1 1.4 %collective-permute-done.3 = bf16[800,128]{1,0:T(8,128)(2,1)S(1)} collective-permute-done((bf16[800,128]{1,0:T(8,128)(2,1)S(1)}, bf16[800,128]{1,0:T(8,128)(2,1)S(1)}, u32[]{:S(2)}, u32[]{:S(2)}) %collective-permute-start.3) | collective-permute-done | bytes 204832 | tf_op jit(solution)/shard_map/ppermute | solution.py:286
  26.6 1.5 %collective-permute-start.8 = (bf16[800,128]{1,0:T(8,128)(2,1)S(1)}, bf16[800,128]{1,0:T(8,128)(2,1)S(1)}, u32[]{:S(2)}, u32[]{:S(2)}) collective-permute-start(bf16[800,128]{1,0:T(8,128)(2,1)S(1)} %broadcast_add_fusion.1.refs_1_), channel_id=1, source_target_pairs={{0,2},{1,3},{2,0},{3,1},{4,6},{5,7},{6,4},{7,5},{8,10},{9,11},{10,... | collective-permute-start | bytes 614408 | tf_op jit(solution)/shard_map/ppermute | solution.py:286
  28.1 2.6 %collective-permute-done.2 = bf16[800,128]{1,0:T(8,128)(2,1)S(1)} collective-permute-done((bf16[800,128]{1,0:T(8,128)(2,1)S(1)}, bf16[800,128]{1,0:T(8,128)(2,1)S(1)}, u32[]{:S(2)}, u32[]{:S(2)}) %collective-permute-start.2) | collective-permute-done | bytes 204832 | tf_op jit(solution)/shard_map/ppermute | solution.py:286
  30.8 1.6 %collective-permute-start.6 = (bf16[800,128]{1,0:T(8,128)(2,1)S(1)}, bf16[800,128]{1,0:T(8,128)(2,1)S(1)}, u32[]{:S(2)}, u32[]{:S(2)}) collective-permute-start(bf16[800,128]{1,0:T(8,128)(2,1)S(1)} %broadcast_add_fusion.refs_1_.refs_3_.refs_0_), channel_id=1, source_target_pairs={{0,2},{1,3},{2,0},{3,1},{4,6},{5,7},{6,4},{7,5},{8,10},{9,11},{10,... | collective-permute-start | bytes 614408 | tf_op jit(solution)/shard_map/ppermute | solution.py:286
  32.4 2.6 %add_lists.10.refs_1_ = f32[2048,256]{1,0:T(8,128)S(1)} custom-call(bf16[800,128]{1,0:T(8,128)(2,1)S(1)} %broadcast_add_fusion.2.refs_0_, bf16[800,128]{1,0:T(8,128)(2,1)S(1)} %broadcast_add_fusion.1.refs_1_, f32[2048,256]{1,0:T(8,128)S(1)} %add_lists.7.refs_2_, ...), custom_call_target="tpu_custom_call", output_to_operand_aliasing={{}: (2, {})} | custom-call | flops 100000000 | bytes 1024 | tf_op jit(solution)/shard_map/add_lists/pallas_call | solution.py:213
  35.0 1.5 %add_lists.11.refs_2_ = f32[2048,256]{1,0:T(8,128)S(1)} custom-call(bf16[800,128]{1,0:T(8,128)(2,1)S(1)} %broadcast_add_fusion.refs_1_.refs_3_.refs_0_, f32[2048,256]{1,0:T(8,128)S(1)} %add_lists.10.refs_1_), custom_call_target="tpu_custom_call", output_to_operand_aliasing={{}: (1, {})} | custom-call | flops 100000000 | bytes 1024 | tf_op jit(solution)/shard_map/add_lists/pallas_call | solution.py:213
  36.5 1.3 %add_lists.8.refs_2_ = f32[2048,256]{1,0:T(8,128)S(1)} custom-call(bf16[800,128]{1,0:T(8,128)(2,1)S(1)} %collective-permute-done.9.refs_0_, bf16[800,128]{1,0:T(8,128)(2,1)S(1)} %broadcast_add_fusion.refs_1_.refs_3_.refs_0_), custom_call_target="tpu_custom_call" | custom-call | flops 100000000 | bytes 1024 | tf_op jit(solution)/shard_map/add_lists/pallas_call | solution.py:213
  38.2 2.6 %add_lists.9.refs_1_ = f32[2048,256]{1,0:T(8,128)S(1)} custom-call(bf16[800,128]{1,0:T(8,128)(2,1)S(1)} %collective-permute-done.7.refs_0_, bf16[800,128]{1,0:T(8,128)(2,1)S(1)} %collective-permute-done.8.refs_1_, f32[2048,256]{1,0:T(8,128)S(1)} %add_lists.8.refs_2_), custom_call_target="tpu_custom_call", output_to_operand_aliasing={{}: (2, {})} | custom-call | flops 100000000 | bytes 1024 | tf_op jit(solution)/shard_map/add_lists/pallas_call | solution.py:213
  40.7 1.1 %add_lists.13.own_ref = bf16[1024,256]{1,0:T(8,128)(2,1)S(1)} custom-call(bf16[800,128]{1,0:T(8,128)(2,1)S(1)} %collective-permute-done.6.refs_0_, f32[2048,256]{1,0:T(8,128)S(1)} %add_lists.9.refs_1_, f32[2048,256]{1,0:T(8,128)S(1)} %add_lists.11.refs_2_), custom_call_target="tpu_custom_call" | custom-call | flops 100000000 | bytes 1024 | tf_op jit(solution)/shard_map/add_lists/pallas_call | solution.py:213
  42.0 0.9 %add_lists.12.own_ref = bf16[1024,256]{1,0:T(8,128)(2,1)S(1)} custom-call(bf16[800,128]{1,0:T(8,128)(2,1)S(1)} %collective-permute-done.6.refs_0_, f32[2048,256]{1,0:T(8,128)S(1)} %add_lists.9.refs_1_, f32[2048,256]{1,0:T(8,128)S(1)} %add_lists.11.refs_2_), custom_call_target="tpu_custom_call" | custom-call | flops 100000000 | bytes 1024 | tf_op jit(solution)/shard_map/add_lists/pallas_call | solution.py:213
  42.9 0.6 %collective-permute-start.10 = (bf16[1024,256]{1,0:T(8,128)(2,1)S(1)}, bf16[1024,256]{1,0:T(8,128)(2,1)S(1)}, u32[]{:S(2)}, u32[]{:S(2)}) collective-permute-start(bf16[1024,256]{1,0:T(8,128)(2,1)S(1)} %add_lists.12.own_ref), channel_id=1, source_target_pairs={{0,1},{1,0},{2,3},{3,2},{4,5},{5,4},{6,7},{7,6},{8,9},{9,8},{10,11... | collective-permute-start | bytes 1572872 | tf_op jit(solution)/shard_map/ppermute | solution.py:286
  43.5 0.4 collective-permute-done.11.other_ref
  43.9 1.7 %update.2 = (f32[4096,128]{1,0:T(8,128)}, f32[32,128]{1,0:T(8,128)S(1)}) custom-call(bf16[1024,256]{1,0:T(8,128)(2,1)S(1)} %add_lists.13.own_ref, bf16[1024,256]{1,0:T(8,128)(2,1)S(1)} %collective-permute-done.11.other_ref, f32[4096,128]{1,0:T(8,128)S(1)} %copy-done, f32[32,128]{1,0:T(8,128)S(1)} %bitcast.29), custom_call_target="tpu_custom_call" | custom-call | tf_op jit(solution)/shard_map/update/pallas_call | solution.py:261
  45.6 2.3 %update.3 = (f32[4096,128]{1,0:T(8,128)}, f32[32,128]{1,0:T(8,128)}) custom-call(bf16[1024,256]{1,0:T(8,128)(2,1)S(1)} %add_lists.12.own_ref, bf16[1024,256]{1,0:T(8,128)(2,1)S(1)} %collective-permute-done.10.other_ref, f32[4096,128]{1,0:T(8,128)S(1)} %copy-done, f32[32,128]{1,0:T(8,128)S(1)} %get-tuple-element.10.accum_ref, ...), custom_call_target="tpu_custom_call", output_to_operand_aliasing={{0}: (4, {})} | custom-call | tf_op jit(solution)/shard_map/update/pallas_call | solution.py:261
  (32 shorter events, 1.0 us)
Async XLA Ops:
  0.6 0.7 %copy-start.5 = (s32[2048,1]{0,1:T(1,128)S(1)}, s32[2048,1]{0,1:T(1,128)}, u32[]{:S(2)}) copy-start(s32[2048,1]{0,1:T(1,128)} %param.8) | copy-start | bytes 24580
  1.3 0.9 %copy-start.1 = (bf16[128,8,128]{2,1,0:T(8,128)(2,1)S(1)}, bf16[128,8,128]{2,1,0:T(8,128)(2,1)}, u32[]{:S(2)}) copy-start(bf16[128,8,128]{2,1,0:T(8,128)(2,1)} %param.6) | copy-start | bytes 786436
  1.3 1.0 %copy-start.3 = (s32[2048]{0:T(1024)S(1)}, s32[2048]{0:T(1024)}, u32[]{:S(2)}) copy-start(s32[2048]{0:T(1024)} %param.9) | copy-start | bytes 24580
  1.3 1.0 %copy-start.4 = (f32[2048]{0:T(1024)S(1)}, f32[2048]{0:T(1024)}, u32[]{:S(2)}) copy-start(f32[2048]{0:T(1024)} %param.7) | copy-start | bytes 24580
  3.8 1.5 %collective-permute-start = (bf16[1,400,128]{2,1,0:T(8,128)(2,1)S(1)}, bf16[1,400,128]{2,1,0:T(8,128)(2,1)S(1)}, u32[]{:S(2)}, u32[]{:S(2)}) collective-permute-start(bf16[1,400,128]{2,1,0:T(8,128)(2,1)S(1)} %get-tuple-element.9), channel_id=1, source_target_pairs={{0,1},{1,0},{2,3},{3,2},{4,5},{5,4},{6,7},{7,6},{8,9},{9,8},{10,11... | collective-permute-start | bytes 307208 | tf_op jit(solution)/shard_map/ppermute | solution.py:286
  7.4 17.2 %collective-permute-start.4 = (bf16[800,128]{1,0:T(8,128)(2,1)S(1)}, bf16[800,128]{1,0:T(8,128)(2,1)S(1)}, u32[]{:S(2)}, u32[]{:S(2)}) collective-permute-start(bf16[800,128]{1,0:T(8,128)(2,1)S(1)} %pad_maximum_fusion.refs_0_), channel_id=1, source_target_pairs={{0,24},{1,29},{2,26},{3,31},{4,28},{5,25},{6,30},{7,27},{8,16},{9,... | collective-permute-start | bytes 614408 | tf_op jit(solution)/shard_map/ppermute | solution.py:286
  12.4 1.9 %collective-permute-start.1 = (bf16[2,400,128]{2,1,0:T(8,128)(2,1)S(1)}, bf16[2,400,128]{2,1,0:T(8,128)(2,1)S(1)}, u32[]{:S(2)}, u32[]{:S(2)}) collective-permute-start(bf16[2,400,128]{2,1,0:T(8,128)(2,1)S(1)} %pack_next.6), channel_id=1, source_target_pairs={{0,1},{1,0},{2,3},{3,2},{4,5},{5,4},{6,7},{7,6},{8,9},{9,8},{10,11... | collective-permute-start | bytes 614408 | tf_op jit(solution)/shard_map/ppermute | solution.py:286
  15.3 6.3 %collective-permute-start.5 = (bf16[400,128]{1,0:T(8,128)(2,1)S(1)}, bf16[400,128]{1,0:T(8,128)(2,1)S(1)}, u32[]{:S(2)}, u32[]{:S(2)}) collective-permute-start(bf16[400,128]{1,0:T(8,128)(2,1)S(1)} %get-tuple-element.15), channel_id=1, source_target_pairs={{0,4},{1,5},{2,6},{3,7},{4,0},{5,1},{6,2},{7,3},{8,12},{9,13},{10,... | collective-permute-start | bytes 307208 | tf_op jit(solution)/shard_map/ppermute | solution.py:286
  16.5 14.3 %collective-permute-start.2 = (bf16[800,128]{1,0:T(8,128)(2,1)S(1)}, bf16[800,128]{1,0:T(8,128)(2,1)S(1)}, u32[]{:S(2)}, u32[]{:S(2)}) collective-permute-start(bf16[800,128]{1,0:T(8,128)(2,1)S(1)} %pad_maximum_fusion.1), channel_id=1, source_target_pairs={{0,16},{1,21},{2,18},{3,23},{4,20},{5,17},{6,22},{7,19},{8,24},{9,... | collective-permute-start | bytes 614408 | tf_op jit(solution)/shard_map/ppermute | solution.py:286
  16.6 10.0 %collective-permute-start.3 = (bf16[800,128]{1,0:T(8,128)(2,1)S(1)}, bf16[800,128]{1,0:T(8,128)(2,1)S(1)}, u32[]{:S(2)}, u32[]{:S(2)}) collective-permute-start(bf16[800,128]{1,0:T(8,128)(2,1)S(1)} %pad_maximum_fusion.2), channel_id=1, source_target_pairs={{0,8},{1,13},{2,10},{3,15},{4,12},{5,9},{6,14},{7,11},{8,0},{9,5},... | collective-permute-start | bytes 614408 | tf_op jit(solution)/shard_map/ppermute | solution.py:286
  21.6 14.9 %collective-permute-start.9 = (bf16[800,128]{1,0:T(8,128)(2,1)S(1)}, bf16[800,128]{1,0:T(8,128)(2,1)S(1)}, u32[]{:S(2)}, u32[]{:S(2)}) collective-permute-start(bf16[800,128]{1,0:T(8,128)(2,1)S(1)} %pad_maximum_fusion.3.refs_0_), channel_id=1, source_target_pairs={{0,2},{1,3},{2,0},{3,1},{4,6},{5,7},{6,4},{7,5},{8,10},{9,11},{10,... | collective-permute-start | bytes 614408 | tf_op jit(solution)/shard_map/ppermute | solution.py:286
  24.6 13.3 %collective-permute-start.7 = (bf16[800,128]{1,0:T(8,128)(2,1)S(1)}, bf16[800,128]{1,0:T(8,128)(2,1)S(1)}, u32[]{:S(2)}, u32[]{:S(2)}) collective-permute-start(bf16[800,128]{1,0:T(8,128)(2,1)S(1)} %broadcast_add_fusion.2.refs_0_), channel_id=1, source_target_pairs={{0,2},{1,3},{2,0},{3,1},{4,6},{5,7},{6,4},{7,5},{8,10},{9,11},{10,... | collective-permute-start | bytes 614408 | tf_op jit(solution)/shard_map/ppermute | solution.py:286
  26.6 11.6 %collective-permute-start.8 = (bf16[800,128]{1,0:T(8,128)(2,1)S(1)}, bf16[800,128]{1,0:T(8,128)(2,1)S(1)}, u32[]{:S(2)}, u32[]{:S(2)}) collective-permute-start(bf16[800,128]{1,0:T(8,128)(2,1)S(1)} %broadcast_add_fusion.1.refs_1_), channel_id=1, source_target_pairs={{0,2},{1,3},{2,0},{3,1},{4,6},{5,7},{6,4},{7,5},{8,10},{9,11},{10,... | collective-permute-start | bytes 614408 | tf_op jit(solution)/shard_map/ppermute | solution.py:286
  30.8 9.9 %collective-permute-start.6 = (bf16[800,128]{1,0:T(8,128)(2,1)S(1)}, bf16[800,128]{1,0:T(8,128)(2,1)S(1)}, u32[]{:S(2)}, u32[]{:S(2)}) collective-permute-start(bf16[800,128]{1,0:T(8,128)(2,1)S(1)} %broadcast_add_fusion.refs_1_.refs_3_.refs_0_), channel_id=1, source_target_pairs={{0,2},{1,3},{2,0},{3,1},{4,6},{5,7},{6,4},{7,5},{8,10},{9,11},{10,... | collective-permute-start | bytes 614408 | tf_op jit(solution)/shard_map/ppermute | solution.py:286
  41.9 2.0 %copy-start = (f32[4096,128]{1,0:T(8,128)S(1)}, f32[4096,128]{1,0:T(8,128)}, u32[]{:S(2)}) copy-start(f32[4096,128]{1,0:T(8,128)} %weight_ref.3) | copy-start | bytes 6291460
  41.9 2.0 %copy-start.2 = (f32[4096]{0:T(1024)S(1)}, f32[4096]{0:T(1024)}, u32[]{:S(2)}) copy-start(f32[4096]{0:T(1024)} %param.11) | copy-start | bytes 49156
  41.9 2.0 %collective-permute-start.11 = (bf16[1024,256]{1,0:T(8,128)(2,1)S(1)}, bf16[1024,256]{1,0:T(8,128)(2,1)S(1)}, u32[]{:S(2)}, u32[]{:S(2)}) collective-permute-start(bf16[1024,256]{1,0:T(8,128)(2,1)S(1)} %add_lists.13.own_ref), channel_id=1, source_target_pairs={{0,1},{1,0},{2,3},{3,2},{4,5},{5,4},{6,7},{7,6},{8,9},{9,8},{10,11... | collective-permute-start | bytes 1572872 | tf_op jit(solution)/shard_map/ppermute | solution.py:286
  42.9 2.7 %collective-permute-start.10 = (bf16[1024,256]{1,0:T(8,128)(2,1)S(1)}, bf16[1024,256]{1,0:T(8,128)(2,1)S(1)}, u32[]{:S(2)}, u32[]{:S(2)}) collective-permute-start(bf16[1024,256]{1,0:T(8,128)(2,1)S(1)} %add_lists.12.own_ref), channel_id=1, source_target_pairs={{0,1},{1,0},{2,3},{3,2},{4,5},{5,4},{6,7},{7,6},{8,9},{9,8},{10,11... | collective-permute-start | bytes 1572872 | tf_op jit(solution)/shard_map/ppermute | solution.py:286

commit v5 on v4

--- a/solution.py
+++ b/solution.py
@@ -320,12 +320,14 @@
     there_far = to_copy(here_far)
     here_near = tied(lists[1], here_far)
     there_near = to_copy(here_near)
-    here_last = tied(lists[last], here_near)
+    own = add_lists([here_far], own, None, half, capacity, after=[here_near])
+    copy = add_lists([there], None, None, half, capacity, after=[here_near])
+    here_last = tied(lists[last], own)
     there_last = to_copy(here_last)
-    own = add_lists([here_far, here_near], own, None, half, capacity, after=[here_last])
-    copy = add_lists([there], None, None, half, capacity, after=[here_last])
+    own = add_lists([here_near], own, None, half, capacity, after=[here_last])
+    copy = add_lists([there_far], copy, None, half, capacity, after=[here_last])
     own = add_lists([here_last], own, None, half, capacity)
-    copy = add_lists([there_far, there_near], copy, None, half, capacity)
+    copy = add_lists([there_near], copy, None, half, capacity)
     there = there_last
 
     pieces = 2

time: 48.3 us -> 47.9 us (level)
  waiting for transfers between devices: 10.4 us -> 8.96 us
  Pallas kernels: 20.8 us -> 21.9 us
    ppermute x12, waiting for transfers between devices: 10.4 us -> 8.96 us  [permute(): return lax.ppermute(value, axes, pairs)]
    pallas_call x7 -> x9, Pallas kernels: 11.3 us -> 12.4 us  [add_lists(): pl.pallas_call(functools.partial(add_kernel, capacity, n, before is None,...]
  transfers between devices with their start and end apart: 12 -> 12, of which waited for: 7 -> 7; matrix products, arithmetic and copies ran while one was open for 0% -> 0% of each run, Pallas kernels for 28% -> 31%
where the time goes in v5:
time: 47.9 us; the launch traced here: 47.7 us
  Pallas kernels  21.9 us (46%)
  starting transfers between devices  14.3 us (30%)
  waiting for transfers between devices  8.96 us (19%)
  local copies, waits for them, and re-layouts  1.41 us (3%)
  between operations  1.03 us (2%)
    ppermute x12, starting transfers between devices, permute(): return lax.ppermute(value, axes, pairs)  14.3 us
    pallas_call x9, Pallas kernels, add_lists(): pl.pallas_call(functools.partial(add_kernel, capacity, n, before is None,...  12.4 us
    ppermute x12, waiting for transfers between devices, permute(): return lax.ppermute(value, axes, pairs)  8.96 us
    pallas_call x2, Pallas kernels, update(): pl.pallas_call(functools.partial(update_kernel, piece), out_shape=[jax.Sh...  4.03 us
    pallas_call x4, Pallas kernels, pack_next(): pl.pallas_call(functools.partial(next_kernel, groups, capacity, wanted),...  3.72 us
    pallas_call x1, Pallas kernels, pack_first(): pl.pallas_call(functools.partial(first_kernel, groups, capacity, wanted),...  1.52 us
    unnamed x12, local copies, waits for them, and re-layouts  1.36 us
  transfers between devices with their start and end apart: 12, of which 7 were waited for; matrix products, arithmetic and copies ran while one was open for 0% of the time, Pallas kernels for 31%

profile of v5, /device:TPU:0, one launch (start us, length us, event | category | flops | bytes accessed | tf_op | source)
XLA Modules:
  0.0 47.7 jit_solution(6594546327749741765)
XLA Ops:
  0.6 0.7 %copy-done.5 = s32[2048,1]{0,1:T(1,128)S(1)} copy-done((s32[2048,1]{0,1:T(1,128)S(1)}, s32[2048,1]{0,1:T(1,128)}, u32[]{:S(2)}) %copy-start.5) | copy-done | bytes 8216
  1.6 0.6 %copy-done.1 = bf16[128,8,128]{2,1,0:T(8,128)(2,1)S(1)} copy-done((bf16[128,8,128]{2,1,0:T(8,128)(2,1)S(1)}, bf16[128,8,128]{2,1,0:T(8,128)(2,1)}, u32[]{:S(2)}) %copy-start.1) | copy-done | bytes 262168
  2.3 1.5 %pack_first.1 = (bf16[1,400,128]{2,1,0:T(8,128)(2,1)S(1)}, bf16[2048,256]{1,0:T(8,128)(2,1)S(1)}) custom-call(f32[16,128]{1,0:T(8,128)S(1)} %find_slots.1.slot_ref, s32[16,128]{1,0:T(8,128)S(1)} %bitcast.30, f32[16,128]{1,0:T(8,128)S(1)} %bitcast.31, bf16[1024,128]{1,0:T(8,128)(2,1)S(1)} %bitcast.28), custom_call_target="tpu_custom_call" | custom-call | tf_op jit(solution)/shard_map/pack_first/pallas_call | solution.py:145
  3.8 0.5 %collective-permute-start = (bf16[1,400,128]{2,1,0:T(8,128)(2,1)S(1)}, bf16[1,400,128]{2,1,0:T(8,128)(2,1)S(1)}, u32[]{:S(2)}, u32[]{:S(2)}) collective-permute-start(bf16[1,400,128]{2,1,0:T(8,128)(2,1)S(1)} %get-tuple-element.9), channel_id=1, source_target_pairs={{0,1},{1,0},{2,3},{3,2},{4,5},{5,4},{6,7},{7,6},{8,9},{9,8},{10,11... | collective-permute-start | bytes 307208 | tf_op jit(solution)/shard_map/ppermute | solution.py:286
  4.3 0.6 %pack_next.4 = bf16[1,400,128]{2,1,0:T(8,128)(2,1)S(1)} custom-call(f32[16,128]{1,0:T(8,128)S(1)} %find_slots.1.slot_ref, bf16[2048,256]{1,0:T(8,128)(2,1)S(1)} %get-tuple-element.8.ext_ref), custom_call_target="tpu_custom_call" | custom-call | flops 1024 | bytes 1024 | tf_op jit(solution)/shard_map/pack_next/pallas_call | solution.py:157
  5.3 1.0 %pack_next.6 = bf16[2,400,128]{2,1,0:T(8,128)(2,1)S(1)} custom-call(f32[16,128]{1,0:T(8,128)S(1)} %find_slots.1.slot_ref, bf16[2048,256]{1,0:T(8,128)(2,1)S(1)} %get-tuple-element.8.ext_ref, bf16[800,128]{1,0:T(8,128)(2,1)S(1)} %pad_maximum_fusion.refs_0_), custom_call_target="tpu_custom_call" | custom-call | flops 1024 | bytes 1024 | tf_op jit(solution)/shard_map/pack_next/pallas_call | solution.py:157
  6.3 1.0 %pack_next.5 = bf16[2,400,128]{2,1,0:T(8,128)(2,1)S(1)} custom-call(f32[16,128]{1,0:T(8,128)S(1)} %find_slots.1.slot_ref, bf16[2048,256]{1,0:T(8,128)(2,1)S(1)} %get-tuple-element.8.ext_ref, bf16[800,128]{1,0:T(8,128)(2,1)S(1)} %pad_maximum_fusion.refs_0_), custom_call_target="tpu_custom_call" | custom-call | flops 1024 | bytes 1024 | tf_op jit(solution)/shard_map/pack_next/pallas_call | solution.py:157
  7.4 5.0 %collective-permute-start.3 = (bf16[800,128]{1,0:T(8,128)(2,1)S(1)}, bf16[800,128]{1,0:T(8,128)(2,1)S(1)}, u32[]{:S(2)}, u32[]{:S(2)}) collective-permute-start(bf16[800,128]{1,0:T(8,128)(2,1)S(1)} %pad_maximum_fusion.refs_0_), channel_id=1, source_target_pairs={{0,24},{1,29},{2,26},{3,31},{4,28},{5,25},{6,30},{7,27},{8,16},{9,... | collective-permute-start | bytes 614408 | tf_op jit(solution)/shard_map/ppermute | solution.py:286
  12.4 0.8 %collective-permute-start.1 = (bf16[2,400,128]{2,1,0:T(8,128)(2,1)S(1)}, bf16[2,400,128]{2,1,0:T(8,128)(2,1)S(1)}, u32[]{:S(2)}, u32[]{:S(2)}) collective-permute-start(bf16[2,400,128]{2,1,0:T(8,128)(2,1)S(1)} %pack_next.6), channel_id=1, source_target_pairs={{0,1},{1,0},{2,3},{3,2},{4,5},{5,4},{6,7},{7,6},{8,9},{9,8},{10,11... | collective-permute-start | bytes 614408 | tf_op jit(solution)/shard_map/ppermute | solution.py:286
  13.2 1.1 %collective-permute-done.1.refs_0_ = bf16[2,400,128]{2,1,0:T(8,128)(2,1)S(1)} collective-permute-done((bf16[2,400,128]{2,1,0:T(8,128)(2,1)S(1)}, bf16[2,400,128]{2,1,0:T(8,128)(2,1)S(1)}, u32[]{:S(2)}, u32[]{:S(2)}) %collective-permute-start.1) | collective-permute-done | bytes 204832 | tf_op jit(solution)/shard_map/ppermute | solution.py:286
  14.2 1.0 %pack_next.7 = bf16[2,400,128]{2,1,0:T(8,128)(2,1)S(1)} custom-call(f32[16,128]{1,0:T(8,128)S(1)} %find_slots.1.slot_ref, bf16[2048,256]{1,0:T(8,128)(2,1)S(1)} %get-tuple-element.8.ext_ref, bf16[2,400,128]{2,1,0:T(8,128)(2,1)S(1)} %collective-permute-done.1.refs_0_), custom_call_target="tpu_custom_call" | custom-call | flops 1024 | bytes 1024 | tf_op jit(solution)/shard_map/pack_next/pallas_call | solution.py:157
  15.3 1.1 %collective-permute-start.4 = (bf16[400,128]{1,0:T(8,128)(2,1)S(1)}, bf16[400,128]{1,0:T(8,128)(2,1)S(1)}, u32[]{:S(2)}, u32[]{:S(2)}) collective-permute-start(bf16[400,128]{1,0:T(8,128)(2,1)S(1)} %get-tuple-element.19), channel_id=1, source_target_pairs={{0,4},{1,5},{2,6},{3,7},{4,0},{5,1},{6,2},{7,3},{8,12},{9,13},{10,... | collective-permute-start | bytes 307208 | tf_op jit(solution)/shard_map/ppermute | solution.py:286
  16.6 0.8 %collective-permute-start.5 = (bf16[800,128]{1,0:T(8,128)(2,1)S(1)}, bf16[800,128]{1,0:T(8,128)(2,1)S(1)}, u32[]{:S(2)}, u32[]{:S(2)}) collective-permute-start(bf16[800,128]{1,0:T(8,128)(2,1)S(1)} %pad_maximum_fusion.3), channel_id=1, source_target_pairs={{0,8},{1,13},{2,10},{3,15},{4,12},{5,9},{6,14},{7,11},{8,0},{9,5},... | collective-permute-start | bytes 614408 | tf_op jit(solution)/shard_map/ppermute | solution.py:286
  17.4 4.2 %collective-permute-done.4 = bf16[400,128]{1,0:T(8,128)(2,1)S(1)} collective-permute-done((bf16[400,128]{1,0:T(8,128)(2,1)S(1)}, bf16[400,128]{1,0:T(8,128)(2,1)S(1)}, u32[]{:S(2)}, u32[]{:S(2)}) %collective-permute-start.4) | collective-permute-done | bytes 102432 | tf_op jit(solution)/shard_map/ppermute | solution.py:286
  21.6 1.6 %collective-permute-start.9 = (bf16[800,128]{1,0:T(8,128)(2,1)S(1)}, bf16[800,128]{1,0:T(8,128)(2,1)S(1)}, u32[]{:S(2)}, u32[]{:S(2)}) collective-permute-start(bf16[800,128]{1,0:T(8,128)(2,1)S(1)} %pad_maximum_fusion.2.refs_0_), channel_id=1, source_target_pairs={{0,2},{1,3},{2,0},{3,1},{4,6},{5,7},{6,4},{7,5},{8,10},{9,11},{10,... | collective-permute-start | bytes 614408 | tf_op jit(solution)/shard_map/ppermute | solution.py:286
  23.2 1.3 %add_lists.9.refs_1_ = f32[2048,256]{1,0:T(8,128)S(1)} custom-call(bf16[800,128]{1,0:T(8,128)(2,1)S(1)} %pad_maximum_fusion.2.refs_0_), custom_call_target="tpu_custom_call" | custom-call | flops 100000000 | bytes 1024 | tf_op jit(solution)/shard_map/add_lists/pallas_call | solution.py:213
  24.6 0.5 %collective-permute-start.8 = (bf16[800,128]{1,0:T(8,128)(2,1)S(1)}, bf16[800,128]{1,0:T(8,128)(2,1)S(1)}, u32[]{:S(2)}, u32[]{:S(2)}) collective-permute-start(bf16[800,128]{1,0:T(8,128)(2,1)S(1)} %broadcast_add_fusion.2.refs_0_), channel_id=1, source_target_pairs={{0,2},{1,3},{2,0},{3,1},{4,6},{5,7},{6,4},{7,5},{8,10},{9,11},{10,... | collective-permute-start | bytes 614408 | tf_op jit(solution)/shard_map/ppermute | solution.py:286
  25.1 1.4 %collective-permute-done.5 = bf16[800,128]{1,0:T(8,128)(2,1)S(1)} collective-permute-done((bf16[800,128]{1,0:T(8,128)(2,1)S(1)}, bf16[800,128]{1,0:T(8,128)(2,1)S(1)}, u32[]{:S(2)}, u32[]{:S(2)}) %collective-permute-start.5) | collective-permute-done | bytes 204832 | tf_op jit(solution)/shard_map/ppermute | solution.py:286
  26.6 1.5 %add_lists.10.refs_1_ = f32[2048,256]{1,0:T(8,128)S(1)} custom-call(bf16[800,128]{1,0:T(8,128)(2,1)S(1)} %broadcast_add_fusion.2.refs_0_, f32[2048,256]{1,0:T(8,128)S(1)} %add_lists.9.refs_1_, bf16[800,128]{1,0:T(8,128)(2,1)S(1)} %broadcast_add_fusion.1.refs_2_.refs_1_.refs_0_), custom_call_target="tpu_custom_call", output_to_operand_aliasing={{}: (1, {})} | custom-call | flops 100000000 | bytes 1024 | tf_op jit(solution)/shard_map/add_lists/pallas_call | solution.py:213
  28.1 1.6 %collective-permute-start.7 = (bf16[800,128]{1,0:T(8,128)(2,1)S(1)}, bf16[800,128]{1,0:T(8,128)(2,1)S(1)}, u32[]{:S(2)}, u32[]{:S(2)}) collective-permute-start(bf16[800,128]{1,0:T(8,128)(2,1)S(1)} %broadcast_add_fusion.1.refs_2_.refs_1_.refs_0_), channel_id=1, source_target_pairs={{0,2},{1,3},{2,0},{3,1},{4,6},{5,7},{6,4},{7,5},{8,10},{9,11},{10,... | collective-permute-start | bytes 614408 | tf_op jit(solution)/shard_map/ppermute | solution.py:286
  29.7 1.1 %collective-permute-done.2 = bf16[800,128]{1,0:T(8,128)(2,1)S(1)} collective-permute-done((bf16[800,128]{1,0:T(8,128)(2,1)S(1)}, bf16[800,128]{1,0:T(8,128)(2,1)S(1)}, u32[]{:S(2)}, u32[]{:S(2)}) %collective-permute-start.2) | collective-permute-done | bytes 204832 | tf_op jit(solution)/shard_map/ppermute | solution.py:286
  30.8 1.6 %collective-permute-start.6 = (bf16[800,128]{1,0:T(8,128)(2,1)S(1)}, bf16[800,128]{1,0:T(8,128)(2,1)S(1)}, u32[]{:S(2)}, u32[]{:S(2)}) collective-permute-start(bf16[800,128]{1,0:T(8,128)(2,1)S(1)} %broadcast_add_fusion.refs_2_.refs_0_), channel_id=1, source_target_pairs={{0,2},{1,3},{2,0},{3,1},{4,6},{5,7},{6,4},{7,5},{8,10},{9,11},{10,... | collective-permute-start | bytes 614408 | tf_op jit(solution)/shard_map/ppermute | solution.py:286
  32.4 1.5 %add_lists.14.refs_1_ = f32[2048,256]{1,0:T(8,128)S(1)} custom-call(bf16[800,128]{1,0:T(8,128)(2,1)S(1)} %broadcast_add_fusion.1.refs_2_.refs_1_.refs_0_, f32[2048,256]{1,0:T(8,128)S(1)} %add_lists.10.refs_1_, bf16[800,128]{1,0:T(8,128)(2,1)S(1)} %broadcast_add_fusion.refs_2_.refs_0_), custom_call_target="tpu_custom_call", output_to_operand_aliasing={{}: (1, {})} | custom-call | flops 100000000 | bytes 1024 | tf_op jit(solution)/shard_map/add_lists/pallas_call | solution.py:213
  34.0 1.5 %add_lists.15.refs_2_ = f32[2048,256]{1,0:T(8,128)S(1)} custom-call(bf16[800,128]{1,0:T(8,128)(2,1)S(1)} %broadcast_add_fusion.refs_2_.refs_0_, f32[2048,256]{1,0:T(8,128)S(1)} %add_lists.14.refs_1_), custom_call_target="tpu_custom_call", output_to_operand_aliasing={{}: (1, {})} | custom-call | flops 100000000 | bytes 1024 | tf_op jit(solution)/shard_map/add_lists/pallas_call | solution.py:213
  35.5 1.3 %add_lists.11.refs_1_ = f32[2048,256]{1,0:T(8,128)S(1)} custom-call(bf16[800,128]{1,0:T(8,128)(2,1)S(1)} %collective-permute-done.9.refs_0_, bf16[800,128]{1,0:T(8,128)(2,1)S(1)} %broadcast_add_fusion.1.refs_2_.refs_1_.refs_0_), custom_call_target="tpu_custom_call" | custom-call | flops 100000000 | bytes 1024 | tf_op jit(solution)/shard_map/add_lists/pallas_call | solution.py:213
  36.8 1.5 %add_lists.12.refs_1_ = f32[2048,256]{1,0:T(8,128)S(1)} custom-call(bf16[800,128]{1,0:T(8,128)(2,1)S(1)} %collective-permute-done.8.refs_0_, f32[2048,256]{1,0:T(8,128)S(1)} %add_lists.11.refs_1_, bf16[800,128]{1,0:T(8,128)(2,1)S(1)} %broadcast_add_fusion.refs_2_.refs_0_), custom_call_target="tpu_custom_call", output_to_operand_aliasing={{}: (1, {})} | custom-call | flops 100000000 | bytes 1024 | tf_op jit(solution)/shard_map/add_lists/pallas_call | solution.py:213
  38.4 1.7 %add_lists.13.refs_1_ = f32[2048,256]{1,0:T(8,128)S(1)} custom-call(bf16[800,128]{1,0:T(8,128)(2,1)S(1)} %collective-permute-done.7.refs_0_, f32[2048,256]{1,0:T(8,128)S(1)} %add_lists.12.refs_1_), custom_call_target="tpu_custom_call", output_to_operand_aliasing={{}: (1, {})} | custom-call | flops 100000000 | bytes 1024 | tf_op jit(solution)/shard_map/add_lists/pallas_call | solution.py:213
  40.6 0.9 %add_lists.17.own_ref = bf16[1024,256]{1,0:T(8,128)(2,1)S(1)} custom-call(bf16[800,128]{1,0:T(8,128)(2,1)S(1)} %collective-permute-done.6.refs_0_, f32[2048,256]{1,0:T(8,128)S(1)} %add_lists.13.refs_1_, f32[2048,256]{1,0:T(8,128)S(1)} %add_lists.15.refs_2_), custom_call_target="tpu_custom_call" | custom-call | flops 100000000 | bytes 1024 | tf_op jit(solution)/shard_map/add_lists/pallas_call | solution.py:213
  41.6 0.9 %add_lists.16.own_ref = bf16[1024,256]{1,0:T(8,128)(2,1)S(1)} custom-call(bf16[800,128]{1,0:T(8,128)(2,1)S(1)} %collective-permute-done.6.refs_0_, f32[2048,256]{1,0:T(8,128)S(1)} %add_lists.13.refs_1_, f32[2048,256]{1,0:T(8,128)S(1)} %add_lists.15.refs_2_), custom_call_target="tpu_custom_call" | custom-call | flops 100000000 | bytes 1024 | tf_op jit(solution)/shard_map/add_lists/pallas_call | solution.py:213
  42.6 0.6 %collective-permute-start.10 = (bf16[1024,256]{1,0:T(8,128)(2,1)S(1)}, bf16[1024,256]{1,0:T(8,128)(2,1)S(1)}, u32[]{:S(2)}, u32[]{:S(2)}) collective-permute-start(bf16[1024,256]{1,0:T(8,128)(2,1)S(1)} %add_lists.16.own_ref), channel_id=1, source_target_pairs={{0,1},{1,0},{2,3},{3,2},{4,5},{5,4},{6,7},{7,6},{8,9},{9,8},{10,11... | collective-permute-start | bytes 1572872 | tf_op jit(solution)/shard_map/ppermute | solution.py:286
  43.5 1.7 %update.2 = (f32[4096,128]{1,0:T(8,128)}, f32[32,128]{1,0:T(8,128)S(1)}) custom-call(bf16[1024,256]{1,0:T(8,128)(2,1)S(1)} %add_lists.17.own_ref, bf16[1024,256]{1,0:T(8,128)(2,1)S(1)} %collective-permute-done.11.other_ref, f32[4096,128]{1,0:T(8,128)S(1)} %copy-done, f32[32,128]{1,0:T(8,128)S(1)} %bitcast.29), custom_call_target="tpu_custom_call" | custom-call | tf_op jit(solution)/shard_map/update/pallas_call | solution.py:261
  45.2 2.3 %update.3 = (f32[4096,128]{1,0:T(8,128)}, f32[32,128]{1,0:T(8,128)}) custom-call(bf16[1024,256]{1,0:T(8,128)(2,1)S(1)} %add_lists.16.own_ref, bf16[1024,256]{1,0:T(8,128)(2,1)S(1)} %collective-permute-done.10.other_ref, f32[4096,128]{1,0:T(8,128)S(1)} %copy-done, f32[32,128]{1,0:T(8,128)S(1)} %get-tuple-element.10.accum_ref, ...), custom_call_target="tpu_custom_call", output_to_operand_aliasing={{0}: (4, {})} | custom-call | tf_op jit(solution)/shard_map/update/pallas_call | solution.py:261
  (34 shorter events, 1.8 us)
Async XLA Ops:
  0.6 0.7 %copy-start.5 = (s32[2048,1]{0,1:T(1,128)S(1)}, s32[2048,1]{0,1:T(1,128)}, u32[]{:S(2)}) copy-start(s32[2048,1]{0,1:T(1,128)} %param.8) | copy-start | bytes 24580
  1.3 0.9 %copy-start.1 = (bf16[128,8,128]{2,1,0:T(8,128)(2,1)S(1)}, bf16[128,8,128]{2,1,0:T(8,128)(2,1)}, u32[]{:S(2)}) copy-start(bf16[128,8,128]{2,1,0:T(8,128)(2,1)} %param.6) | copy-start | bytes 786436
  1.3 1.0 %copy-start.3 = (s32[2048]{0:T(1024)S(1)}, s32[2048]{0:T(1024)}, u32[]{:S(2)}) copy-start(s32[2048]{0:T(1024)} %param.9) | copy-start | bytes 24580
  1.3 1.0 %copy-start.4 = (f32[2048]{0:T(1024)S(1)}, f32[2048]{0:T(1024)}, u32[]{:S(2)}) copy-start(f32[2048]{0:T(1024)} %param.7) | copy-start | bytes 24580
  3.8 1.5 %collective-permute-start = (bf16[1,400,128]{2,1,0:T(8,128)(2,1)S(1)}, bf16[1,400,128]{2,1,0:T(8,128)(2,1)S(1)}, u32[]{:S(2)}, u32[]{:S(2)}) collective-permute-start(bf16[1,400,128]{2,1,0:T(8,128)(2,1)S(1)} %get-tuple-element.9), channel_id=1, source_target_pairs={{0,1},{1,0},{2,3},{3,2},{4,5},{5,4},{6,7},{7,6},{8,9},{9,8},{10,11... | collective-permute-start | bytes 307208 | tf_op jit(solution)/shard_map/ppermute | solution.py:286
  7.4 17.2 %collective-permute-start.3 = (bf16[800,128]{1,0:T(8,128)(2,1)S(1)}, bf16[800,128]{1,0:T(8,128)(2,1)S(1)}, u32[]{:S(2)}, u32[]{:S(2)}) collective-permute-start(bf16[800,128]{1,0:T(8,128)(2,1)S(1)} %pad_maximum_fusion.refs_0_), channel_id=1, source_target_pairs={{0,24},{1,29},{2,26},{3,31},{4,28},{5,25},{6,30},{7,27},{8,16},{9,... | collective-permute-start | bytes 614408 | tf_op jit(solution)/shard_map/ppermute | solution.py:286
  12.4 1.9 %collective-permute-start.1 = (bf16[2,400,128]{2,1,0:T(8,128)(2,1)S(1)}, bf16[2,400,128]{2,1,0:T(8,128)(2,1)S(1)}, u32[]{:S(2)}, u32[]{:S(2)}) collective-permute-start(bf16[2,400,128]{2,1,0:T(8,128)(2,1)S(1)} %pack_next.6), channel_id=1, source_target_pairs={{0,1},{1,0},{2,3},{3,2},{4,5},{5,4},{6,7},{7,6},{8,9},{9,8},{10,11... | collective-permute-start | bytes 614408 | tf_op jit(solution)/shard_map/ppermute | solution.py:286
  15.3 6.3 %collective-permute-start.4 = (bf16[400,128]{1,0:T(8,128)(2,1)S(1)}, bf16[400,128]{1,0:T(8,128)(2,1)S(1)}, u32[]{:S(2)}, u32[]{:S(2)}) collective-permute-start(bf16[400,128]{1,0:T(8,128)(2,1)S(1)} %get-tuple-element.19), channel_id=1, source_target_pairs={{0,4},{1,5},{2,6},{3,7},{4,0},{5,1},{6,2},{7,3},{8,12},{9,13},{10,... | collective-permute-start | bytes 307208 | tf_op jit(solution)/shard_map/ppermute | solution.py:286
  16.5 14.3 %collective-permute-start.2 = (bf16[800,128]{1,0:T(8,128)(2,1)S(1)}, bf16[800,128]{1,0:T(8,128)(2,1)S(1)}, u32[]{:S(2)}, u32[]{:S(2)}) collective-permute-start(bf16[800,128]{1,0:T(8,128)(2,1)S(1)} %pad_maximum_fusion.1), channel_id=1, source_target_pairs={{0,16},{1,21},{2,18},{3,23},{4,20},{5,17},{6,22},{7,19},{8,24},{9,... | collective-permute-start | bytes 614408 | tf_op jit(solution)/shard_map/ppermute | solution.py:286
  16.6 10.0 %collective-permute-start.5 = (bf16[800,128]{1,0:T(8,128)(2,1)S(1)}, bf16[800,128]{1,0:T(8,128)(2,1)S(1)}, u32[]{:S(2)}, u32[]{:S(2)}) collective-permute-start(bf16[800,128]{1,0:T(8,128)(2,1)S(1)} %pad_maximum_fusion.3), channel_id=1, source_target_pairs={{0,8},{1,13},{2,10},{3,15},{4,12},{5,9},{6,14},{7,11},{8,0},{9,5},... | collective-permute-start | bytes 614408 | tf_op jit(solution)/shard_map/ppermute | solution.py:286
  21.6 13.9 %collective-permute-start.9 = (bf16[800,128]{1,0:T(8,128)(2,1)S(1)}, bf16[800,128]{1,0:T(8,128)(2,1)S(1)}, u32[]{:S(2)}, u32[]{:S(2)}) collective-permute-start(bf16[800,128]{1,0:T(8,128)(2,1)S(1)} %pad_maximum_fusion.2.refs_0_), channel_id=1, source_target_pairs={{0,2},{1,3},{2,0},{3,1},{4,6},{5,7},{6,4},{7,5},{8,10},{9,11},{10,... | collective-permute-start | bytes 614408 | tf_op jit(solution)/shard_map/ppermute | solution.py:286
  24.6 12.3 %collective-permute-start.8 = (bf16[800,128]{1,0:T(8,128)(2,1)S(1)}, bf16[800,128]{1,0:T(8,128)(2,1)S(1)}, u32[]{:S(2)}, u32[]{:S(2)}) collective-permute-start(bf16[800,128]{1,0:T(8,128)(2,1)S(1)} %broadcast_add_fusion.2.refs_0_), channel_id=1, source_target_pairs={{0,2},{1,3},{2,0},{3,1},{4,6},{5,7},{6,4},{7,5},{8,10},{9,11},{10,... | collective-permute-start | bytes 614408 | tf_op jit(solution)/shard_map/ppermute | solution.py:286
  28.1 10.3 %collective-permute-start.7 = (bf16[800,128]{1,0:T(8,128)(2,1)S(1)}, bf16[800,128]{1,0:T(8,128)(2,1)S(1)}, u32[]{:S(2)}, u32[]{:S(2)}) collective-permute-start(bf16[800,128]{1,0:T(8,128)(2,1)S(1)} %broadcast_add_fusion.1.refs_2_.refs_1_.refs_0_), channel_id=1, source_target_pairs={{0,2},{1,3},{2,0},{3,1},{4,6},{5,7},{6,4},{7,5},{8,10},{9,11},{10,... | collective-permute-start | bytes 614408 | tf_op jit(solution)/shard_map/ppermute | solution.py:286
  30.8 9.8 %collective-permute-start.6 = (bf16[800,128]{1,0:T(8,128)(2,1)S(1)}, bf16[800,128]{1,0:T(8,128)(2,1)S(1)}, u32[]{:S(2)}, u32[]{:S(2)}) collective-permute-start(bf16[800,128]{1,0:T(8,128)(2,1)S(1)} %broadcast_add_fusion.refs_2_.refs_0_), channel_id=1, source_target_pairs={{0,2},{1,3},{2,0},{3,1},{4,6},{5,7},{6,4},{7,5},{8,10},{9,11},{10,... | collective-permute-start | bytes 614408 | tf_op jit(solution)/shard_map/ppermute | solution.py:286
  41.5 2.0 %copy-start = (f32[4096,128]{1,0:T(8,128)S(1)}, f32[4096,128]{1,0:T(8,128)}, u32[]{:S(2)}) copy-start(f32[4096,128]{1,0:T(8,128)} %weight_ref.3) | copy-start | bytes 6291460
  41.5 2.0 %copy-start.2 = (f32[4096]{0:T(1024)S(1)}, f32[4096]{0:T(1024)}, u32[]{:S(2)}) copy-start(f32[4096]{0:T(1024)} %param.11) | copy-start | bytes 49156
  41.5 2.0 %collective-permute-start.11 = (bf16[1024,256]{1,0:T(8,128)(2,1)S(1)}, bf16[1024,256]{1,0:T(8,128)(2,1)S(1)}, u32[]{:S(2)}, u32[]{:S(2)}) collective-permute-start(bf16[1024,256]{1,0:T(8,128)(2,1)S(1)} %add_lists.17.own_ref), channel_id=1, source_target_pairs={{0,1},{1,0},{2,3},{3,2},{4,5},{5,4},{6,7},{7,6},{8,9},{9,8},{10,11... | collective-permute-start | bytes 1572872 | tf_op jit(solution)/shard_map/ppermute | solution.py:286
  42.6 2.7 %collective-permute-start.10 = (bf16[1024,256]{1,0:T(8,128)(2,1)S(1)}, bf16[1024,256]{1,0:T(8,128)(2,1)S(1)}, u32[]{:S(2)}, u32[]{:S(2)}) collective-permute-start(bf16[1024,256]{1,0:T(8,128)(2,1)S(1)} %add_lists.16.own_ref), channel_id=1, source_target_pairs={{0,1},{1,0},{2,3},{3,2},{4,5},{5,4},{6,7},{7,6},{8,9},{9,8},{10,11... | collective-permute-start | bytes 1572872 | tf_op jit(solution)/shard_map/ppermute | solution.py:286

commit v6 on v5

--- a/solution.py
+++ b/solution.py
@@ -224,7 +224,7 @@
 
 
 def update_kernel(first, own_ref, other_ref, weight_ref, accum_ref, *refs):
-    new_weight_hbm, new_accum_ref, out_ref, sems = refs[-4:]
+    new_weight_hbm, new_accum_hbm, out_ref, new_accum_ref, sems = refs[-5:]
     blocks = accum_ref.shape[0]
     span = own_ref.shape[0] // LANES
     lane = iota((LANES, LANES), 1)
@@ -251,6 +251,8 @@
             new_weight_hbm.at[base * LANES:(base + span) * LANES], sems.at[side]))
         copies[-1].start()
     new_accum_ref[...] = new.T[:blocks]
+    copies.append(pltpu.make_async_copy(new_accum_ref, new_accum_hbm, sems.at[2]))
+    copies[-1].start()
     for copy in copies:
         copy.wait()
 
@@ -262,8 +264,9 @@
         functools.partial(update_kernel, piece),
         out_shape=[jax.ShapeDtypeStruct(weight.shape, f32), jax.ShapeDtypeStruct(accum.shape, f32)],
         in_specs=[vmem] * 4 + [hbm] * len(more),
-        out_specs=[hbm, vmem],
-        scratch_shapes=[pltpu.VMEM((2 * own.shape[0], LANES), f32), pltpu.SemaphoreType.DMA((2,))],
+        out_specs=[hbm, pl.BlockSpec(memory_space=pl.ANY)],
+        scratch_shapes=[pltpu.VMEM((2 * own.shape[0], LANES), f32), pltpu.VMEM(accum.shape, f32),
+                        pltpu.SemaphoreType.DMA((3,))],
         input_output_aliases={4: 0} if more else {},
         compiler_params=pltpu.CompilerParams(vmem_limit_bytes=VMEM_LIMIT),
         name="update",

time: 47.9 us -> 47.4 us (0.990)
  Pallas kernels: 21.9 us -> 21.3 us
    pallas_call x2, Pallas kernels: 4.03 us -> 3.44 us  [update(): pl.pallas_call(functools.partial(update_kernel, piece), out_shape=[jax.Sh...]
where the time goes in v6:
time: 47.4 us; the launch traced here: 47.1 us
  Pallas kernels  21.3 us (45%)
  starting transfers between devices  14.3 us (30%)
  waiting for transfers between devices  8.96 us (19%)
  local copies, waits for them, and re-layouts  1.41 us (3%)
  between operations  1.03 us (2%)
    ppermute x12, starting transfers between devices, permute(): return lax.ppermute(value, axes, pairs)  14.3 us
    pallas_call x9, Pallas kernels, add_lists(): pl.pallas_call(functools.partial(add_kernel, capacity, n, before is None,...  12.4 us
    ppermute x12, waiting for transfers between devices, permute(): return lax.ppermute(value, axes, pairs)  8.96 us
    pallas_call x4, Pallas kernels, pack_next(): pl.pallas_call(functools.partial(next_kernel, groups, capacity, wanted),...  3.72 us
    pallas_call x2, Pallas kernels, update(): pl.pallas_call(functools.partial(update_kernel, piece), out_shape=[jax.Sh...  3.44 us
    pallas_call x1, Pallas kernels, pack_first(): pl.pallas_call(functools.partial(first_kernel, groups, capacity, wanted),...  1.52 us
    unnamed x12, local copies, waits for them, and re-layouts  1.36 us
  transfers between devices with their start and end apart: 12, of which 7 were waited for; matrix products, arithmetic and copies ran while one was open for 0% of the time, Pallas kernels for 31%

profile of v6, /device:TPU:0, one launch (start us, length us, event | category | flops | bytes accessed | tf_op | source)
XLA Modules:
  0.0 47.1 jit_solution(2805908348929296632)
XLA Ops:
  0.6 0.7 %copy-done.5 = s32[2048,1]{0,1:T(1,128)S(1)} copy-done((s32[2048,1]{0,1:T(1,128)S(1)}, s32[2048,1]{0,1:T(1,128)}, u32[]{:S(2)}) %copy-start.5) | copy-done | bytes 8216
  1.6 0.6 %copy-done.1 = bf16[128,8,128]{2,1,0:T(8,128)(2,1)S(1)} copy-done((bf16[128,8,128]{2,1,0:T(8,128)(2,1)S(1)}, bf16[128,8,128]{2,1,0:T(8,128)(2,1)}, u32[]{:S(2)}) %copy-start.1) | copy-done | bytes 262168
  2.3 1.5 %pack_first.1 = (bf16[1,400,128]{2,1,0:T(8,128)(2,1)S(1)}, bf16[2048,256]{1,0:T(8,128)(2,1)S(1)}) custom-call(f32[16,128]{1,0:T(8,128)S(1)} %find_slots.1.slot_ref, s32[16,128]{1,0:T(8,128)S(1)} %bitcast.30, f32[16,128]{1,0:T(8,128)S(1)} %bitcast.31, bf16[1024,128]{1,0:T(8,128)(2,1)S(1)} %bitcast.28), custom_call_target="tpu_custom_call" | custom-call | tf_op jit(solution)/shard_map/pack_first/pallas_call | solution.py:145
  3.8 0.5 %collective-permute-start = (bf16[1,400,128]{2,1,0:T(8,128)(2,1)S(1)}, bf16[1,400,128]{2,1,0:T(8,128)(2,1)S(1)}, u32[]{:S(2)}, u32[]{:S(2)}) collective-permute-start(bf16[1,400,128]{2,1,0:T(8,128)(2,1)S(1)} %get-tuple-element.9), channel_id=1, source_target_pairs={{0,1},{1,0},{2,3},{3,2},{4,5},{5,4},{6,7},{7,6},{8,9},{9,8},{10,11... | collective-permute-start | bytes 307208 | tf_op jit(solution)/shard_map/ppermute | solution.py:289
  4.3 0.6 %pack_next.4 = bf16[1,400,128]{2,1,0:T(8,128)(2,1)S(1)} custom-call(f32[16,128]{1,0:T(8,128)S(1)} %find_slots.1.slot_ref, bf16[2048,256]{1,0:T(8,128)(2,1)S(1)} %get-tuple-element.8.ext_ref), custom_call_target="tpu_custom_call" | custom-call | flops 1024 | bytes 1024 | tf_op jit(solution)/shard_map/pack_next/pallas_call | solution.py:157
  5.3 1.0 %pack_next.6 = bf16[2,400,128]{2,1,0:T(8,128)(2,1)S(1)} custom-call(f32[16,128]{1,0:T(8,128)S(1)} %find_slots.1.slot_ref, bf16[2048,256]{1,0:T(8,128)(2,1)S(1)} %get-tuple-element.8.ext_ref, bf16[800,128]{1,0:T(8,128)(2,1)S(1)} %pad_maximum_fusion.refs_0_), custom_call_target="tpu_custom_call" | custom-call | flops 1024 | bytes 1024 | tf_op jit(solution)/shard_map/pack_next/pallas_call | solution.py:157
  6.3 1.0 %pack_next.5 = bf16[2,400,128]{2,1,0:T(8,128)(2,1)S(1)} custom-call(f32[16,128]{1,0:T(8,128)S(1)} %find_slots.1.slot_ref, bf16[2048,256]{1,0:T(8,128)(2,1)S(1)} %get-tuple-element.8.ext_ref, bf16[800,128]{1,0:T(8,128)(2,1)S(1)} %pad_maximum_fusion.refs_0_), custom_call_target="tpu_custom_call" | custom-call | flops 1024 | bytes 1024 | tf_op jit(solution)/shard_map/pack_next/pallas_call | solution.py:157
  7.4 5.0 %collective-permute-start.3 = (bf16[800,128]{1,0:T(8,128)(2,1)S(1)}, bf16[800,128]{1,0:T(8,128)(2,1)S(1)}, u32[]{:S(2)}, u32[]{:S(2)}) collective-permute-start(bf16[800,128]{1,0:T(8,128)(2,1)S(1)} %pad_maximum_fusion.refs_0_), channel_id=1, source_target_pairs={{0,24},{1,29},{2,26},{3,31},{4,28},{5,25},{6,30},{7,27},{8,16},{9,... | collective-permute-start | bytes 614408 | tf_op jit(solution)/shard_map/ppermute | solution.py:289
  12.4 0.8 %collective-permute-start.1 = (bf16[2,400,128]{2,1,0:T(8,128)(2,1)S(1)}, bf16[2,400,128]{2,1,0:T(8,128)(2,1)S(1)}, u32[]{:S(2)}, u32[]{:S(2)}) collective-permute-start(bf16[2,400,128]{2,1,0:T(8,128)(2,1)S(1)} %pack_next.6), channel_id=1, source_target_pairs={{0,1},{1,0},{2,3},{3,2},{4,5},{5,4},{6,7},{7,6},{8,9},{9,8},{10,11... | collective-permute-start | bytes 614408 | tf_op jit(solution)/shard_map/ppermute | solution.py:289
  13.2 1.1 %collective-permute-done.1.refs_0_ = bf16[2,400,128]{2,1,0:T(8,128)(2,1)S(1)} collective-permute-done((bf16[2,400,128]{2,1,0:T(8,128)(2,1)S(1)}, bf16[2,400,128]{2,1,0:T(8,128)(2,1)S(1)}, u32[]{:S(2)}, u32[]{:S(2)}) %collective-permute-start.1) | collective-permute-done | bytes 204832 | tf_op jit(solution)/shard_map/ppermute | solution.py:289
  14.2 1.0 %pack_next.7 = bf16[2,400,128]{2,1,0:T(8,128)(2,1)S(1)} custom-call(f32[16,128]{1,0:T(8,128)S(1)} %find_slots.1.slot_ref, bf16[2048,256]{1,0:T(8,128)(2,1)S(1)} %get-tuple-element.8.ext_ref, bf16[2,400,128]{2,1,0:T(8,128)(2,1)S(1)} %collective-permute-done.1.refs_0_), custom_call_target="tpu_custom_call" | custom-call | flops 1024 | bytes 1024 | tf_op jit(solution)/shard_map/pack_next/pallas_call | solution.py:157
  15.3 1.1 %collective-permute-start.4 = (bf16[400,128]{1,0:T(8,128)(2,1)S(1)}, bf16[400,128]{1,0:T(8,128)(2,1)S(1)}, u32[]{:S(2)}, u32[]{:S(2)}) collective-permute-start(bf16[400,128]{1,0:T(8,128)(2,1)S(1)} %get-tuple-element.19), channel_id=1, source_target_pairs={{0,4},{1,5},{2,6},{3,7},{4,0},{5,1},{6,2},{7,3},{8,12},{9,13},{10,... | collective-permute-start | bytes 307208 | tf_op jit(solution)/shard_map/ppermute | solution.py:289
  16.6 0.8 %collective-permute-start.5 = (bf16[800,128]{1,0:T(8,128)(2,1)S(1)}, bf16[800,128]{1,0:T(8,128)(2,1)S(1)}, u32[]{:S(2)}, u32[]{:S(2)}) collective-permute-start(bf16[800,128]{1,0:T(8,128)(2,1)S(1)} %pad_maximum_fusion.3), channel_id=1, source_target_pairs={{0,8},{1,13},{2,10},{3,15},{4,12},{5,9},{6,14},{7,11},{8,0},{9,5},... | collective-permute-start | bytes 614408 | tf_op jit(solution)/shard_map/ppermute | solution.py:289
  17.4 4.2 %collective-permute-done.4 = bf16[400,128]{1,0:T(8,128)(2,1)S(1)} collective-permute-done((bf16[400,128]{1,0:T(8,128)(2,1)S(1)}, bf16[400,128]{1,0:T(8,128)(2,1)S(1)}, u32[]{:S(2)}, u32[]{:S(2)}) %collective-permute-start.4) | collective-permute-done | bytes 102432 | tf_op jit(solution)/shard_map/ppermute | solution.py:289
  21.6 1.6 %collective-permute-start.9 = (bf16[800,128]{1,0:T(8,128)(2,1)S(1)}, bf16[800,128]{1,0:T(8,128)(2,1)S(1)}, u32[]{:S(2)}, u32[]{:S(2)}) collective-permute-start(bf16[800,128]{1,0:T(8,128)(2,1)S(1)} %pad_maximum_fusion.2.refs_0_), channel_id=1, source_target_pairs={{0,2},{1,3},{2,0},{3,1},{4,6},{5,7},{6,4},{7,5},{8,10},{9,11},{10,... | collective-permute-start | bytes 614408 | tf_op jit(solution)/shard_map/ppermute | solution.py:289
  23.2 1.3 %add_lists.9.refs_1_ = f32[2048,256]{1,0:T(8,128)S(1)} custom-call(bf16[800,128]{1,0:T(8,128)(2,1)S(1)} %pad_maximum_fusion.2.refs_0_), custom_call_target="tpu_custom_call" | custom-call | flops 100000000 | bytes 1024 | tf_op jit(solution)/shard_map/add_lists/pallas_call | solution.py:213
  24.6 0.5 %collective-permute-start.8 = (bf16[800,128]{1,0:T(8,128)(2,1)S(1)}, bf16[800,128]{1,0:T(8,128)(2,1)S(1)}, u32[]{:S(2)}, u32[]{:S(2)}) collective-permute-start(bf16[800,128]{1,0:T(8,128)(2,1)S(1)} %broadcast_add_fusion.2.refs_0_), channel_id=1, source_target_pairs={{0,2},{1,3},{2,0},{3,1},{4,6},{5,7},{6,4},{7,5},{8,10},{9,11},{10,... | collective-permute-start | bytes 614408 | tf_op jit(solution)/shard_map/ppermute | solution.py:289
  25.1 1.4 %collective-permute-done.5 = bf16[800,128]{1,0:T(8,128)(2,1)S(1)} collective-permute-done((bf16[800,128]{1,0:T(8,128)(2,1)S(1)}, bf16[800,128]{1,0:T(8,128)(2,1)S(1)}, u32[]{:S(2)}, u32[]{:S(2)}) %collective-permute-start.5) | collective-permute-done | bytes 204832 | tf_op jit(solution)/shard_map/ppermute | solution.py:289
  26.6 1.5 %add_lists.10.refs_1_ = f32[2048,256]{1,0:T(8,128)S(1)} custom-call(bf16[800,128]{1,0:T(8,128)(2,1)S(1)} %broadcast_add_fusion.2.refs_0_, f32[2048,256]{1,0:T(8,128)S(1)} %add_lists.9.refs_1_, bf16[800,128]{1,0:T(8,128)(2,1)S(1)} %broadcast_add_fusion.1.refs_2_.refs_1_.refs_0_), custom_call_target="tpu_custom_call", output_to_operand_aliasing={{}: (1, {})} | custom-call | flops 100000000 | bytes 1024 | tf_op jit(solution)/shard_map/add_lists/pallas_call | solution.py:213
  28.1 1.6 %collective-permute-start.7 = (bf16[800,128]{1,0:T(8,128)(2,1)S(1)}, bf16[800,128]{1,0:T(8,128)(2,1)S(1)}, u32[]{:S(2)}, u32[]{:S(2)}) collective-permute-start(bf16[800,128]{1,0:T(8,128)(2,1)S(1)} %broadcast_add_fusion.1.refs_2_.refs_1_.refs_0_), channel_id=1, source_target_pairs={{0,2},{1,3},{2,0},{3,1},{4,6},{5,7},{6,4},{7,5},{8,10},{9,11},{10,... | collective-permute-start | bytes 614408 | tf_op jit(solution)/shard_map/ppermute | solution.py:289
  29.7 1.1 %collective-permute-done.2 = bf16[800,128]{1,0:T(8,128)(2,1)S(1)} collective-permute-done((bf16[800,128]{1,0:T(8,128)(2,1)S(1)}, bf16[800,128]{1,0:T(8,128)(2,1)S(1)}, u32[]{:S(2)}, u32[]{:S(2)}) %collective-permute-start.2) | collective-permute-done | bytes 204832 | tf_op jit(solution)/shard_map/ppermute | solution.py:289
  30.8 1.6 %collective-permute-start.6 = (bf16[800,128]{1,0:T(8,128)(2,1)S(1)}, bf16[800,128]{1,0:T(8,128)(2,1)S(1)}, u32[]{:S(2)}, u32[]{:S(2)}) collective-permute-start(bf16[800,128]{1,0:T(8,128)(2,1)S(1)} %broadcast_add_fusion.refs_2_.refs_0_), channel_id=1, source_target_pairs={{0,2},{1,3},{2,0},{3,1},{4,6},{5,7},{6,4},{7,5},{8,10},{9,11},{10,... | collective-permute-start | bytes 614408 | tf_op jit(solution)/shard_map/ppermute | solution.py:289
  32.4 1.5 %add_lists.14.refs_1_ = f32[2048,256]{1,0:T(8,128)S(1)} custom-call(bf16[800,128]{1,0:T(8,128)(2,1)S(1)} %broadcast_add_fusion.1.refs_2_.refs_1_.refs_0_, f32[2048,256]{1,0:T(8,128)S(1)} %add_lists.10.refs_1_, bf16[800,128]{1,0:T(8,128)(2,1)S(1)} %broadcast_add_fusion.refs_2_.refs_0_), custom_call_target="tpu_custom_call", output_to_operand_aliasing={{}: (1, {})} | custom-call | flops 100000000 | bytes 1024 | tf_op jit(solution)/shard_map/add_lists/pallas_call | solution.py:213
  34.0 1.5 %add_lists.15.refs_2_ = f32[2048,256]{1,0:T(8,128)S(1)} custom-call(bf16[800,128]{1,0:T(8,128)(2,1)S(1)} %broadcast_add_fusion.refs_2_.refs_0_, f32[2048,256]{1,0:T(8,128)S(1)} %add_lists.14.refs_1_), custom_call_target="tpu_custom_call", output_to_operand_aliasing={{}: (1, {})} | custom-call | flops 100000000 | bytes 1024 | tf_op jit(solution)/shard_map/add_lists/pallas_call | solution.py:213
  35.5 1.3 %add_lists.11.refs_1_ = f32[2048,256]{1,0:T(8,128)S(1)} custom-call(bf16[800,128]{1,0:T(8,128)(2,1)S(1)} %collective-permute-done.9.refs_0_, bf16[800,128]{1,0:T(8,128)(2,1)S(1)} %broadcast_add_fusion.1.refs_2_.refs_1_.refs_0_), custom_call_target="tpu_custom_call" | custom-call | flops 100000000 | bytes 1024 | tf_op jit(solution)/shard_map/add_lists/pallas_call | solution.py:213
  36.8 1.5 %add_lists.12.refs_1_ = f32[2048,256]{1,0:T(8,128)S(1)} custom-call(bf16[800,128]{1,0:T(8,128)(2,1)S(1)} %collective-permute-done.8.refs_0_, f32[2048,256]{1,0:T(8,128)S(1)} %add_lists.11.refs_1_, bf16[800,128]{1,0:T(8,128)(2,1)S(1)} %broadcast_add_fusion.refs_2_.refs_0_), custom_call_target="tpu_custom_call", output_to_operand_aliasing={{}: (1, {})} | custom-call | flops 100000000 | bytes 1024 | tf_op jit(solution)/shard_map/add_lists/pallas_call | solution.py:213
  38.4 1.7 %add_lists.13.refs_1_ = f32[2048,256]{1,0:T(8,128)S(1)} custom-call(bf16[800,128]{1,0:T(8,128)(2,1)S(1)} %collective-permute-done.7.refs_0_, f32[2048,256]{1,0:T(8,128)S(1)} %add_lists.12.refs_1_), custom_call_target="tpu_custom_call", output_to_operand_aliasing={{}: (1, {})} | custom-call | flops 100000000 | bytes 1024 | tf_op jit(solution)/shard_map/add_lists/pallas_call | solution.py:213
  40.6 0.9 %add_lists.17.own_ref = bf16[1024,256]{1,0:T(8,128)(2,1)S(1)} custom-call(bf16[800,128]{1,0:T(8,128)(2,1)S(1)} %collective-permute-done.6.refs_0_, f32[2048,256]{1,0:T(8,128)S(1)} %add_lists.13.refs_1_, f32[2048,256]{1,0:T(8,128)S(1)} %add_lists.15.refs_2_), custom_call_target="tpu_custom_call" | custom-call | flops 100000000 | bytes 1024 | tf_op jit(solution)/shard_map/add_lists/pallas_call | solution.py:213
  41.6 0.9 %add_lists.16.own_ref = bf16[1024,256]{1,0:T(8,128)(2,1)S(1)} custom-call(bf16[800,128]{1,0:T(8,128)(2,1)S(1)} %collective-permute-done.6.refs_0_, f32[2048,256]{1,0:T(8,128)S(1)} %add_lists.13.refs_1_, f32[2048,256]{1,0:T(8,128)S(1)} %add_lists.15.refs_2_), custom_call_target="tpu_custom_call" | custom-call | flops 100000000 | bytes 1024 | tf_op jit(solution)/shard_map/add_lists/pallas_call | solution.py:213
  42.6 0.6 %collective-permute-start.10 = (bf16[1024,256]{1,0:T(8,128)(2,1)S(1)}, bf16[1024,256]{1,0:T(8,128)(2,1)S(1)}, u32[]{:S(2)}, u32[]{:S(2)}) collective-permute-start(bf16[1024,256]{1,0:T(8,128)(2,1)S(1)} %add_lists.16.own_ref), channel_id=1, source_target_pairs={{0,1},{1,0},{2,3},{3,2},{4,5},{5,4},{6,7},{7,6},{8,9},{9,8},{10,11... | collective-permute-start | bytes 1572872 | tf_op jit(solution)/shard_map/ppermute | solution.py:289
  43.5 1.7 %update.2 = (f32[4096,128]{1,0:T(8,128)}, f32[32,128]{1,0:T(8,128)S(1)}) custom-call(bf16[1024,256]{1,0:T(8,128)(2,1)S(1)} %add_lists.17.own_ref, bf16[1024,256]{1,0:T(8,128)(2,1)S(1)} %collective-permute-done.11.other_ref, f32[4096,128]{1,0:T(8,128)S(1)} %copy-done, f32[32,128]{1,0:T(8,128)S(1)} %bitcast.29), custom_call_target="tpu_custom_call" | custom-call | tf_op jit(solution)/shard_map/update/pallas_call | solution.py:263
  45.3 1.7 %update.3 = (f32[4096,128]{1,0:T(8,128)}, f32[32,128]{1,0:T(8,128)}) custom-call(bf16[1024,256]{1,0:T(8,128)(2,1)S(1)} %add_lists.16.own_ref, bf16[1024,256]{1,0:T(8,128)(2,1)S(1)} %collective-permute-done.10.other_ref, f32[4096,128]{1,0:T(8,128)S(1)} %copy-done, f32[32,128]{1,0:T(8,128)S(1)} %get-tuple-element.10.accum_ref, ...), custom_call_target="tpu_custom_call", output_to_operand_aliasing={{0}: (4, {})} | custom-call | tf_op jit(solution)/shard_map/update/pallas_call | solution.py:263
  (34 shorter events, 1.8 us)
Async XLA Ops:
  0.6 0.7 %copy-start.5 = (s32[2048,1]{0,1:T(1,128)S(1)}, s32[2048,1]{0,1:T(1,128)}, u32[]{:S(2)}) copy-start(s32[2048,1]{0,1:T(1,128)} %param.8) | copy-start | bytes 24580
  1.3 0.9 %copy-start.1 = (bf16[128,8,128]{2,1,0:T(8,128)(2,1)S(1)}, bf16[128,8,128]{2,1,0:T(8,128)(2,1)}, u32[]{:S(2)}) copy-start(bf16[128,8,128]{2,1,0:T(8,128)(2,1)} %param.6) | copy-start | bytes 786436
  1.3 1.0 %copy-start.3 = (s32[2048]{0:T(1024)S(1)}, s32[2048]{0:T(1024)}, u32[]{:S(2)}) copy-start(s32[2048]{0:T(1024)} %param.9) | copy-start | bytes 24580
  1.3 1.0 %copy-start.4 = (f32[2048]{0:T(1024)S(1)}, f32[2048]{0:T(1024)}, u32[]{:S(2)}) copy-start(f32[2048]{0:T(1024)} %param.7) | copy-start | bytes 24580
  3.8 1.5 %collective-permute-start = (bf16[1,400,128]{2,1,0:T(8,128)(2,1)S(1)}, bf16[1,400,128]{2,1,0:T(8,128)(2,1)S(1)}, u32[]{:S(2)}, u32[]{:S(2)}) collective-permute-start(bf16[1,400,128]{2,1,0:T(8,128)(2,1)S(1)} %get-tuple-element.9), channel_id=1, source_target_pairs={{0,1},{1,0},{2,3},{3,2},{4,5},{5,4},{6,7},{7,6},{8,9},{9,8},{10,11... | collective-permute-start | bytes 307208 | tf_op jit(solution)/shard_map/ppermute | solution.py:289
  7.4 17.2 %collective-permute-start.3 = (bf16[800,128]{1,0:T(8,128)(2,1)S(1)}, bf16[800,128]{1,0:T(8,128)(2,1)S(1)}, u32[]{:S(2)}, u32[]{:S(2)}) collective-permute-start(bf16[800,128]{1,0:T(8,128)(2,1)S(1)} %pad_maximum_fusion.refs_0_), channel_id=1, source_target_pairs={{0,24},{1,29},{2,26},{3,31},{4,28},{5,25},{6,30},{7,27},{8,16},{9,... | collective-permute-start | bytes 614408 | tf_op jit(solution)/shard_map/ppermute | solution.py:289
  12.4 1.9 %collective-permute-start.1 = (bf16[2,400,128]{2,1,0:T(8,128)(2,1)S(1)}, bf16[2,400,128]{2,1,0:T(8,128)(2,1)S(1)}, u32[]{:S(2)}, u32[]{:S(2)}) collective-permute-start(bf16[2,400,128]{2,1,0:T(8,128)(2,1)S(1)} %pack_next.6), channel_id=1, source_target_pairs={{0,1},{1,0},{2,3},{3,2},{4,5},{5,4},{6,7},{7,6},{8,9},{9,8},{10,11... | collective-permute-start | bytes 614408 | tf_op jit(solution)/shard_map/ppermute | solution.py:289
  15.3 6.3 %collective-permute-start.4 = (bf16[400,128]{1,0:T(8,128)(2,1)S(1)}, bf16[400,128]{1,0:T(8,128)(2,1)S(1)}, u32[]{:S(2)}, u32[]{:S(2)}) collective-permute-start(bf16[400,128]{1,0:T(8,128)(2,1)S(1)} %get-tuple-element.19), channel_id=1, source_target_pairs={{0,4},{1,5},{2,6},{3,7},{4,0},{5,1},{6,2},{7,3},{8,12},{9,13},{10,... | collective-permute-start | bytes 307208 | tf_op jit(solution)/shard_map/ppermute | solution.py:289
  16.5 14.3 %collective-permute-start.2 = (bf16[800,128]{1,0:T(8,128)(2,1)S(1)}, bf16[800,128]{1,0:T(8,128)(2,1)S(1)}, u32[]{:S(2)}, u32[]{:S(2)}) collective-permute-start(bf16[800,128]{1,0:T(8,128)(2,1)S(1)} %pad_maximum_fusion.1), channel_id=1, source_target_pairs={{0,16},{1,21},{2,18},{3,23},{4,20},{5,17},{6,22},{7,19},{8,24},{9,... | collective-permute-start | bytes 614408 | tf_op jit(solution)/shard_map/ppermute | solution.py:289
  16.6 10.0 %collective-permute-start.5 = (bf16[800,128]{1,0:T(8,128)(2,1)S(1)}, bf16[800,128]{1,0:T(8,128)(2,1)S(1)}, u32[]{:S(2)}, u32[]{:S(2)}) collective-permute-start(bf16[800,128]{1,0:T(8,128)(2,1)S(1)} %pad_maximum_fusion.3), channel_id=1, source_target_pairs={{0,8},{1,13},{2,10},{3,15},{4,12},{5,9},{6,14},{7,11},{8,0},{9,5},... | collective-permute-start | bytes 614408 | tf_op jit(solution)/shard_map/ppermute | solution.py:289
  21.6 13.9 %collective-permute-start.9 = (bf16[800,128]{1,0:T(8,128)(2,1)S(1)}, bf16[800,128]{1,0:T(8,128)(2,1)S(1)}, u32[]{:S(2)}, u32[]{:S(2)}) collective-permute-start(bf16[800,128]{1,0:T(8,128)(2,1)S(1)} %pad_maximum_fusion.2.refs_0_), channel_id=1, source_target_pairs={{0,2},{1,3},{2,0},{3,1},{4,6},{5,7},{6,4},{7,5},{8,10},{9,11},{10,... | collective-permute-start | bytes 614408 | tf_op jit(solution)/shard_map/ppermute | solution.py:289
  24.6 12.3 %collective-permute-start.8 = (bf16[800,128]{1,0:T(8,128)(2,1)S(1)}, bf16[800,128]{1,0:T(8,128)(2,1)S(1)}, u32[]{:S(2)}, u32[]{:S(2)}) collective-permute-start(bf16[800,128]{1,0:T(8,128)(2,1)S(1)} %broadcast_add_fusion.2.refs_0_), channel_id=1, source_target_pairs={{0,2},{1,3},{2,0},{3,1},{4,6},{5,7},{6,4},{7,5},{8,10},{9,11},{10,... | collective-permute-start | bytes 614408 | tf_op jit(solution)/shard_map/ppermute | solution.py:289
  28.1 10.3 %collective-permute-start.7 = (bf16[800,128]{1,0:T(8,128)(2,1)S(1)}, bf16[800,128]{1,0:T(8,128)(2,1)S(1)}, u32[]{:S(2)}, u32[]{:S(2)}) collective-permute-start(bf16[800,128]{1,0:T(8,128)(2,1)S(1)} %broadcast_add_fusion.1.refs_2_.refs_1_.refs_0_), channel_id=1, source_target_pairs={{0,2},{1,3},{2,0},{3,1},{4,6},{5,7},{6,4},{7,5},{8,10},{9,11},{10,... | collective-permute-start | bytes 614408 | tf_op jit(solution)/shard_map/ppermute | solution.py:289
  30.8 9.8 %collective-permute-start.6 = (bf16[800,128]{1,0:T(8,128)(2,1)S(1)}, bf16[800,128]{1,0:T(8,128)(2,1)S(1)}, u32[]{:S(2)}, u32[]{:S(2)}) collective-permute-start(bf16[800,128]{1,0:T(8,128)(2,1)S(1)} %broadcast_add_fusion.refs_2_.refs_0_), channel_id=1, source_target_pairs={{0,2},{1,3},{2,0},{3,1},{4,6},{5,7},{6,4},{7,5},{8,10},{9,11},{10,... | collective-permute-start | bytes 614408 | tf_op jit(solution)/shard_map/ppermute | solution.py:289
  41.5 2.0 %copy-start = (f32[4096,128]{1,0:T(8,128)S(1)}, f32[4096,128]{1,0:T(8,128)}, u32[]{:S(2)}) copy-start(f32[4096,128]{1,0:T(8,128)} %weight_ref.3) | copy-start | bytes 6291460
  41.5 2.0 %copy-start.2 = (f32[4096]{0:T(1024)S(1)}, f32[4096]{0:T(1024)}, u32[]{:S(2)}) copy-start(f32[4096]{0:T(1024)} %param.11) | copy-start | bytes 49156
  41.5 2.0 %collective-permute-start.11 = (bf16[1024,256]{1,0:T(8,128)(2,1)S(1)}, bf16[1024,256]{1,0:T(8,128)(2,1)S(1)}, u32[]{:S(2)}, u32[]{:S(2)}) collective-permute-start(bf16[1024,256]{1,0:T(8,128)(2,1)S(1)} %add_lists.17.own_ref), channel_id=1, source_target_pairs={{0,1},{1,0},{2,3},{3,2},{4,5},{5,4},{6,7},{7,6},{8,9},{9,8},{10,11... | collective-permute-start | bytes 1572872 | tf_op jit(solution)/shard_map/ppermute | solution.py:289
  42.6 2.7 %collective-permute-start.10 = (bf16[1024,256]{1,0:T(8,128)(2,1)S(1)}, bf16[1024,256]{1,0:T(8,128)(2,1)S(1)}, u32[]{:S(2)}, u32[]{:S(2)}) collective-permute-start(bf16[1024,256]{1,0:T(8,128)(2,1)S(1)} %add_lists.16.own_ref), channel_id=1, source_target_pairs={{0,1},{1,0},{2,3},{3,2},{4,5},{5,4},{6,7},{7,6},{8,9},{9,8},{10,11... | collective-permute-start | bytes 1572872 | tf_op jit(solution)/shard_map/ppermute | solution.py:289

commit v7 on v6

--- a/solution.py
+++ b/solution.py
@@ -165,9 +165,9 @@
     )(slot, ext, *after)
 
 
-def add_kernel(capacity, lists, first, last, total, start, *refs):
+def add_kernel(capacity, lists, first, last, total, start, built, *refs):
     in_refs, refs = refs[:lists], list(refs[lists:])
-    out_ref, rhs_ref = refs[-2:]
+    out_ref, rhs_ref = (refs[-1], refs[-2]) if built else refs[-2:]
     before = None if first else refs.pop(0)
     beside = refs.pop(0) if last else None
     half = total
@@ -183,6 +183,8 @@
             high = high - upper * float(half // 256)
             highs += [high[k:k + 1] for k in range(chunks)]
             lows += [digits[chunks + k:chunks + k + 1] for k in range(chunks)]
+            if built:
+                continue
             turned = jnp.concatenate([upper, jnp.zeros((LANES - chunks, LANES), f32)], axis=0).T
             for k in range(chunks):
                 rows = ref[base + k * LANES:base + (k + 1) * LANES, :].astype(f32)
@@ -205,22 +207,26 @@
         out_ref[n * 256:(n + 1) * 256, :] = part.astype(out_ref.dtype)
 
 
-def add_lists(lists, before, beside, half, capacity, piece=0, pieces=1, after=()):
+def add_lists(lists, before, beside, half, capacity, piece=0, pieces=1, after=(), rhs=None):
     vmem = pl.BlockSpec(memory_space=pltpu.VMEM)
     n = len(lists)
     depth = sum(value.shape[0] for value in lists) // (capacity + PAD) * capacity
     more = [value for value in (before, beside) if value is not None]
-    return pl.pallas_call(
-        functools.partial(add_kernel, capacity, n, before is None, beside is not None, half, piece * (half // pieces // 256)),
-        out_shape=jax.ShapeDtypeStruct((half // pieces, 2 * LANES), f32 if beside is None else bf16),
-        in_specs=[vmem] * (n + len(more)) + [pl.BlockSpec(memory_space=pl.ANY)] * len(after),
-        out_specs=vmem,
-        scratch_shapes=[pltpu.VMEM((depth, 2 * LANES), bf16)],
+    out = jax.ShapeDtypeStruct((half // pieces, 2 * LANES), f32 if beside is None else bf16)
+    product = jax.ShapeDtypeStruct((depth, 2 * LANES), bf16)
+    results = pl.pallas_call(
+        functools.partial(add_kernel, capacity, n, before is None, beside is not None, half, piece * (half // pieces // 256),
+                          rhs is not None),
+        out_shape=[out] if rhs is not None else [out, product] if beside is not None else [out],
+        in_specs=[vmem] * (n + len(more)) + [pl.BlockSpec(memory_space=pl.ANY)] * len(after) + [vmem] * (rhs is not None),
+        out_specs=[vmem, vmem] if rhs is None and beside is not None else [vmem],
+        scratch_shapes=[pltpu.VMEM(product.shape, bf16)] if beside is None else [],
         input_output_aliases={n: 0} if beside is None and before is not None else {},
         compiler_params=pltpu.CompilerParams(vmem_limit_bytes=VMEM_LIMIT),
         cost_estimate=MEDIUM,
         name="add_lists",
-    )(*lists, *more, *after)
+    )(*lists, *more, *after, *([] if rhs is None else [rhs]))
+    return results if beside is not None and rhs is None else results[0]
 
 
 def update_kernel(first, own_ref, other_ref, weight_ref, accum_ref, *refs):
@@ -231,6 +237,7 @@
     old = jnp.concatenate([accum_ref[...], jnp.zeros((LANES - blocks, LANES), f32)], axis=0).T
     new = old
     copies = []
+    group = 4
     for side in range(2):
         base = side * (blocks // 2) + first * span
 
@@ -246,12 +253,14 @@
             b = base + n
             out_ref[(side * span + n) * LANES:(side * span + n + 1) * LANES, :] = (
                 weight_ref[b * LANES:(b + 1) * LANES, :] - grad(n) * scale[:, b:b + 1])
-        copies.append(pltpu.make_async_copy(
-            out_ref.at[side * span * LANES:(side + 1) * span * LANES],
-            new_weight_hbm.at[base * LANES:(base + span) * LANES], sems.at[side]))
-        copies[-1].start()
+            if (n + 1) % group == 0:
+                m = n + 1 - group
+                copies.append(pltpu.make_async_copy(
+                    out_ref.at[(side * span + m) * LANES:(side * span + n + 1) * LANES],
+                    new_weight_hbm.at[(base + m) * LANES:(b + 1) * LANES], sems.at[len(copies)]))
+                copies[-1].start()
     new_accum_ref[...] = new.T[:blocks]
-    copies.append(pltpu.make_async_copy(new_accum_ref, new_accum_hbm, sems.at[2]))
+    copies.append(pltpu.make_async_copy(new_accum_ref, new_accum_hbm, sems.at[len(copies)]))
     copies[-1].start()
     for copy in copies:
         copy.wait()
@@ -266,7 +275,7 @@
         in_specs=[vmem] * 4 + [hbm] * len(more),
         out_specs=[hbm, pl.BlockSpec(memory_space=pl.ANY)],
         scratch_shapes=[pltpu.VMEM((2 * own.shape[0], LANES), f32), pltpu.VMEM(accum.shape, f32),
-                        pltpu.SemaphoreType.DMA((3,))],
+                        pltpu.SemaphoreType.DMA((5,))],
         input_output_aliases={4: 0} if more else {},
         compiler_params=pltpu.CompilerParams(vmem_limit_bytes=VMEM_LIMIT),
         name="update",
@@ -334,7 +343,8 @@
     there = there_last
 
     pieces = 2
-    sums = [add_lists([there], copy, own, half, capacity, n, pieces) for n in range(pieces)]
+    total, rhs = add_lists([there], copy, own, half, capacity, 0, pieces)
+    sums = [total] + [add_lists([there], copy, own, half, capacity, n, pieces, rhs=rhs) for n in range(1, pieces)]
     others = [to_core(value) for value in sums]
     new_weight, new_accum = None, accum.reshape(-1, LANES)
     for n in range(pieces):

time: 47.4 us -> 47.2 us (level)
  no operation moved by 1% of the time
where the time goes in v7:
time: 47.2 us; the launch traced here: 47 us
  Pallas kernels  20.9 us (44%)
  starting transfers between devices  14.2 us (30%)
  waiting for transfers between devices  9.3 us (20%)
  local copies, waits for them, and re-layouts  1.41 us (3%)
  between operations  1.03 us (2%)
    ppermute x12, starting transfers between devices, permute(): return lax.ppermute(value, axes, pairs)  14.2 us
    pallas_call x9, Pallas kernels, add_lists(): pl.pallas_call(functools.partial(add_kernel, capacity, n, before is None,...  12 us
    ppermute x12, waiting for transfers between devices, permute(): return lax.ppermute(value, axes, pairs)  9.3 us
    pallas_call x4, Pallas kernels, pack_next(): pl.pallas_call(functools.partial(next_kernel, groups, capacity, wanted),...  3.72 us
    pallas_call x2, Pallas kernels, update(): pl.pallas_call(functools.partial(update_kernel, piece), out_shape=[jax.Sh...  3.32 us
    pallas_call x1, Pallas kernels, pack_first(): pl.pallas_call(functools.partial(first_kernel, groups, capacity, wanted),...  1.52 us
    unnamed x12, local copies, waits for them, and re-layouts  1.36 us
  transfers between devices with their start and end apart: 12, of which 7 were waited for; matrix products, arithmetic and copies ran while one was open for 0% of the time, Pallas kernels for 31%

profile of v7, /device:TPU:0, one launch (start us, length us, event | category | flops | bytes accessed | tf_op | source)
XLA Modules:
  0.0 47.0 jit_solution(12715045010783541429)
XLA Ops:
  0.6 0.7 %copy-done.5 = s32[2048,1]{0,1:T(1,128)S(1)} copy-done((s32[2048,1]{0,1:T(1,128)S(1)}, s32[2048,1]{0,1:T(1,128)}, u32[]{:S(2)}) %copy-start.5) | copy-done | bytes 8216
  1.6 0.6 %copy-done.1 = bf16[128,8,128]{2,1,0:T(8,128)(2,1)S(1)} copy-done((bf16[128,8,128]{2,1,0:T(8,128)(2,1)S(1)}, bf16[128,8,128]{2,1,0:T(8,128)(2,1)}, u32[]{:S(2)}) %copy-start.1) | copy-done | bytes 262168
  2.3 1.5 %pack_first.1 = (bf16[1,400,128]{2,1,0:T(8,128)(2,1)S(1)}, bf16[2048,256]{1,0:T(8,128)(2,1)S(1)}) custom-call(f32[16,128]{1,0:T(8,128)S(1)} %find_slots.1.slot_ref, s32[16,128]{1,0:T(8,128)S(1)} %bitcast.30, f32[16,128]{1,0:T(8,128)S(1)} %bitcast.31, bf16[1024,128]{1,0:T(8,128)(2,1)S(1)} %bitcast.28), custom_call_target="tpu_custom_call" | custom-call | tf_op jit(solution)/shard_map/pack_first/pallas_call | solution.py:145
  4.3 0.6 %pack_next.4 = bf16[1,400,128]{2,1,0:T(8,128)(2,1)S(1)} custom-call(f32[16,128]{1,0:T(8,128)S(1)} %find_slots.1.slot_ref, bf16[2048,256]{1,0:T(8,128)(2,1)S(1)} %get-tuple-element.10.ext_ref), custom_call_target="tpu_custom_call" | custom-call | flops 1024 | bytes 1024 | tf_op jit(solution)/shard_map/pack_next/pallas_call | solution.py:157
  5.3 1.0 %pack_next.6 = bf16[2,400,128]{2,1,0:T(8,128)(2,1)S(1)} custom-call(f32[16,128]{1,0:T(8,128)S(1)} %find_slots.1.slot_ref, bf16[2048,256]{1,0:T(8,128)(2,1)S(1)} %get-tuple-element.10.ext_ref, bf16[800,128]{1,0:T(8,128)(2,1)S(1)} %pad_maximum_fusion.refs_0_), custom_call_target="tpu_custom_call" | custom-call | flops 1024 | bytes 1024 | tf_op jit(solution)/shard_map/pack_next/pallas_call | solution.py:157
  6.3 1.0 %pack_next.5 = bf16[2,400,128]{2,1,0:T(8,128)(2,1)S(1)} custom-call(f32[16,128]{1,0:T(8,128)S(1)} %find_slots.1.slot_ref, bf16[2048,256]{1,0:T(8,128)(2,1)S(1)} %get-tuple-element.10.ext_ref, bf16[800,128]{1,0:T(8,128)(2,1)S(1)} %pad_maximum_fusion.refs_0_), custom_call_target="tpu_custom_call" | custom-call | flops 1024 | bytes 1024 | tf_op jit(solution)/shard_map/pack_next/pallas_call | solution.py:157
  7.4 5.0 %collective-permute-start.3 = (bf16[800,128]{1,0:T(8,128)(2,1)S(1)}, bf16[800,128]{1,0:T(8,128)(2,1)S(1)}, u32[]{:S(2)}, u32[]{:S(2)}) collective-permute-start(bf16[800,128]{1,0:T(8,128)(2,1)S(1)} %pad_maximum_fusion.refs_0_), channel_id=1, source_target_pairs={{0,24},{1,29},{2,26},{3,31},{4,28},{5,25},{6,30},{7,27},{8,16},{9,... | collective-permute-start | bytes 614408 | tf_op jit(solution)/shard_map/ppermute | solution.py:298
  12.4 0.8 %collective-permute-start.1 = (bf16[2,400,128]{2,1,0:T(8,128)(2,1)S(1)}, bf16[2,400,128]{2,1,0:T(8,128)(2,1)S(1)}, u32[]{:S(2)}, u32[]{:S(2)}) collective-permute-start(bf16[2,400,128]{2,1,0:T(8,128)(2,1)S(1)} %pack_next.6), channel_id=1, source_target_pairs={{0,1},{1,0},{2,3},{3,2},{4,5},{5,4},{6,7},{7,6},{8,9},{9,8},{10,11... | collective-permute-start | bytes 614408 | tf_op jit(solution)/shard_map/ppermute | solution.py:298
  13.2 1.1 %collective-permute-done.1.refs_0_ = bf16[2,400,128]{2,1,0:T(8,128)(2,1)S(1)} collective-permute-done((bf16[2,400,128]{2,1,0:T(8,128)(2,1)S(1)}, bf16[2,400,128]{2,1,0:T(8,128)(2,1)S(1)}, u32[]{:S(2)}, u32[]{:S(2)}) %collective-permute-start.1) | collective-permute-done | bytes 204832 | tf_op jit(solution)/shard_map/ppermute | solution.py:298
  14.2 1.0 %pack_next.7 = bf16[2,400,128]{2,1,0:T(8,128)(2,1)S(1)} custom-call(f32[16,128]{1,0:T(8,128)S(1)} %find_slots.1.slot_ref, bf16[2048,256]{1,0:T(8,128)(2,1)S(1)} %get-tuple-element.10.ext_ref, bf16[2,400,128]{2,1,0:T(8,128)(2,1)S(1)} %collective-permute-done.1.refs_0_), custom_call_target="tpu_custom_call" | custom-call | flops 1024 | bytes 1024 | tf_op jit(solution)/shard_map/pack_next/pallas_call | solution.py:157
  15.3 1.1 %collective-permute-start.4 = (bf16[400,128]{1,0:T(8,128)(2,1)S(1)}, bf16[400,128]{1,0:T(8,128)(2,1)S(1)}, u32[]{:S(2)}, u32[]{:S(2)}) collective-permute-start(bf16[400,128]{1,0:T(8,128)(2,1)S(1)} %get-tuple-element.23), channel_id=1, source_target_pairs={{0,4},{1,5},{2,6},{3,7},{4,0},{5,1},{6,2},{7,3},{8,12},{9,13},{10,... | collective-permute-start | bytes 307208 | tf_op jit(solution)/shard_map/ppermute | solution.py:298
  16.6 0.8 %collective-permute-start.5 = (bf16[800,128]{1,0:T(8,128)(2,1)S(1)}, bf16[800,128]{1,0:T(8,128)(2,1)S(1)}, u32[]{:S(2)}, u32[]{:S(2)}) collective-permute-start(bf16[800,128]{1,0:T(8,128)(2,1)S(1)} %pad_maximum_fusion.3), channel_id=1, source_target_pairs={{0,8},{1,13},{2,10},{3,15},{4,12},{5,9},{6,14},{7,11},{8,0},{9,5},... | collective-permute-start | bytes 614408 | tf_op jit(solution)/shard_map/ppermute | solution.py:298
  17.4 4.2 %collective-permute-done.4 = bf16[400,128]{1,0:T(8,128)(2,1)S(1)} collective-permute-done((bf16[400,128]{1,0:T(8,128)(2,1)S(1)}, bf16[400,128]{1,0:T(8,128)(2,1)S(1)}, u32[]{:S(2)}, u32[]{:S(2)}) %collective-permute-start.4) | collective-permute-done | bytes 102432 | tf_op jit(solution)/shard_map/ppermute | solution.py:298
  21.6 1.6 %collective-permute-start.9 = (bf16[800,128]{1,0:T(8,128)(2,1)S(1)}, bf16[800,128]{1,0:T(8,128)(2,1)S(1)}, u32[]{:S(2)}, u32[]{:S(2)}) collective-permute-start(bf16[800,128]{1,0:T(8,128)(2,1)S(1)} %pad_maximum_fusion.2.refs_0_), channel_id=1, source_target_pairs={{0,2},{1,3},{2,0},{3,1},{4,6},{5,7},{6,4},{7,5},{8,10},{9,11},{10,... | collective-permute-start | bytes 614408 | tf_op jit(solution)/shard_map/ppermute | solution.py:298
  23.2 1.3 %add_lists.9.refs_1_ = f32[2048,256]{1,0:T(8,128)S(1)} custom-call(bf16[800,128]{1,0:T(8,128)(2,1)S(1)} %pad_maximum_fusion.2.refs_0_), custom_call_target="tpu_custom_call" | custom-call | flops 100000000 | bytes 1024 | tf_op jit(solution)/shard_map/add_lists/pallas_call | solution.py:217
  24.6 0.5 %collective-permute-start.8 = (bf16[800,128]{1,0:T(8,128)(2,1)S(1)}, bf16[800,128]{1,0:T(8,128)(2,1)S(1)}, u32[]{:S(2)}, u32[]{:S(2)}) collective-permute-start(bf16[800,128]{1,0:T(8,128)(2,1)S(1)} %broadcast_add_fusion.2.refs_0_), channel_id=1, source_target_pairs={{0,2},{1,3},{2,0},{3,1},{4,6},{5,7},{6,4},{7,5},{8,10},{9,11},{10,... | collective-permute-start | bytes 614408 | tf_op jit(solution)/shard_map/ppermute | solution.py:298
  25.1 1.4 %collective-permute-done.5 = bf16[800,128]{1,0:T(8,128)(2,1)S(1)} collective-permute-done((bf16[800,128]{1,0:T(8,128)(2,1)S(1)}, bf16[800,128]{1,0:T(8,128)(2,1)S(1)}, u32[]{:S(2)}, u32[]{:S(2)}) %collective-permute-start.5) | collective-permute-done | bytes 204832 | tf_op jit(solution)/shard_map/ppermute | solution.py:298
  26.6 1.5 %add_lists.10.refs_1_ = f32[2048,256]{1,0:T(8,128)S(1)} custom-call(bf16[800,128]{1,0:T(8,128)(2,1)S(1)} %broadcast_add_fusion.2.refs_0_, f32[2048,256]{1,0:T(8,128)S(1)} %add_lists.9.refs_1_, bf16[800,128]{1,0:T(8,128)(2,1)S(1)} %broadcast_add_fusion.1.refs_2_.refs_1_.refs_0_), custom_call_target="tpu_custom_call", output_to_operand_aliasing={{}: (1, {})} | custom-call | flops 100000000 | bytes 1024 | tf_op jit(solution)/shard_map/add_lists/pallas_call | solution.py:217
  28.1 1.6 %collective-permute-start.7 = (bf16[800,128]{1,0:T(8,128)(2,1)S(1)}, bf16[800,128]{1,0:T(8,128)(2,1)S(1)}, u32[]{:S(2)}, u32[]{:S(2)}) collective-permute-start(bf16[800,128]{1,0:T(8,128)(2,1)S(1)} %broadcast_add_fusion.1.refs_2_.refs_1_.refs_0_), channel_id=1, source_target_pairs={{0,2},{1,3},{2,0},{3,1},{4,6},{5,7},{6,4},{7,5},{8,10},{9,11},{10,... | collective-permute-start | bytes 614408 | tf_op jit(solution)/shard_map/ppermute | solution.py:298
  29.7 1.1 %collective-permute-done.2 = bf16[800,128]{1,0:T(8,128)(2,1)S(1)} collective-permute-done((bf16[800,128]{1,0:T(8,128)(2,1)S(1)}, bf16[800,128]{1,0:T(8,128)(2,1)S(1)}, u32[]{:S(2)}, u32[]{:S(2)}) %collective-permute-start.2) | collective-permute-done | bytes 204832 | tf_op jit(solution)/shard_map/ppermute | solution.py:298
  30.8 1.6 %collective-permute-start.6 = (bf16[800,128]{1,0:T(8,128)(2,1)S(1)}, bf16[800,128]{1,0:T(8,128)(2,1)S(1)}, u32[]{:S(2)}, u32[]{:S(2)}) collective-permute-start(bf16[800,128]{1,0:T(8,128)(2,1)S(1)} %broadcast_add_fusion.refs_2_.refs_0_), channel_id=1, source_target_pairs={{0,2},{1,3},{2,0},{3,1},{4,6},{5,7},{6,4},{7,5},{8,10},{9,11},{10,... | collective-permute-start | bytes 614408 | tf_op jit(solution)/shard_map/ppermute | solution.py:298
  32.4 1.5 %add_lists.14.refs_1_ = f32[2048,256]{1,0:T(8,128)S(1)} custom-call(bf16[800,128]{1,0:T(8,128)(2,1)S(1)} %broadcast_add_fusion.1.refs_2_.refs_1_.refs_0_, f32[2048,256]{1,0:T(8,128)S(1)} %add_lists.10.refs_1_, bf16[800,128]{1,0:T(8,128)(2,1)S(1)} %broadcast_add_fusion.refs_2_.refs_0_), custom_call_target="tpu_custom_call", output_to_operand_aliasing={{}: (1, {})} | custom-call | flops 100000000 | bytes 1024 | tf_op jit(solution)/shard_map/add_lists/pallas_call | solution.py:217
  34.0 1.5 %add_lists.15.refs_2_ = f32[2048,256]{1,0:T(8,128)S(1)} custom-call(bf16[800,128]{1,0:T(8,128)(2,1)S(1)} %broadcast_add_fusion.refs_2_.refs_0_, f32[2048,256]{1,0:T(8,128)S(1)} %add_lists.14.refs_1_), custom_call_target="tpu_custom_call", output_to_operand_aliasing={{}: (1, {})} | custom-call | flops 100000000 | bytes 1024 | tf_op jit(solution)/shard_map/add_lists/pallas_call | solution.py:217
  35.5 1.3 %add_lists.11.refs_1_ = f32[2048,256]{1,0:T(8,128)S(1)} custom-call(bf16[800,128]{1,0:T(8,128)(2,1)S(1)} %collective-permute-done.9.refs_0_, bf16[800,128]{1,0:T(8,128)(2,1)S(1)} %broadcast_add_fusion.1.refs_2_.refs_1_.refs_0_), custom_call_target="tpu_custom_call" | custom-call | flops 100000000 | bytes 1024 | tf_op jit(solution)/shard_map/add_lists/pallas_call | solution.py:217
  36.8 1.5 %add_lists.12.refs_1_ = f32[2048,256]{1,0:T(8,128)S(1)} custom-call(bf16[800,128]{1,0:T(8,128)(2,1)S(1)} %collective-permute-done.8.refs_0_, f32[2048,256]{1,0:T(8,128)S(1)} %add_lists.11.refs_1_, bf16[800,128]{1,0:T(8,128)(2,1)S(1)} %broadcast_add_fusion.refs_2_.refs_0_), custom_call_target="tpu_custom_call", output_to_operand_aliasing={{}: (1, {})} | custom-call | flops 100000000 | bytes 1024 | tf_op jit(solution)/shard_map/add_lists/pallas_call | solution.py:217
  38.4 1.7 %add_lists.13.refs_1_ = f32[2048,256]{1,0:T(8,128)S(1)} custom-call(bf16[800,128]{1,0:T(8,128)(2,1)S(1)} %collective-permute-done.7.refs_0_, f32[2048,256]{1,0:T(8,128)S(1)} %add_lists.12.refs_1_), custom_call_target="tpu_custom_call", output_to_operand_aliasing={{}: (1, {})} | custom-call | flops 100000000 | bytes 1024 | tf_op jit(solution)/shard_map/add_lists/pallas_call | solution.py:217
  40.6 0.9 %add_lists.16 = (bf16[1024,256]{1,0:T(8,128)(2,1)S(1)}, bf16[768,256]{1,0:T(8,128)(2,1)S(1)}) custom-call(bf16[800,128]{1,0:T(8,128)(2,1)S(1)} %collective-permute-done.6.refs_0_, f32[2048,256]{1,0:T(8,128)S(1)} %add_lists.13.refs_1_, f32[2048,256]{1,0:T(8,128)S(1)} %add_lists.15.refs_2_), custom_call_target="tpu_custom_call" | custom-call | flops 100000000 | bytes 1024 | tf_op jit(solution)/shard_map/add_lists/pallas_call | solution.py:217
  41.6 0.6 %add_lists.17.own_ref = bf16[1024,256]{1,0:T(8,128)(2,1)S(1)} custom-call(bf16[800,128]{1,0:T(8,128)(2,1)S(1)} %collective-permute-done.6.refs_0_, f32[2048,256]{1,0:T(8,128)S(1)} %add_lists.13.refs_1_, f32[2048,256]{1,0:T(8,128)S(1)} %add_lists.15.refs_2_, bf16[768,256]{1,0:T(8,128)(2,1)S(1)} %get-tuple-element.12.refs_3_), custom_call_target="tpu_custom_call" | custom-call | flops 100000000 | bytes 1024 | tf_op jit(solution)/shard_map/add_lists/pallas_call | solution.py:217
  42.2 0.5 %collective-permute-start.10 = (bf16[1024,256]{1,0:T(8,128)(2,1)S(1)}, bf16[1024,256]{1,0:T(8,128)(2,1)S(1)}, u32[]{:S(2)}, u32[]{:S(2)}) collective-permute-start(bf16[1024,256]{1,0:T(8,128)(2,1)S(1)} %add_lists.17.own_ref), channel_id=1, source_target_pairs={{0,1},{1,0},{2,3},{3,2},{4,5},{5,4},{6,7},{7,6},{8,9},{9,8},{10,11... | collective-permute-start | bytes 1572872 | tf_op jit(solution)/shard_map/ppermute | solution.py:298
  42.7 0.7 %collective-permute-done.11.other_ref = bf16[1024,256]{1,0:T(8,128)(2,1)S(1)} collective-permute-done((bf16[1024,256]{1,0:T(8,128)(2,1)S(1)}, bf16[1024,256]{1,0:T(8,128)(2,1)S(1)}, u32[]{:S(2)}, u32[]{:S(2)}) %collective-permute-start.11) | collective-permute-done | bytes 524320 | tf_op jit(solution)/shard_map/ppermute | solution.py:298
  43.5 1.7 %update.2 = (f32[4096,128]{1,0:T(8,128)}, f32[32,128]{1,0:T(8,128)S(1)}) custom-call(bf16[1024,256]{1,0:T(8,128)(2,1)S(1)} %get-tuple-element.13.own_ref, bf16[1024,256]{1,0:T(8,128)(2,1)S(1)} %collective-permute-done.11.other_ref, f32[4096,128]{1,0:T(8,128)S(1)} %copy-done, f32[32,128]{1,0:T(8,128)S(1)} %bitcast.29), custom_call_target="tpu_custom_call" | custom-call | tf_op jit(solution)/shard_map/update/pallas_call | solution.py:272
  45.2 1.7 %update.3 = (f32[4096,128]{1,0:T(8,128)}, f32[32,128]{1,0:T(8,128)}) custom-call(bf16[1024,256]{1,0:T(8,128)(2,1)S(1)} %add_lists.17.own_ref, bf16[1024,256]{1,0:T(8,128)(2,1)S(1)} %collective-permute-done.10.other_ref, f32[4096,128]{1,0:T(8,128)S(1)} %copy-done, f32[32,128]{1,0:T(8,128)S(1)} %get-tuple-element.14.accum_ref, ...), custom_call_target="tpu_custom_call", output_to_operand_aliasing={{0}: (4, {})} | custom-call | tf_op jit(solution)/shard_map/update/pallas_call | solution.py:272
  (34 shorter events, 1.9 us)
Async XLA Ops:
  0.6 0.7 %copy-start.5 = (s32[2048,1]{0,1:T(1,128)S(1)}, s32[2048,1]{0,1:T(1,128)}, u32[]{:S(2)}) copy-start(s32[2048,1]{0,1:T(1,128)} %param.8) | copy-start | bytes 24580
  1.3 0.9 %copy-start.1 = (bf16[128,8,128]{2,1,0:T(8,128)(2,1)S(1)}, bf16[128,8,128]{2,1,0:T(8,128)(2,1)}, u32[]{:S(2)}) copy-start(bf16[128,8,128]{2,1,0:T(8,128)(2,1)} %param.6) | copy-start | bytes 786436
  1.3 1.0 %copy-start.3 = (s32[2048]{0:T(1024)S(1)}, s32[2048]{0:T(1024)}, u32[]{:S(2)}) copy-start(s32[2048]{0:T(1024)} %param.9) | copy-start | bytes 24580
  1.3 1.0 %copy-start.4 = (f32[2048]{0:T(1024)S(1)}, f32[2048]{0:T(1024)}, u32[]{:S(2)}) copy-start(f32[2048]{0:T(1024)} %param.7) | copy-start | bytes 24580
  3.8 1.5 %collective-permute-start = (bf16[1,400,128]{2,1,0:T(8,128)(2,1)S(1)}, bf16[1,400,128]{2,1,0:T(8,128)(2,1)S(1)}, u32[]{:S(2)}, u32[]{:S(2)}) collective-permute-start(bf16[1,400,128]{2,1,0:T(8,128)(2,1)S(1)} %get-tuple-element.11), channel_id=1, source_target_pairs={{0,1},{1,0},{2,3},{3,2},{4,5},{5,4},{6,7},{7,6},{8,9},{9,8},{10,11... | collective-permute-start | bytes 307208 | tf_op jit(solution)/shard_map/ppermute | solution.py:298
  7.4 17.2 %collective-permute-start.3 = (bf16[800,128]{1,0:T(8,128)(2,1)S(1)}, bf16[800,128]{1,0:T(8,128)(2,1)S(1)}, u32[]{:S(2)}, u32[]{:S(2)}) collective-permute-start(bf16[800,128]{1,0:T(8,128)(2,1)S(1)} %pad_maximum_fusion.refs_0_), channel_id=1, source_target_pairs={{0,24},{1,29},{2,26},{3,31},{4,28},{5,25},{6,30},{7,27},{8,16},{9,... | collective-permute-start | bytes 614408 | tf_op jit(solution)/shard_map/ppermute | solution.py:298
  12.4 1.9 %collective-permute-start.1 = (bf16[2,400,128]{2,1,0:T(8,128)(2,1)S(1)}, bf16[2,400,128]{2,1,0:T(8,128)(2,1)S(1)}, u32[]{:S(2)}, u32[]{:S(2)}) collective-permute-start(bf16[2,400,128]{2,1,0:T(8,128)(2,1)S(1)} %pack_next.6), channel_id=1, source_target_pairs={{0,1},{1,0},{2,3},{3,2},{4,5},{5,4},{6,7},{7,6},{8,9},{9,8},{10,11... | collective-permute-start | bytes 614408 | tf_op jit(solution)/shard_map/ppermute | solution.py:298
  15.3 6.3 %collective-permute-start.4 = (bf16[400,128]{1,0:T(8,128)(2,1)S(1)}, bf16[400,128]{1,0:T(8,128)(2,1)S(1)}, u32[]{:S(2)}, u32[]{:S(2)}) collective-permute-start(bf16[400,128]{1,0:T(8,128)(2,1)S(1)} %get-tuple-element.23), channel_id=1, source_target_pairs={{0,4},{1,5},{2,6},{3,7},{4,0},{5,1},{6,2},{7,3},{8,12},{9,13},{10,... | collective-permute-start | bytes 307208 | tf_op jit(solution)/shard_map/ppermute | solution.py:298
  16.5 14.3 %collective-permute-start.2 = (bf16[800,128]{1,0:T(8,128)(2,1)S(1)}, bf16[800,128]{1,0:T(8,128)(2,1)S(1)}, u32[]{:S(2)}, u32[]{:S(2)}) collective-permute-start(bf16[800,128]{1,0:T(8,128)(2,1)S(1)} %pad_maximum_fusion.1), channel_id=1, source_target_pairs={{0,16},{1,21},{2,18},{3,23},{4,20},{5,17},{6,22},{7,19},{8,24},{9,... | collective-permute-start | bytes 614408 | tf_op jit(solution)/shard_map/ppermute | solution.py:298
  16.6 10.0 %collective-permute-start.5 = (bf16[800,128]{1,0:T(8,128)(2,1)S(1)}, bf16[800,128]{1,0:T(8,128)(2,1)S(1)}, u32[]{:S(2)}, u32[]{:S(2)}) collective-permute-start(bf16[800,128]{1,0:T(8,128)(2,1)S(1)} %pad_maximum_fusion.3), channel_id=1, source_target_pairs={{0,8},{1,13},{2,10},{3,15},{4,12},{5,9},{6,14},{7,11},{8,0},{9,5},... | collective-permute-start | bytes 614408 | tf_op jit(solution)/shard_map/ppermute | solution.py:298
  21.6 13.9 %collective-permute-start.9 = (bf16[800,128]{1,0:T(8,128)(2,1)S(1)}, bf16[800,128]{1,0:T(8,128)(2,1)S(1)}, u32[]{:S(2)}, u32[]{:S(2)}) collective-permute-start(bf16[800,128]{1,0:T(8,128)(2,1)S(1)} %pad_maximum_fusion.2.refs_0_), channel_id=1, source_target_pairs={{0,2},{1,3},{2,0},{3,1},{4,6},{5,7},{6,4},{7,5},{8,10},{9,11},{10,... | collective-permute-start | bytes 614408 | tf_op jit(solution)/shard_map/ppermute | solution.py:298
  24.6 12.3 %collective-permute-start.8 = (bf16[800,128]{1,0:T(8,128)(2,1)S(1)}, bf16[800,128]{1,0:T(8,128)(2,1)S(1)}, u32[]{:S(2)}, u32[]{:S(2)}) collective-permute-start(bf16[800,128]{1,0:T(8,128)(2,1)S(1)} %broadcast_add_fusion.2.refs_0_), channel_id=1, source_target_pairs={{0,2},{1,3},{2,0},{3,1},{4,6},{5,7},{6,4},{7,5},{8,10},{9,11},{10,... | collective-permute-start | bytes 614408 | tf_op jit(solution)/shard_map/ppermute | solution.py:298
  28.1 10.3 %collective-permute-start.7 = (bf16[800,128]{1,0:T(8,128)(2,1)S(1)}, bf16[800,128]{1,0:T(8,128)(2,1)S(1)}, u32[]{:S(2)}, u32[]{:S(2)}) collective-permute-start(bf16[800,128]{1,0:T(8,128)(2,1)S(1)} %broadcast_add_fusion.1.refs_2_.refs_1_.refs_0_), channel_id=1, source_target_pairs={{0,2},{1,3},{2,0},{3,1},{4,6},{5,7},{6,4},{7,5},{8,10},{9,11},{10,... | collective-permute-start | bytes 614408 | tf_op jit(solution)/shard_map/ppermute | solution.py:298
  30.8 9.8 %collective-permute-start.6 = (bf16[800,128]{1,0:T(8,128)(2,1)S(1)}, bf16[800,128]{1,0:T(8,128)(2,1)S(1)}, u32[]{:S(2)}, u32[]{:S(2)}) collective-permute-start(bf16[800,128]{1,0:T(8,128)(2,1)S(1)} %broadcast_add_fusion.refs_2_.refs_0_), channel_id=1, source_target_pairs={{0,2},{1,3},{2,0},{3,1},{4,6},{5,7},{6,4},{7,5},{8,10},{9,11},{10,... | collective-permute-start | bytes 614408 | tf_op jit(solution)/shard_map/ppermute | solution.py:298
  41.5 2.0 %collective-permute-start.11 = (bf16[1024,256]{1,0:T(8,128)(2,1)S(1)}, bf16[1024,256]{1,0:T(8,128)(2,1)S(1)}, u32[]{:S(2)}, u32[]{:S(2)}) collective-permute-start(bf16[1024,256]{1,0:T(8,128)(2,1)S(1)} %get-tuple-element.13.own_ref), channel_id=1, source_target_pairs={{0,1},{1,0},{2,3},{3,2},{4,5},{5,4},{6,7},{7,6},{8,9},{9,8},{10,11... | collective-permute-start | bytes 1572872 | tf_op jit(solution)/shard_map/ppermute | solution.py:298
  41.6 1.9 %copy-start = (f32[4096,128]{1,0:T(8,128)S(1)}, f32[4096,128]{1,0:T(8,128)}, u32[]{:S(2)}) copy-start(f32[4096,128]{1,0:T(8,128)} %weight_ref.3) | copy-start | bytes 6291460
  41.6 1.9 %copy-start.2 = (f32[4096]{0:T(1024)S(1)}, f32[4096]{0:T(1024)}, u32[]{:S(2)}) copy-start(f32[4096]{0:T(1024)} %param.11) | copy-start | bytes 49156
  42.2 2.9 %collective-permute-start.10 = (bf16[1024,256]{1,0:T(8,128)(2,1)S(1)}, bf16[1024,256]{1,0:T(8,128)(2,1)S(1)}, u32[]{:S(2)}, u32[]{:S(2)}) collective-permute-start(bf16[1024,256]{1,0:T(8,128)(2,1)S(1)} %add_lists.17.own_ref), channel_id=1, source_target_pairs={{0,1},{1,0},{2,3},{3,2},{4,5},{5,4},{6,7},{7,6},{8,9},{9,8},{10,11... | collective-permute-start | bytes 1572872 | tf_op jit(solution)/shard_map/ppermute | solution.py:298

commit v8 on v7

--- a/solution.py
+++ b/solution.py
@@ -187,11 +187,11 @@
                 continue
             turned = jnp.concatenate([upper, jnp.zeros((LANES - chunks, LANES), f32)], axis=0).T
             for k in range(chunks):
-                rows = ref[base + k * LANES:base + (k + 1) * LANES, :].astype(f32)
-                above = turned[:, k:k + 1] > 0.5
+                rows = ref[base + k * LANES:base + (k + 1) * LANES, :]
+                above = rows * jnp.broadcast_to(turned[:, k:k + 1], (LANES, LANES)).astype(bf16)
                 here = slice(at, at + LANES)
-                rhs_ref[here, 0:LANES] = jnp.where(above, 0.0, rows).astype(bf16)
-                rhs_ref[here, LANES:2 * LANES] = jnp.where(above, rows, 0.0).astype(bf16)
+                rhs_ref[here, 0:LANES] = rows - above
+                rhs_ref[here, LANES:2 * LANES] = above
                 at += LANES
     place = iota((256, LANES), 0, f32)
     for n in range(out_ref.shape[0] // 256):

time: 47.2 us -> 47.3 us (level)
  Pallas kernels: 20.9 us -> 19.9 us
  waiting for transfers between devices: 9.3 us -> 10.3 us
    ppermute x12, waiting for transfers between devices: 9.3 us -> 10.3 us  [permute(): return lax.ppermute(value, axes, pairs)]
    pallas_call x9, Pallas kernels: 12 us -> 11.1 us  [add_lists(): pl.pallas_call(functools.partial(add_kernel, capacity, n, before is None,...]
  transfers between devices with their start and end apart: 12 -> 12, of which waited for: 7 -> 7; matrix products, arithmetic and copies ran while one was open for 0% -> 0% of each run, Pallas kernels for 31% -> 28%
where the time goes in v8:
time: 47.3 us; the launch traced here: 47.1 us
  Pallas kernels  19.9 us (42%)
  starting transfers between devices  14.2 us (30%)
  waiting for transfers between devices  10.3 us (22%)
  local copies, waits for them, and re-layouts  1.41 us (3%)
  between operations  1.03 us (2%)
    ppermute x12, starting transfers between devices, permute(): return lax.ppermute(value, axes, pairs)  14.2 us
    pallas_call x9, Pallas kernels, add_lists(): pl.pallas_call(functools.partial(add_kernel, capacity, n, before is None,...  11.1 us
    ppermute x12, waiting for transfers between devices, permute(): return lax.ppermute(value, axes, pairs)  10.3 us
    pallas_call x4, Pallas kernels, pack_next(): pl.pallas_call(functools.partial(next_kernel, groups, capacity, wanted),...  3.72 us
    pallas_call x2, Pallas kernels, update(): pl.pallas_call(functools.partial(update_kernel, piece), out_shape=[jax.Sh...  3.32 us
    pallas_call x1, Pallas kernels, pack_first(): pl.pallas_call(functools.partial(first_kernel, groups, capacity, wanted),...  1.52 us
    unnamed x12, local copies, waits for them, and re-layouts  1.36 us
  transfers between devices with their start and end apart: 12, of which 7 were waited for; matrix products, arithmetic and copies ran while one was open for 0% of the time, Pallas kernels for 28%

profile of v8, /device:TPU:0, one launch (start us, length us, event | category | flops | bytes accessed | tf_op | source)
XLA Modules:
  0.0 47.1 jit_solution(10939376657447955109)
XLA Ops:
  0.6 0.7 %copy-done.5 = s32[2048,1]{0,1:T(1,128)S(1)} copy-done((s32[2048,1]{0,1:T(1,128)S(1)}, s32[2048,1]{0,1:T(1,128)}, u32[]{:S(2)}) %copy-start.5) | copy-done | bytes 8216
  1.6 0.6 %copy-done.1 = bf16[128,8,128]{2,1,0:T(8,128)(2,1)S(1)} copy-done((bf16[128,8,128]{2,1,0:T(8,128)(2,1)S(1)}, bf16[128,8,128]{2,1,0:T(8,128)(2,1)}, u32[]{:S(2)}) %copy-start.1) | copy-done | bytes 262168
  2.3 1.5 %pack_first.1 = (bf16[1,400,128]{2,1,0:T(8,128)(2,1)S(1)}, bf16[2048,256]{1,0:T(8,128)(2,1)S(1)}) custom-call(f32[16,128]{1,0:T(8,128)S(1)} %find_slots.1.slot_ref, s32[16,128]{1,0:T(8,128)S(1)} %bitcast.30, f32[16,128]{1,0:T(8,128)S(1)} %bitcast.31, bf16[1024,128]{1,0:T(8,128)(2,1)S(1)} %bitcast.28), custom_call_target="tpu_custom_call" | custom-call | tf_op jit(solution)/shard_map/pack_first/pallas_call | solution.py:145
  4.3 0.6 %pack_next.4 = bf16[1,400,128]{2,1,0:T(8,128)(2,1)S(1)} custom-call(f32[16,128]{1,0:T(8,128)S(1)} %find_slots.1.slot_ref, bf16[2048,256]{1,0:T(8,128)(2,1)S(1)} %get-tuple-element.10.ext_ref), custom_call_target="tpu_custom_call" | custom-call | flops 1024 | bytes 1024 | tf_op jit(solution)/shard_map/pack_next/pallas_call | solution.py:157
  5.3 1.0 %pack_next.6 = bf16[2,400,128]{2,1,0:T(8,128)(2,1)S(1)} custom-call(f32[16,128]{1,0:T(8,128)S(1)} %find_slots.1.slot_ref, bf16[2048,256]{1,0:T(8,128)(2,1)S(1)} %get-tuple-element.10.ext_ref, bf16[800,128]{1,0:T(8,128)(2,1)S(1)} %pad_maximum_fusion.refs_0_), custom_call_target="tpu_custom_call" | custom-call | flops 1024 | bytes 1024 | tf_op jit(solution)/shard_map/pack_next/pallas_call | solution.py:157
  6.3 1.0 %pack_next.5 = bf16[2,400,128]{2,1,0:T(8,128)(2,1)S(1)} custom-call(f32[16,128]{1,0:T(8,128)S(1)} %find_slots.1.slot_ref, bf16[2048,256]{1,0:T(8,128)(2,1)S(1)} %get-tuple-element.10.ext_ref, bf16[800,128]{1,0:T(8,128)(2,1)S(1)} %pad_maximum_fusion.refs_0_), custom_call_target="tpu_custom_call" | custom-call | flops 1024 | bytes 1024 | tf_op jit(solution)/shard_map/pack_next/pallas_call | solution.py:157
  7.4 5.0 %collective-permute-start.3 = (bf16[800,128]{1,0:T(8,128)(2,1)S(1)}, bf16[800,128]{1,0:T(8,128)(2,1)S(1)}, u32[]{:S(2)}, u32[]{:S(2)}) collective-permute-start(bf16[800,128]{1,0:T(8,128)(2,1)S(1)} %pad_maximum_fusion.refs_0_), channel_id=1, source_target_pairs={{0,24},{1,29},{2,26},{3,31},{4,28},{5,25},{6,30},{7,27},{8,16},{9,... | collective-permute-start | bytes 614408 | tf_op jit(solution)/shard_map/ppermute | solution.py:298
  12.4 0.8 %collective-permute-start.1 = (bf16[2,400,128]{2,1,0:T(8,128)(2,1)S(1)}, bf16[2,400,128]{2,1,0:T(8,128)(2,1)S(1)}, u32[]{:S(2)}, u32[]{:S(2)}) collective-permute-start(bf16[2,400,128]{2,1,0:T(8,128)(2,1)S(1)} %pack_next.6), channel_id=1, source_target_pairs={{0,1},{1,0},{2,3},{3,2},{4,5},{5,4},{6,7},{7,6},{8,9},{9,8},{10,11... | collective-permute-start | bytes 614408 | tf_op jit(solution)/shard_map/ppermute | solution.py:298
  13.2 1.1 %collective-permute-done.1.refs_0_ = bf16[2,400,128]{2,1,0:T(8,128)(2,1)S(1)} collective-permute-done((bf16[2,400,128]{2,1,0:T(8,128)(2,1)S(1)}, bf16[2,400,128]{2,1,0:T(8,128)(2,1)S(1)}, u32[]{:S(2)}, u32[]{:S(2)}) %collective-permute-start.1) | collective-permute-done | bytes 204832 | tf_op jit(solution)/shard_map/ppermute | solution.py:298
  14.2 1.0 %pack_next.7 = bf16[2,400,128]{2,1,0:T(8,128)(2,1)S(1)} custom-call(f32[16,128]{1,0:T(8,128)S(1)} %find_slots.1.slot_ref, bf16[2048,256]{1,0:T(8,128)(2,1)S(1)} %get-tuple-element.10.ext_ref, bf16[2,400,128]{2,1,0:T(8,128)(2,1)S(1)} %collective-permute-done.1.refs_0_), custom_call_target="tpu_custom_call" | custom-call | flops 1024 | bytes 1024 | tf_op jit(solution)/shard_map/pack_next/pallas_call | solution.py:157
  15.3 1.1 %collective-permute-start.4 = (bf16[400,128]{1,0:T(8,128)(2,1)S(1)}, bf16[400,128]{1,0:T(8,128)(2,1)S(1)}, u32[]{:S(2)}, u32[]{:S(2)}) collective-permute-start(bf16[400,128]{1,0:T(8,128)(2,1)S(1)} %get-tuple-element.23), channel_id=1, source_target_pairs={{0,4},{1,5},{2,6},{3,7},{4,0},{5,1},{6,2},{7,3},{8,12},{9,13},{10,... | collective-permute-start | bytes 307208 | tf_op jit(solution)/shard_map/ppermute | solution.py:298
  16.6 0.8 %collective-permute-start.5 = (bf16[800,128]{1,0:T(8,128)(2,1)S(1)}, bf16[800,128]{1,0:T(8,128)(2,1)S(1)}, u32[]{:S(2)}, u32[]{:S(2)}) collective-permute-start(bf16[800,128]{1,0:T(8,128)(2,1)S(1)} %pad_maximum_fusion.3), channel_id=1, source_target_pairs={{0,8},{1,13},{2,10},{3,15},{4,12},{5,9},{6,14},{7,11},{8,0},{9,5},... | collective-permute-start | bytes 614408 | tf_op jit(solution)/shard_map/ppermute | solution.py:298
  17.4 4.2 %collective-permute-done.4 = bf16[400,128]{1,0:T(8,128)(2,1)S(1)} collective-permute-done((bf16[400,128]{1,0:T(8,128)(2,1)S(1)}, bf16[400,128]{1,0:T(8,128)(2,1)S(1)}, u32[]{:S(2)}, u32[]{:S(2)}) %collective-permute-start.4) | collective-permute-done | bytes 102432 | tf_op jit(solution)/shard_map/ppermute | solution.py:298
  21.6 1.6 %collective-permute-start.9 = (bf16[800,128]{1,0:T(8,128)(2,1)S(1)}, bf16[800,128]{1,0:T(8,128)(2,1)S(1)}, u32[]{:S(2)}, u32[]{:S(2)}) collective-permute-start(bf16[800,128]{1,0:T(8,128)(2,1)S(1)} %pad_maximum_fusion.2.refs_0_), channel_id=1, source_target_pairs={{0,2},{1,3},{2,0},{3,1},{4,6},{5,7},{6,4},{7,5},{8,10},{9,11},{10,... | collective-permute-start | bytes 614408 | tf_op jit(solution)/shard_map/ppermute | solution.py:298
  23.2 1.3 %add_lists.9.refs_1_ = f32[2048,256]{1,0:T(8,128)S(1)} custom-call(bf16[800,128]{1,0:T(8,128)(2,1)S(1)} %pad_maximum_fusion.2.refs_0_), custom_call_target="tpu_custom_call" | custom-call | flops 100000000 | bytes 1024 | tf_op jit(solution)/shard_map/add_lists/pallas_call | solution.py:217
  25.1 1.5 %collective-permute-done.5 = bf16[800,128]{1,0:T(8,128)(2,1)S(1)} collective-permute-done((bf16[800,128]{1,0:T(8,128)(2,1)S(1)}, bf16[800,128]{1,0:T(8,128)(2,1)S(1)}, u32[]{:S(2)}, u32[]{:S(2)}) %collective-permute-start.5) | collective-permute-done | bytes 204832 | tf_op jit(solution)/shard_map/ppermute | solution.py:298
  26.6 1.4 %add_lists.10.refs_1_ = f32[2048,256]{1,0:T(8,128)S(1)} custom-call(bf16[800,128]{1,0:T(8,128)(2,1)S(1)} %broadcast_add_fusion.2.refs_0_, f32[2048,256]{1,0:T(8,128)S(1)} %add_lists.9.refs_1_, bf16[800,128]{1,0:T(8,128)(2,1)S(1)} %broadcast_add_fusion.1.refs_2_.refs_1_.refs_0_), custom_call_target="tpu_custom_call", output_to_operand_aliasing={{}: (1, {})} | custom-call | flops 100000000 | bytes 1024 | tf_op jit(solution)/shard_map/add_lists/pallas_call | solution.py:217
  28.0 1.6 %collective-permute-start.7 = (bf16[800,128]{1,0:T(8,128)(2,1)S(1)}, bf16[800,128]{1,0:T(8,128)(2,1)S(1)}, u32[]{:S(2)}, u32[]{:S(2)}) collective-permute-start(bf16[800,128]{1,0:T(8,128)(2,1)S(1)} %broadcast_add_fusion.1.refs_2_.refs_1_.refs_0_), channel_id=1, source_target_pairs={{0,2},{1,3},{2,0},{3,1},{4,6},{5,7},{6,4},{7,5},{8,10},{9,11},{10,... | collective-permute-start | bytes 614408 | tf_op jit(solution)/shard_map/ppermute | solution.py:298
  29.5 1.3 %collective-permute-done.2 = bf16[800,128]{1,0:T(8,128)(2,1)S(1)} collective-permute-done((bf16[800,128]{1,0:T(8,128)(2,1)S(1)}, bf16[800,128]{1,0:T(8,128)(2,1)S(1)}, u32[]{:S(2)}, u32[]{:S(2)}) %collective-permute-start.2) | collective-permute-done | bytes 204832 | tf_op jit(solution)/shard_map/ppermute | solution.py:298
  30.8 1.6 %collective-permute-start.6 = (bf16[800,128]{1,0:T(8,128)(2,1)S(1)}, bf16[800,128]{1,0:T(8,128)(2,1)S(1)}, u32[]{:S(2)}, u32[]{:S(2)}) collective-permute-start(bf16[800,128]{1,0:T(8,128)(2,1)S(1)} %broadcast_add_fusion.refs_2_.refs_0_), channel_id=1, source_target_pairs={{0,2},{1,3},{2,0},{3,1},{4,6},{5,7},{6,4},{7,5},{8,10},{9,11},{10,... | collective-permute-start | bytes 614408 | tf_op jit(solution)/shard_map/ppermute | solution.py:298
  32.4 1.4 %add_lists.14.refs_1_ = f32[2048,256]{1,0:T(8,128)S(1)} custom-call(bf16[800,128]{1,0:T(8,128)(2,1)S(1)} %broadcast_add_fusion.1.refs_2_.refs_1_.refs_0_, f32[2048,256]{1,0:T(8,128)S(1)} %add_lists.10.refs_1_, bf16[800,128]{1,0:T(8,128)(2,1)S(1)} %broadcast_add_fusion.refs_2_.refs_0_), custom_call_target="tpu_custom_call", output_to_operand_aliasing={{}: (1, {})} | custom-call | flops 100000000 | bytes 1024 | tf_op jit(solution)/shard_map/add_lists/pallas_call | solution.py:217
  33.8 1.4 %add_lists.15.refs_2_ = f32[2048,256]{1,0:T(8,128)S(1)} custom-call(bf16[800,128]{1,0:T(8,128)(2,1)S(1)} %broadcast_add_fusion.refs_2_.refs_0_, f32[2048,256]{1,0:T(8,128)S(1)} %add_lists.14.refs_1_), custom_call_target="tpu_custom_call", output_to_operand_aliasing={{}: (1, {})} | custom-call | flops 100000000 | bytes 1024 | tf_op jit(solution)/shard_map/add_lists/pallas_call | solution.py:217
  35.2 1.3 %add_lists.11.refs_1_ = f32[2048,256]{1,0:T(8,128)S(1)} custom-call(bf16[800,128]{1,0:T(8,128)(2,1)S(1)} %collective-permute-done.9.refs_0_, bf16[800,128]{1,0:T(8,128)(2,1)S(1)} %broadcast_add_fusion.1.refs_2_.refs_1_.refs_0_), custom_call_target="tpu_custom_call" | custom-call | flops 100000000 | bytes 1024 | tf_op jit(solution)/shard_map/add_lists/pallas_call | solution.py:217
  36.5 1.4 %add_lists.12.refs_1_ = f32[2048,256]{1,0:T(8,128)S(1)} custom-call(bf16[800,128]{1,0:T(8,128)(2,1)S(1)} %collective-permute-done.8.refs_0_, f32[2048,256]{1,0:T(8,128)S(1)} %add_lists.11.refs_1_, bf16[800,128]{1,0:T(8,128)(2,1)S(1)} %broadcast_add_fusion.refs_2_.refs_0_), custom_call_target="tpu_custom_call", output_to_operand_aliasing={{}: (1, {})} | custom-call | flops 100000000 | bytes 1024 | tf_op jit(solution)/shard_map/add_lists/pallas_call | solution.py:217
  37.9 1.4 %add_lists.13.refs_1_ = f32[2048,256]{1,0:T(8,128)S(1)} custom-call(bf16[800,128]{1,0:T(8,128)(2,1)S(1)} %collective-permute-done.7.refs_0_, f32[2048,256]{1,0:T(8,128)S(1)} %add_lists.12.refs_1_), custom_call_target="tpu_custom_call", output_to_operand_aliasing={{}: (1, {})} | custom-call | flops 100000000 | bytes 1024 | tf_op jit(solution)/shard_map/add_lists/pallas_call | solution.py:217
  39.3 1.3 %collective-permute-done.6.refs_0_ = bf16[800,128]{1,0:T(8,128)(2,1)S(1)} collective-permute-done((bf16[800,128]{1,0:T(8,128)(2,1)S(1)}, bf16[800,128]{1,0:T(8,128)(2,1)S(1)}, u32[]{:S(2)}, u32[]{:S(2)}) %collective-permute-start.6) | collective-permute-done | bytes 204832 | tf_op jit(solution)/shard_map/ppermute | solution.py:298
  40.6 1.0 %add_lists.16 = (bf16[1024,256]{1,0:T(8,128)(2,1)S(1)}, bf16[768,256]{1,0:T(8,128)(2,1)S(1)}) custom-call(bf16[800,128]{1,0:T(8,128)(2,1)S(1)} %collective-permute-done.6.refs_0_, f32[2048,256]{1,0:T(8,128)S(1)} %add_lists.13.refs_1_, f32[2048,256]{1,0:T(8,128)S(1)} %add_lists.15.refs_2_), custom_call_target="tpu_custom_call" | custom-call | flops 100000000 | bytes 1024 | tf_op jit(solution)/shard_map/add_lists/pallas_call | solution.py:217
  41.7 0.6 %add_lists.17.own_ref = bf16[1024,256]{1,0:T(8,128)(2,1)S(1)} custom-call(bf16[800,128]{1,0:T(8,128)(2,1)S(1)} %collective-permute-done.6.refs_0_, f32[2048,256]{1,0:T(8,128)S(1)} %add_lists.13.refs_1_, f32[2048,256]{1,0:T(8,128)S(1)} %add_lists.15.refs_2_, bf16[768,256]{1,0:T(8,128)(2,1)S(1)} %get-tuple-element.12.refs_3_), custom_call_target="tpu_custom_call" | custom-call | flops 100000000 | bytes 1024 | tf_op jit(solution)/shard_map/add_lists/pallas_call | solution.py:217
  42.3 0.5 %collective-permute-start.10 = (bf16[1024,256]{1,0:T(8,128)(2,1)S(1)}, bf16[1024,256]{1,0:T(8,128)(2,1)S(1)}, u32[]{:S(2)}, u32[]{:S(2)}) collective-permute-start(bf16[1024,256]{1,0:T(8,128)(2,1)S(1)} %add_lists.17.own_ref), channel_id=1, source_target_pairs={{0,1},{1,0},{2,3},{3,2},{4,5},{5,4},{6,7},{7,6},{8,9},{9,8},{10,11... | collective-permute-start | bytes 1572872 | tf_op jit(solution)/shard_map/ppermute | solution.py:298
  42.8 0.7 %collective-permute-done.11.other_ref = bf16[1024,256]{1,0:T(8,128)(2,1)S(1)} collective-permute-done((bf16[1024,256]{1,0:T(8,128)(2,1)S(1)}, bf16[1024,256]{1,0:T(8,128)(2,1)S(1)}, u32[]{:S(2)}, u32[]{:S(2)}) %collective-permute-start.11) | collective-permute-done | bytes 524320 | tf_op jit(solution)/shard_map/ppermute | solution.py:298
  43.6 1.7 %update.2 = (f32[4096,128]{1,0:T(8,128)}, f32[32,128]{1,0:T(8,128)S(1)}) custom-call(bf16[1024,256]{1,0:T(8,128)(2,1)S(1)} %get-tuple-element.13.own_ref, bf16[1024,256]{1,0:T(8,128)(2,1)S(1)} %collective-permute-done.11.other_ref, f32[4096,128]{1,0:T(8,128)S(1)} %copy-done, f32[32,128]{1,0:T(8,128)S(1)} %bitcast.29), custom_call_target="tpu_custom_call" | custom-call | tf_op jit(solution)/shard_map/update/pallas_call | solution.py:272
  45.2 1.7 %update.3 = (f32[4096,128]{1,0:T(8,128)}, f32[32,128]{1,0:T(8,128)}) custom-call(bf16[1024,256]{1,0:T(8,128)(2,1)S(1)} %add_lists.17.own_ref, bf16[1024,256]{1,0:T(8,128)(2,1)S(1)} %collective-permute-done.10.other_ref, f32[4096,128]{1,0:T(8,128)S(1)} %copy-done, f32[32,128]{1,0:T(8,128)S(1)} %get-tuple-element.14.accum_ref, ...), custom_call_target="tpu_custom_call", output_to_operand_aliasing={{0}: (4, {})} | custom-call | tf_op jit(solution)/shard_map/update/pallas_call | solution.py:272
  (34 shorter events, 2.0 us)
Async XLA Ops:
  0.6 0.7 %copy-start.5 = (s32[2048,1]{0,1:T(1,128)S(1)}, s32[2048,1]{0,1:T(1,128)}, u32[]{:S(2)}) copy-start(s32[2048,1]{0,1:T(1,128)} %param.8) | copy-start | bytes 24580
  1.3 0.9 %copy-start.1 = (bf16[128,8,128]{2,1,0:T(8,128)(2,1)S(1)}, bf16[128,8,128]{2,1,0:T(8,128)(2,1)}, u32[]{:S(2)}) copy-start(bf16[128,8,128]{2,1,0:T(8,128)(2,1)} %param.6) | copy-start | bytes 786436
  1.3 1.0 %copy-start.3 = (s32[2048]{0:T(1024)S(1)}, s32[2048]{0:T(1024)}, u32[]{:S(2)}) copy-start(s32[2048]{0:T(1024)} %param.9) | copy-start | bytes 24580
  1.3 1.0 %copy-start.4 = (f32[2048]{0:T(1024)S(1)}, f32[2048]{0:T(1024)}, u32[]{:S(2)}) copy-start(f32[2048]{0:T(1024)} %param.7) | copy-start | bytes 24580
  3.8 1.5 %collective-permute-start = (bf16[1,400,128]{2,1,0:T(8,128)(2,1)S(1)}, bf16[1,400,128]{2,1,0:T(8,128)(2,1)S(1)}, u32[]{:S(2)}, u32[]{:S(2)}) collective-permute-start(bf16[1,400,128]{2,1,0:T(8,128)(2,1)S(1)} %get-tuple-element.11), channel_id=1, source_target_pairs={{0,1},{1,0},{2,3},{3,2},{4,5},{5,4},{6,7},{7,6},{8,9},{9,8},{10,11... | collective-permute-start | bytes 307208 | tf_op jit(solution)/shard_map/ppermute | solution.py:298
  7.4 17.2 %collective-permute-start.3 = (bf16[800,128]{1,0:T(8,128)(2,1)S(1)}, bf16[800,128]{1,0:T(8,128)(2,1)S(1)}, u32[]{:S(2)}, u32[]{:S(2)}) collective-permute-start(bf16[800,128]{1,0:T(8,128)(2,1)S(1)} %pad_maximum_fusion.refs_0_), channel_id=1, source_target_pairs={{0,24},{1,29},{2,26},{3,31},{4,28},{5,25},{6,30},{7,27},{8,16},{9,... | collective-permute-start | bytes 614408 | tf_op jit(solution)/shard_map/ppermute | solution.py:298
  12.4 1.9 %collective-permute-start.1 = (bf16[2,400,128]{2,1,0:T(8,128)(2,1)S(1)}, bf16[2,400,128]{2,1,0:T(8,128)(2,1)S(1)}, u32[]{:S(2)}, u32[]{:S(2)}) collective-permute-start(bf16[2,400,128]{2,1,0:T(8,128)(2,1)S(1)} %pack_next.6), channel_id=1, source_target_pairs={{0,1},{1,0},{2,3},{3,2},{4,5},{5,4},{6,7},{7,6},{8,9},{9,8},{10,11... | collective-permute-start | bytes 614408 | tf_op jit(solution)/shard_map/ppermute | solution.py:298
  15.3 6.3 %collective-permute-start.4 = (bf16[400,128]{1,0:T(8,128)(2,1)S(1)}, bf16[400,128]{1,0:T(8,128)(2,1)S(1)}, u32[]{:S(2)}, u32[]{:S(2)}) collective-permute-start(bf16[400,128]{1,0:T(8,128)(2,1)S(1)} %get-tuple-element.23), channel_id=1, source_target_pairs={{0,4},{1,5},{2,6},{3,7},{4,0},{5,1},{6,2},{7,3},{8,12},{9,13},{10,... | collective-permute-start | bytes 307208 | tf_op jit(solution)/shard_map/ppermute | solution.py:298
  16.5 14.3 %collective-permute-start.2 = (bf16[800,128]{1,0:T(8,128)(2,1)S(1)}, bf16[800,128]{1,0:T(8,128)(2,1)S(1)}, u32[]{:S(2)}, u32[]{:S(2)}) collective-permute-start(bf16[800,128]{1,0:T(8,128)(2,1)S(1)} %pad_maximum_fusion.1), channel_id=1, source_target_pairs={{0,16},{1,21},{2,18},{3,23},{4,20},{5,17},{6,22},{7,19},{8,24},{9,... | collective-permute-start | bytes 614408 | tf_op jit(solution)/shard_map/ppermute | solution.py:298
  16.6 10.0 %collective-permute-start.5 = (bf16[800,128]{1,0:T(8,128)(2,1)S(1)}, bf16[800,128]{1,0:T(8,128)(2,1)S(1)}, u32[]{:S(2)}, u32[]{:S(2)}) collective-permute-start(bf16[800,128]{1,0:T(8,128)(2,1)S(1)} %pad_maximum_fusion.3), channel_id=1, source_target_pairs={{0,8},{1,13},{2,10},{3,15},{4,12},{5,9},{6,14},{7,11},{8,0},{9,5},... | collective-permute-start | bytes 614408 | tf_op jit(solution)/shard_map/ppermute | solution.py:298
  21.6 13.6 %collective-permute-start.9 = (bf16[800,128]{1,0:T(8,128)(2,1)S(1)}, bf16[800,128]{1,0:T(8,128)(2,1)S(1)}, u32[]{:S(2)}, u32[]{:S(2)}) collective-permute-start(bf16[800,128]{1,0:T(8,128)(2,1)S(1)} %pad_maximum_fusion.2.refs_0_), channel_id=1, source_target_pairs={{0,2},{1,3},{2,0},{3,1},{4,6},{5,7},{6,4},{7,5},{8,10},{9,11},{10,... | collective-permute-start | bytes 614408 | tf_op jit(solution)/shard_map/ppermute | solution.py:298
  24.5 11.9 %collective-permute-start.8 = (bf16[800,128]{1,0:T(8,128)(2,1)S(1)}, bf16[800,128]{1,0:T(8,128)(2,1)S(1)}, u32[]{:S(2)}, u32[]{:S(2)}) collective-permute-start(bf16[800,128]{1,0:T(8,128)(2,1)S(1)} %broadcast_add_fusion.2.refs_0_), channel_id=1, source_target_pairs={{0,2},{1,3},{2,0},{3,1},{4,6},{5,7},{6,4},{7,5},{8,10},{9,11},{10,... | collective-permute-start | bytes 614408 | tf_op jit(solution)/shard_map/ppermute | solution.py:298
  28.0 9.9 %collective-permute-start.7 = (bf16[800,128]{1,0:T(8,128)(2,1)S(1)}, bf16[800,128]{1,0:T(8,128)(2,1)S(1)}, u32[]{:S(2)}, u32[]{:S(2)}) collective-permute-start(bf16[800,128]{1,0:T(8,128)(2,1)S(1)} %broadcast_add_fusion.1.refs_2_.refs_1_.refs_0_), channel_id=1, source_target_pairs={{0,2},{1,3},{2,0},{3,1},{4,6},{5,7},{6,4},{7,5},{8,10},{9,11},{10,... | collective-permute-start | bytes 614408 | tf_op jit(solution)/shard_map/ppermute | solution.py:298
  30.8 9.8 %collective-permute-start.6 = (bf16[800,128]{1,0:T(8,128)(2,1)S(1)}, bf16[800,128]{1,0:T(8,128)(2,1)S(1)}, u32[]{:S(2)}, u32[]{:S(2)}) collective-permute-start(bf16[800,128]{1,0:T(8,128)(2,1)S(1)} %broadcast_add_fusion.refs_2_.refs_0_), channel_id=1, source_target_pairs={{0,2},{1,3},{2,0},{3,1},{4,6},{5,7},{6,4},{7,5},{8,10},{9,11},{10,... | collective-permute-start | bytes 614408 | tf_op jit(solution)/shard_map/ppermute | solution.py:298
  41.6 2.0 %collective-permute-start.11 = (bf16[1024,256]{1,0:T(8,128)(2,1)S(1)}, bf16[1024,256]{1,0:T(8,128)(2,1)S(1)}, u32[]{:S(2)}, u32[]{:S(2)}) collective-permute-start(bf16[1024,256]{1,0:T(8,128)(2,1)S(1)} %get-tuple-element.13.own_ref), channel_id=1, source_target_pairs={{0,1},{1,0},{2,3},{3,2},{4,5},{5,4},{6,7},{7,6},{8,9},{9,8},{10,11... | collective-permute-start | bytes 1572872 | tf_op jit(solution)/shard_map/ppermute | solution.py:298
  41.7 1.9 %copy-start = (f32[4096,128]{1,0:T(8,128)S(1)}, f32[4096,128]{1,0:T(8,128)}, u32[]{:S(2)}) copy-start(f32[4096,128]{1,0:T(8,128)} %weight_ref.3) | copy-start | bytes 6291460
  41.7 1.9 %copy-start.2 = (f32[4096]{0:T(1024)S(1)}, f32[4096]{0:T(1024)}, u32[]{:S(2)}) copy-start(f32[4096]{0:T(1024)} %param.11) | copy-start | bytes 49156
  42.3 2.9 %collective-permute-start.10 = (bf16[1024,256]{1,0:T(8,128)(2,1)S(1)}, bf16[1024,256]{1,0:T(8,128)(2,1)S(1)}, u32[]{:S(2)}, u32[]{:S(2)}) collective-permute-start(bf16[1024,256]{1,0:T(8,128)(2,1)S(1)} %add_lists.17.own_ref), channel_id=1, source_target_pairs={{0,1},{1,0},{2,3},{3,2},{4,5},{5,4},{6,7},{7,6},{8,9},{9,8},{10,11... | collective-permute-start | bytes 1572872 | tf_op jit(solution)/shard_map/ppermute | solution.py:298
